TPU v7x, 256 devices: a whole 4x4x8 slice. The times are simulated.
256 devices in a mesh: rad: 16 (over y, x), azi: 16 (over z, core).
Axes of the slice: x: 4, y: 4, z: 8, core: 2. Of those that a mesh axis runs over, the one named last changes fastest.
Arguments:
- relative_base_heat: float32 [256, 512, 512], P('rad', 'azi'), may hold values from 0.75 to 1.25
- base_deformation_size: float32 [256, 512, 512], P('rad', 'azi'), may hold values from 0.25 to 1
- base_streamwise_flux: float32 [256, 512, 512], P('rad', 'azi'), may hold values from 0.2 to 1
- goal_heat_change: float32 [256, 512, 512], P('rad', 'azi'), may hold values from 0.25 to 2
- initial_costate_heat: float32 [256, 512, 512], P('rad', 'azi'), may hold values from 0.2 to 2
Outputs:
- temperature_adjoint: float32 [256, 512, 512], P('rad', 'azi')
- lengthwise_velocity_sensitivity: float32 [256, 512, 512], P('rad', 'azi')
All inputs are finite; a program needn't handle non-finite values.
Results may differ from a plain program's by a relative error of at most 0.00045.
Values sent between devices are 32-bit elements; how exact they have to be, the bound alone decides.
No kernel may reach another device: no remote copies, remote signals or barrier semaphores. Data moves between devices by JAX's collectives and lax.ppermute only.
A program may use at most 128 MiB of HBM per device.

v0:
```python
import jax
import jax.numpy as jnp
from jax import lax
from jax.sharding import PartitionSpec as P

radial_weight = 8.0
azimuth_weight = 0.25
axial_weight = 0.25
flow_weight = 0.5
mass_weight = 1.0
heat_weight = 0.25
arrhenius_exponent = 2.0
slope_weight = 2.0


def prefix(value, axis, join, neutral, backward):
    count, mine = (lax.axis_size(axis), lax.axis_index(axis))
    pieces = jax.tree.map(lambda part: lax.all_gather(part, axis), value)
    if backward:
        pieces = jax.tree.map(lambda part: part[::-1], pieces)
        mine = count - 1 - mine
    running = jax.tree.map(
        lambda part, zero: jnp.full_like(part, 0) + jnp.asarray(zero, part.dtype), value, neutral
    )

    def lap(position, running):
        longer = join(running, jax.tree.map(lambda part: part[position], pieces))
        return jax.tree.map(lambda new, old: jnp.where(position < mine, new, old), longer, running)

    return lax.fori_loop(0, count - 1, lap, running)


def padded(block, sides, width):
    for axis, dim in sides:
        count = lax.axis_size(axis)
        forward = [(i, i + 1) for i in range(count - 1)]
        forward.append((count - 1, 0))
        backward = [(target, source) for source, target in forward]
        low = lax.ppermute(
            lax.slice_in_dim(block, block.shape[dim] - width, None, axis=dim), axis, forward
        )
        high = lax.ppermute(lax.slice_in_dim(block, 0, width, axis=dim), axis, backward)
        block = jnp.concatenate([low, block, high], axis=dim)
    return block


def line_geometry(first_row, number_lines_total, total_rows, segment_rows):
    row_int = jnp.arange(number_lines_total, dtype=jnp.int32) + first_row
    row_float = row_int.astype(jnp.float32)
    total_float = float(total_rows)
    segment_float = float(segment_rows)
    radius = 1.0 + (row_float + 0.5) / total_float
    inner_face = 1.0 + row_float / total_float
    outer_face = 1.0 + (row_float + 1.0) / total_float
    stiffness = radial_weight * segment_float * segment_float
    lower_off = jnp.where(row_int == 0, 0.0, -stiffness * inner_face / radius)
    upper_off = jnp.where(row_int == total_rows - 1, 0.0, -stiffness * outer_face / radius)
    radial_diag = stiffness * (inner_face + outer_face) / radius
    azimuth_coef = azimuth_weight / (radius * radius)
    return (lower_off, upper_off, radial_diag, azimuth_coef)


def plate_arrays(relative_base_heat, base_deformation_size, base_streamwise_flux):
    polymer_resistance = jnp.exp(-arrhenius_exponent * (relative_base_heat - 1.0))
    heating = (
        heat_weight
        * arrhenius_exponent
        * polymer_resistance
        * base_deformation_size
        * base_deformation_size
    )
    transport_factor = flow_weight * base_streamwise_flux
    extra_pivot_entry = mass_weight + 2.0 * axial_weight + transport_factor + heating
    return (polymer_resistance, transport_factor, extra_pivot_entry)


def explicit_rhs(old_center, side_sum, azimuth_coef, transport_factor, source_field):
    edge_nulls = jnp.zeros_like(old_center[:, :, :1])
    next_cell = jnp.concatenate([old_center[:, :, 1:], edge_nulls], axis=2)
    prev_cell = jnp.concatenate([edge_nulls, old_center[:, :, :-1]], axis=2)
    return (
        source_field
        + azimuth_coef[:, None, None] * side_sum
        + axial_weight * (prev_cell + next_cell)
        + transport_factor * next_cell
        + mass_weight * old_center
    )


def velocity_factor(relative_base_heat, polymer_resistance, base_deformation_size):
    edge_nulls = jnp.zeros_like(relative_base_heat[:, :, :1])
    resistance_derivative_array = jnp.concatenate(
        [relative_base_heat[:, :, 1:] - relative_base_heat[:, :, :-1], edge_nulls], axis=2
    )
    return (
        slope_weight * resistance_derivative_array
        - 2.0 * heat_weight * polymer_resistance * base_deformation_size
    )


def compose_maps(earlier, later):
    first_entry = later[0] * earlier[0]
    second_entry = later[0] * earlier[1] + later[1] * earlier[3] + later[2] * earlier[5]
    third_entry = later[0] * earlier[2] + later[1] * earlier[4] + later[2]
    fourth_entry = later[3] * earlier[3] + later[4] * earlier[5]
    fifth_entry = later[3] * earlier[4] + later[4]
    sixth_entry = later[5] * earlier[3] + earlier[5]
    inverse_norm = 1.0 / (later[5] * earlier[4] + 1.0)
    return (
        first_entry * inverse_norm,
        second_entry * inverse_norm,
        third_entry * inverse_norm,
        fourth_entry * inverse_norm,
        fifth_entry * inverse_norm,
        sixth_entry * inverse_norm,
    )


def compose_affine(earlier, later):
    return (later[0] + later[1] * earlier[0], later[1] * earlier[1])


def solve_lines(lower_off, diagonal, upper_off, right_side):
    number_lines_total = right_side.shape[0]
    zero_plane = jnp.zeros_like(right_side[0])
    unit_plane = jnp.ones_like(right_side[0])
    unit_map = (unit_plane, zero_plane, zero_plane, unit_plane, zero_plane, zero_plane)
    transfer = unit_map
    for index_of_row in range(number_lines_total):
        inverse_diag = 1.0 / diagonal[index_of_row]
        pivot_ratio = -lower_off[index_of_row] * inverse_diag
        step_map = (
            pivot_ratio,
            zero_plane,
            right_side[index_of_row] * inverse_diag,
            zero_plane,
            upper_off[index_of_row] * inverse_diag,
            pivot_ratio,
        )
        transfer = compose_maps(transfer, step_map)
    incoming = prefix(
        (transfer[0], transfer[1], transfer[2], transfer[3], transfer[4], transfer[5]),
        "rad",
        compose_maps,
        (unit_plane, zero_plane, zero_plane, unit_plane, zero_plane, zero_plane),
        False,
    )
    running_g_term = incoming[2]
    running_h_term = incoming[4]
    eliminated_g_term = []
    eliminated_h_term = []
    for index_of_row in range(number_lines_total):
        denominator = diagonal[index_of_row] - lower_off[index_of_row] * running_h_term
        running_g_term = (
            right_side[index_of_row] - lower_off[index_of_row] * running_g_term
        ) / denominator
        running_h_term = upper_off[index_of_row] / denominator
        eliminated_g_term = eliminated_g_term + [running_g_term]
        eliminated_h_term = eliminated_h_term + [running_h_term]
    current_offset = eliminated_g_term[number_lines_total - 1]
    current_slope = -eliminated_h_term[number_lines_total - 1]
    offsets = [current_offset]
    slopes = [current_slope]
    for index_of_row in range(number_lines_total - 2, -1, -1):
        current_offset = (
            eliminated_g_term[index_of_row] - eliminated_h_term[index_of_row] * current_offset
        )
        current_slope = -eliminated_h_term[index_of_row] * current_slope
        offsets = [current_offset] + offsets
        slopes = [current_slope] + slopes
    through = prefix(
        (current_offset, current_slope), "rad", compose_affine, (zero_plane, unit_plane), True
    )
    beyond = through[0]
    return jnp.stack(
        [
            offsets[index_of_row] + slopes[index_of_row] * beyond
            for index_of_row in range(number_lines_total)
        ]
    )


def line_sweep(widened, extra_pivot_entry, transport_factor, source_field, geometry):
    lower_off, upper_off, radial_diag, azimuth_coef = geometry
    old_center = widened[:, 1:-1]
    side_sum = widened[:, :-2] + widened[:, 2:]
    right_side = explicit_rhs(old_center, side_sum, azimuth_coef, transport_factor, source_field)
    diagonal = radial_diag[:, None, None] + 2.0 * azimuth_coef[:, None, None] + extra_pivot_entry
    return solve_lines(lower_off, diagonal, upper_off, right_side)


def body(
    relative_base_heat,
    base_deformation_size,
    base_streamwise_flux,
    goal_heat_change,
    initial_costate_heat,
):
    number_lines_total = relative_base_heat.shape[0]
    total_rows = number_lines_total * lax.axis_size("rad")
    first_row = lax.axis_index("rad") * number_lines_total
    geometry = line_geometry(first_row, number_lines_total, total_rows, number_lines_total)
    polymer_resistance, transport_factor, extra_pivot_entry = plate_arrays(
        relative_base_heat, base_deformation_size, base_streamwise_flux
    )
    sequence_ordinal = initial_costate_heat
    for sweep_index in range(2):
        widened = padded(sequence_ordinal, (("azi", 1),), 1)
        sequence_ordinal = line_sweep(
            widened, extra_pivot_entry, transport_factor, goal_heat_change, geometry
        )
    lengthwise_velocity_sensitivity = sequence_ordinal * velocity_factor(
        relative_base_heat, polymer_resistance, base_deformation_size
    )
    return (sequence_ordinal, lengthwise_velocity_sensitivity)


def solution(mesh):
    return jax.shard_map(
        body,
        mesh=mesh,
        in_specs=(
            P("rad", "azi", None),
            P("rad", "azi", None),
            P("rad", "azi", None),
            P("rad", "azi", None),
            P("rad", "azi", None),
        ),
        out_specs=(P("rad", "azi", None), P("rad", "azi", None)),
        check_vma=False,
    )
```

profile of v0, /device:TPU:64, one launch (start us, length us, event | category | flops | bytes accessed | tf_op | source)
XLA Modules:
  0.0 818.6 jit_solution(8486799840284647636)
XLA Ops:
  7.2 1.1 fusion.98
  8.3 1.7 collective-permute-start.1
  10.1 3.3 fusion.97
  24.7 4.8 add_add_fusion
  29.6 11.1 %add_multiply_fusion.2 = (f32[1,32,512]{2,1,0:T(8,128)}, f32[1,32,512]{2,1,0:T(8,128)S(1)}, f32[1,32,512]{2,1,0:T(8,128)S(1)}, f32[1,32,512]{2,1,0:T(8,128)S(1)}...) fusion(f32[]{:T(128)} %bitcast.32, f32[]{:T(128)} %bitcast.31, f32[]{:T(128)S(6)} %neg.157, f32[]{:T(128)S(6)} %neg.156, ...), kind=kLoop, calls=%fused_computation.240 | loop fusion | flops 2326528 | bytes 1441920 | tf_op jit(solution)/shard_map/mul | solution.py:114
  40.7 11.2 %add_multiply_fusion.3 = f32[1,32,512]{2,1,0:T(8,128)} fusion(f32[1,32,512]{2,1,0:T(8,128)S(1)} %get-tuple-element.795, f32[1,32,512]{2,1,0:T(8,128)S(1)} %get-tuple-element.794, f32[1,32,512]{2,1,0:T(8,128)S(1)} %get-tuple-element.793, f32[1,32,512]{2,1,0:T(8,128)S(1)} %get-tuple-element.792, f32[]{:T(128)} %bitcast.32, f32[]{:T(128)} %bitcast.31, ...), kind=kLoop, calls=%fused_computation.241 | loop fusion | flops 3751936 | bytes 1441920 | tf_op jit(solution)/shard_map/mul | solution.py:113
  52.0 10.6 %add_multiply_fusion.4 = f32[1,32,512]{2,1,0:T(8,128)} fusion(f32[1,32,512]{2,1,0:T(8,128)S(1)} %get-tuple-element.795, f32[1,32,512]{2,1,0:T(8,128)S(1)} %get-tuple-element.794, f32[1,32,512]{2,1,0:T(8,128)S(1)} %get-tuple-element.793, f32[1,32,512]{2,1,0:T(8,128)S(1)} %get-tuple-element.792, f32[]{:T(128)} %bitcast.31, f32[]{:T(128)} %bitcast.30, ...), kind=kLoop, calls=%fused_computation.242 | loop fusion | flops 3719168 | bytes 1441916 | tf_op jit(solution)/shard_map/mul | solution.py:115
  62.7 7.6 add_multiply_fusion.5
  70.3 10.8 %add_multiply_fusion.6 = f32[1,32,512]{2,1,0:T(8,128)} fusion(f32[1,32,512]{2,1,0:T(8,128)S(1)} %get-tuple-element.795, f32[1,32,512]{2,1,0:T(8,128)S(1)} %get-tuple-element.794, f32[1,32,512]{2,1,0:T(8,128)S(1)} %get-tuple-element.793, f32[1,32,512]{2,1,0:T(8,128)S(1)} %get-tuple-element.792, f32[]{:T(128)} %bitcast.31, f32[]{:T(128)} %bitcast.30, ...), kind=kLoop, calls=%fused_computation.244 | loop fusion | flops 5226496 | bytes 2490492 | tf_op jit(solution)/shard_map/mul | solution.py:111
  81.2 7.4 multiply_multiply_fusion.2
  89.3 14.1 %all-gather.25.cloned.1.call-done = f32[16,32,512]{2,1,0:T(8,128)} async-done(((f32[1,32,512]{2,1,0:T(8,128)}), f32[16,32,512]{2,1,0:T(8,128)}) %all-gather.25.cloned.1.call-update) | async-done | bytes 1048592 | tf_op jit(solution)/shard_map/all_gather | solution.py:18
  103.3 49.5 %all-gather.23.cloned.1.call-done = f32[16,32,512]{2,1,0:T(8,128)} async-done(((f32[1,32,512]{2,1,0:T(8,128)}), f32[16,32,512]{2,1,0:T(8,128)}) %all-gather.23.cloned.1.call-update) | async-done | bytes 1048592 | tf_op jit(solution)/shard_map/all_gather | solution.py:18
  152.8 49.5 %all-gather.21.cloned.1.call-done = f32[16,32,512]{2,1,0:T(8,128)} async-done(((f32[1,32,512]{2,1,0:T(8,128)}), f32[16,32,512]{2,1,0:T(8,128)}) %all-gather.21.cloned.1.call-update) | async-done | bytes 1048592 | tf_op jit(solution)/shard_map/all_gather | solution.py:18
  202.3 49.3 %all-gather.19.cloned.1.call-done = f32[16,32,512]{2,1,0:T(8,128)} async-done(((f32[1,32,512]{2,1,0:T(8,128)}), f32[16,32,512]{2,1,0:T(8,128)}) %all-gather.19.cloned.1.call-update) | async-done | bytes 1048592 | tf_op jit(solution)/shard_map/all_gather | solution.py:18
  251.6 49.3 %all-gather.17.cloned.1.call-done = f32[16,32,512]{2,1,0:T(8,128)} async-done(((f32[1,32,512]{2,1,0:T(8,128)}), f32[16,32,512]{2,1,0:T(8,128)}) %all-gather.17.cloned.1.call-update) | async-done | bytes 1048592 | tf_op jit(solution)/shard_map/all_gather | solution.py:18
  301.0 49.9 %all-gather.27.cloned.1.call-done = f32[16,32,512]{2,1,0:T(8,128)} async-done(((f32[1,32,512]{2,1,0:T(8,128)}), f32[16,32,512]{2,1,0:T(8,128)}) %all-gather.27.cloned.1.call-update) | async-done | bytes 1048592 | tf_op jit(solution)/shard_map/all_gather | solution.py:18
  350.9 25.7 %while.60 = (s32[]{:T(128)}, f32[32,512]{1,0:T(8,128)}, f32[32,512]{1,0:T(8,128)S(1)}, s32[]{:T(128)}, f32[16,32,512]{2,1,0:T(8,128)}, /*index=5*/f32[16,32,512]...) while((s32[]{:T(128)}, f32[32,512]{1,0:T(8,128)}, ...), condition=%wide.region_1.2_spmd.clone, body=%wide.region_0.1_spmd.clone.sunk | while | flops 245764 | bytes 655501 | solution.py:30
  350.9 1.7 fusion.105
  352.6 1.7 fusion.105
  354.3 1.7 fusion.105
  356.0 1.7 fusion.105
  357.7 1.7 fusion.105
  359.4 1.7 fusion.105
  361.1 1.7 fusion.105
  362.9 1.7 fusion.105
  364.6 1.7 fusion.105
  366.3 1.7 fusion.105
  368.0 1.7 fusion.105
  369.7 1.7 fusion.105
  371.4 1.7 fusion.105
  373.1 1.7 fusion.105
  374.9 1.7 fusion.105
  376.6 21.0 %negate_multiply_fusion.27 = (f32[32,512]{1,0:T(8,128)}, f32[32,512]{1,0:T(8,128)}, f32[32,512]{1,0:T(8,128)}, f32[32,512]{1,0:T(8,128)}, f32[32,512]{1,0:T(8,12...) fusion(f32[]{:T(128)} %bitcast.2, ...), kind=kLoop, calls=%fused_computation.224 | loop fusion | flops 1261568 | bytes 2621568 | tf_op jit(solution)/shard_map/mul | solution.py:168
  397.7 8.4 %fusion.49 = (f32[32,512]{1,0:T(8,128)S(1)}, f32[32,512]{1,0:T(8,128)S(1)}, f32[32,512]{1,0:T(8,128)S(1)}, f32[32,512]{1,0:T(8,128)S(1)}, f32[32,512]{1,0:T(8,12...) fusion(f32[16,32,512]{2,1,0:T(8,128)S(1)} %get-tuple-element.80, ...), kind=kLoop, calls=%fused_computation.131 | loop fusion | flops 1064960 | bytes 3473460 | tf_op jit(solution)/shard_map/div | solution.py:154
  406.2 2.8 multiply_subtract_fusion.15
  409.9 46.4 %all-gather.33.cloned.1.call-done = f32[512,512]{1,0:T(8,128)} async-done(((f32[32,512]{1,0:T(8,128)}), f32[512,512]{1,0:T(8,128)}) %all-gather.33.cloned.1.call-update) | async-done | bytes 1048592 | tf_op jit(solution)/shard_map/all_gather | solution.py:18
  456.2 2.3 rev.12
  458.5 47.2 %all-gather.35.cloned.1.call-done = f32[512,512]{1,0:T(8,128)} async-done(((f32[32,512]{1,0:T(8,128)}), f32[512,512]{1,0:T(8,128)}) %all-gather.35.cloned.1.call-update) | async-done | bytes 1048592 | tf_op jit(solution)/shard_map/all_gather | solution.py:18
  505.7 2.3 rev.13
  508.0 14.0 %while.61 = (s32[]{:T(128)}, f32[32,512]{1,0:T(8,128)S(1)}, s32[]{:T(128)}, f32[16,32,512]{2,1,0:T(8,128)}, f32[16,32,512]{2,1,0:T(8,128)}, /*index=5*/s32[]{:T(128)}, s32[]{:T(128)}) while((s32[]{:T(128)}, f32[32,512]{1,0:T(8,128)S(1)}, s32[]{:T(128)}, f32[16,32,512]{2,1,0:T(8,128)}, f32[16,32,512]{2,1,0:T(8,128)}, ...), condition=%wide.region_3.4_spmd.clone, body=%wide.region_2.3_spmd.clone.sunk | while | flops 65540 | bytes 262245 | solution.py:30
  529.8 1.4 constant_dynamic-update-slice_fusion
  531.3 1.7 collective-permute-start.3
  533.4 1.2 collective-permute-done.2
  535.4 7.6 add_multiply_fusion
  543.3 10.7 %add_multiply_fusion.1 = f32[1,32,512]{2,1,0:T(8,128)} fusion(f32[1,32,512]{2,1,0:T(8,128)S(1)} %get-tuple-element.795, f32[1,32,512]{2,1,0:T(8,128)S(1)} %get-tuple-element.794, f32[1,32,512]{2,1,0:T(8,128)S(1)} %get-tuple-element.793, f32[1,32,512]{2,1,0:T(8,128)S(1)} %get-tuple-element.792, f32[]{:T(128)} %bitcast.31, f32[]{:T(128)} %bitcast.30, ...), kind=kLoop, calls=%fused_computation.210 | loop fusion | flops 5226496 | bytes 2490492 | tf_op jit(solution)/shard_map/mul | solution.py:111
  554.1 37.6 %all-gather.31.cloned.1.call-done = f32[16,32,512]{2,1,0:T(8,128)} async-done(((f32[1,32,512]{2,1,0:T(8,128)}), f32[16,32,512]{2,1,0:T(8,128)}) %all-gather.31.cloned.1.call-update) | async-done | bytes 1048592 | tf_op jit(solution)/shard_map/all_gather | solution.py:18
  591.7 49.9 %all-gather.29.cloned.1.call-done = f32[16,32,512]{2,1,0:T(8,128)} async-done(((f32[1,32,512]{2,1,0:T(8,128)}), f32[16,32,512]{2,1,0:T(8,128)}) %all-gather.29.cloned.1.call-update) | async-done | bytes 1048592 | tf_op jit(solution)/shard_map/all_gather | solution.py:18
  641.6 16.2 %while.62 = (s32[]{:T(128)}, f32[32,512]{1,0:T(8,128)S(1)}, f32[32,512]{1,0:T(8,128)S(1)}, s32[]{:T(128)}, f32[16,32,512]{2,1,0:T(8,128)}, /*index=5*/f32[16,32,...) while((s32[]{:T(128)}, f32[32,512]{1,0:T(8,128)S(1)}, ...), condition=%wide.region_5.6_spmd.clone, body=%wide.region_4.5_spmd.clone.sunk | while | flops 245764 | bytes 655501 | solution.py:30
  644.9 1.1 fusion.107
  646.0 1.1 fusion.107
  649.2 1.1 fusion.107
  650.3 1.1 fusion.107
  653.5 1.1 fusion.107
  657.9 21.0 %negate_multiply_fusion.13 = (f32[32,512]{1,0:T(8,128)}, f32[32,512]{1,0:T(8,128)}, f32[32,512]{1,0:T(8,128)}, f32[32,512]{1,0:T(8,128)}, f32[32,512]{1,0:T(8,12...) fusion(f32[]{:T(128)} %bitcast.2, ...), kind=kLoop, calls=%fused_computation.193 | loop fusion | flops 1261568 | bytes 2621568 | tf_op jit(solution)/shard_map/mul | solution.py:168
  678.8 8.4 %fusion.33 = (f32[32,512]{1,0:T(8,128)S(1)}, f32[32,512]{1,0:T(8,128)S(1)}, f32[32,512]{1,0:T(8,128)S(1)}, f32[32,512]{1,0:T(8,128)S(1)}, f32[32,512]{1,0:T(8,12...) fusion(f32[16,32,512]{2,1,0:T(8,128)S(1)} %fusion.23, ...), kind=kLoop, calls=%fused_computation.91 | loop fusion | flops 1064960 | bytes 3473460 | tf_op jit(solution)/shard_map/div | solution.py:154
  687.3 2.8 multiply_subtract_fusion
  690.8 1.3 slice_subtract_fusion
  692.1 45.3 %all-gather.37.cloned.1.call-done = f32[512,512]{1,0:T(8,128)} async-done(((f32[32,512]{1,0:T(8,128)}), f32[512,512]{1,0:T(8,128)}) %all-gather.37.cloned.1.call-update) | async-done | bytes 1048592 | tf_op jit(solution)/shard_map/all_gather | solution.py:18
  737.3 2.3 rev.14
  739.6 47.1 %all-gather.39.cloned.1.call-done = f32[512,512]{1,0:T(8,128)} async-done(((f32[32,512]{1,0:T(8,128)}), f32[512,512]{1,0:T(8,128)}) %all-gather.39.cloned.1.call-update) | async-done | bytes 1048592 | tf_op jit(solution)/shard_map/all_gather | solution.py:18
  786.7 2.3 rev.15
  789.0 14.0 %while.63 = (s32[]{:T(128)}, f32[32,512]{1,0:T(8,128)S(1)}, s32[]{:T(128)}, f32[16,32,512]{2,1,0:T(8,128)}, f32[16,32,512]{2,1,0:T(8,128)}, /*index=5*/s32[]{:T(128)}, s32[]{:T(128)}) while((s32[]{:T(128)}, f32[32,512]{1,0:T(8,128)S(1)}, s32[]{:T(128)}, f32[16,32,512]{2,1,0:T(8,128)}, f32[16,32,512]{2,1,0:T(8,128)}, ...), condition=%wide.region_7.8_spmd.clone, body=%wide.region_6.7_spmd.clone.sunk | while | flops 65540 | bytes 262245 | solution.py:30
  808.9 1.4 constant_dynamic-update-slice_fusion.16
  810.3 1.5 subtract_multiply_fusion
  (286 shorter events, 56.4 us)
Async XLA Ops:
  7.2 96.2 %all-gather.25.cloned.1.call-start = ((), (), s32[]{:S(2)}) async-start(), calls=%async_computation.4 | async-start | bytes 1114112 | tf_op jit(solution)/shard_map/all_gather | solution.py:18
  8.3 16.4 %collective-permute-start = (f32[16,1,512]{2,1,0:T(1,128)S(1)}, f32[16,1,512]{2,1,0:T(1,128)S(1)}, u32[]{:S(2)}, u32[]{:S(2)}) collective-permute-start(f32[16,1,512]{2,1,0:T(1,128)S(1)} %get-tuple-element.808), channel_id=1, source_target_pairs={{0,1},{1,2},{2,3},{3,4},{4,5},{5,6},{6,7},{7,8},{8,9},{9,10},{10,1... | collective-permute-start | bytes 98312 | tf_op jit(solution)/shard_map/ppermute | solution.py:39
  8.3 16.4 %collective-permute-start.1 = (f32[16,1,512]{2,1,0:T(1,128)S(1)}, f32[16,1,512]{2,1,0:T(1,128)S(1)}, u32[]{:S(2)}, u32[]{:S(2)}) collective-permute-start(f32[16,1,512]{2,1,0:T(1,128)S(1)} %get-tuple-element.809), channel_id=1, source_target_pairs={{1,0},{2,1},{3,2},{4,3},{5,4},{6,5},{7,6},{8,7},{9,8},{10,9},{11,1... | collective-permute-start | bytes 98312 | tf_op jit(solution)/shard_map/ppermute | solution.py:42
  10.1 14.7 %copy-start = (f32[16,32,512]{2,1,0:T(8,128)S(1)}, f32[16,32,512]{2,1,0:T(8,128)}, u32[]{:S(2)}) copy-start(f32[16,32,512]{2,1,0:T(8,128)} %param.13) | copy-start | bytes 3145732
  52.0 100.8 %all-gather.23.cloned.1.call-start = ((), (), s32[]{:S(2)}) async-start(), calls=%async_computation.3 | async-start | bytes 1114112 | tf_op jit(solution)/shard_map/all_gather | solution.py:18
  62.6 139.7 %all-gather.21.cloned.1.call-start = ((), (), s32[]{:S(2)}) async-start(), calls=%async_computation.2 | async-start | bytes 1114112 | tf_op jit(solution)/shard_map/all_gather | solution.py:18
  70.3 181.3 %all-gather.19.cloned.1.call-start = ((), (), s32[]{:S(2)}) async-start(), calls=%async_computation.1 | async-start | bytes 1114112 | tf_op jit(solution)/shard_map/all_gather | solution.py:18
  81.1 219.8 %all-gather.17.cloned.1.call-start = ((), (), s32[]{:S(2)}) async-start(), calls=%async_computation | async-start | bytes 1114112 | tf_op jit(solution)/shard_map/all_gather | solution.py:18
  88.6 262.3 %all-gather.27.cloned.1.call-start = ((), (), s32[]{:S(2)}) async-start(), calls=%async_computation.5 | async-start | bytes 1114112 | tf_op jit(solution)/shard_map/all_gather | solution.py:18
  89.2 367.0 %all-gather.33.cloned.1.call-start = ((), (), s32[]{:S(2)}) async-start(), calls=%async_computation.8 | async-start | bytes 1114112 | tf_op jit(solution)/shard_map/all_gather | solution.py:18
  376.6 21.1 %copy-start.5 = (f32[32,512]{1,0:T(8,128)S(1)}, f32[32,512]{1,0:T(8,128)}, u32[]{:S(2)}) copy-start(f32[32,512]{1,0:T(8,128)} %get-tuple-element.530) | copy-start | bytes 196612
  397.6 8.5 %copy-start.9 = (f32[32,512]{1,0:T(8,128)}, f32[32,512]{1,0:T(8,128)S(1)}, u32[]{:S(2)}) copy-start(f32[32,512]{1,0:T(8,128)S(1)} %get-tuple-element.755) | copy-start | bytes 196612
  397.6 8.5 %copy-start.13 = (f32[32,512]{1,0:T(8,128)}, f32[32,512]{1,0:T(8,128)S(1)}, u32[]{:S(2)}) copy-start(f32[32,512]{1,0:T(8,128)S(1)} %get-tuple-element.757) | copy-start | bytes 196612
  397.6 8.5 %copy-start.15 = (f32[32,512]{1,0:T(8,128)}, f32[32,512]{1,0:T(8,128)S(1)}, u32[]{:S(2)}) copy-start(f32[32,512]{1,0:T(8,128)S(1)} %get-tuple-element.759) | copy-start | bytes 196612
  397.6 8.5 %copy-start.17 = (f32[32,512]{1,0:T(8,128)}, f32[32,512]{1,0:T(8,128)S(1)}, u32[]{:S(2)}) copy-start(f32[32,512]{1,0:T(8,128)S(1)} %get-tuple-element.761) | copy-start | bytes 196612
  397.6 8.5 %copy-start.19 = (f32[32,512]{1,0:T(8,128)}, f32[32,512]{1,0:T(8,128)S(1)}, u32[]{:S(2)}) copy-start(f32[32,512]{1,0:T(8,128)S(1)} %get-tuple-element.763) | copy-start | bytes 196612
  397.6 8.5 %copy-start.21 = (f32[32,512]{1,0:T(8,128)}, f32[32,512]{1,0:T(8,128)S(1)}, u32[]{:S(2)}) copy-start(f32[32,512]{1,0:T(8,128)S(1)} %get-tuple-element.765) | copy-start | bytes 196612
  397.7 8.5 %copy-start.27 = (f32[32,512]{1,0:T(8,128)}, f32[32,512]{1,0:T(8,128)S(1)}, u32[]{:S(2)}) copy-start(f32[32,512]{1,0:T(8,128)S(1)} %get-tuple-element.752) | copy-start | bytes 196612
  397.7 8.5 %copy-start.29 = (f32[32,512]{1,0:T(8,128)}, f32[32,512]{1,0:T(8,128)S(1)}, u32[]{:S(2)}) copy-start(f32[32,512]{1,0:T(8,128)S(1)} %get-tuple-element.753) | copy-start | bytes 196612
  406.1 2.9 copy-start.37
  406.1 2.9 copy-start.41
  406.1 2.9 copy-start.45
  406.1 2.9 copy-start.49
  406.1 2.9 copy-start.51
  406.1 2.9 copy-start.53
  409.1 96.7 %all-gather.35.cloned.1.call-start = ((), (), s32[]{:S(2)}) async-start(), calls=%async_computation.9 | async-start | bytes 1114112 | tf_op jit(solution)/shard_map/all_gather | solution.py:18
  409.8 181.9 %all-gather.31.cloned.1.call-start = ((), (), s32[]{:S(2)}) async-start(), calls=%async_computation.7 | async-start | bytes 1114112 | tf_op jit(solution)/shard_map/all_gather | solution.py:18
  522.0 1.0 copy-start.22
  522.1 1.0 copy-start.54
  522.1 1.0 copy-start.72
  522.1 1.0 copy-start.82
  524.1 0.9 copy-start.78
  525.1 0.9 copy-start.76
  531.2 3.4 collective-permute-start.2
  531.2 3.3 copy-start.1
  531.2 3.3 copy-start.2
  531.3 3.3 collective-permute-start.3
  543.0 98.6 %all-gather.29.cloned.1.call-start = ((), (), s32[]{:S(2)}) async-start(), calls=%async_computation.6 | async-start | bytes 1114112 | tf_op jit(solution)/shard_map/all_gather | solution.py:18
  554.0 183.3 %all-gather.37.cloned.1.call-start = ((), (), s32[]{:S(2)}) async-start(), calls=%async_computation.10 | async-start | bytes 1114112 | tf_op jit(solution)/shard_map/all_gather | solution.py:18
  678.8 8.4 %copy-start.7 = (f32[32,512]{1,0:T(8,128)}, f32[32,512]{1,0:T(8,128)S(1)}, u32[]{:S(2)}) copy-start(f32[32,512]{1,0:T(8,128)S(1)} %get-tuple-element.717) | copy-start | bytes 196612
  678.8 8.5 %copy-start.11 = (f32[32,512]{1,0:T(8,128)}, f32[32,512]{1,0:T(8,128)S(1)}, u32[]{:S(2)}) copy-start(f32[32,512]{1,0:T(8,128)S(1)} %get-tuple-element.719) | copy-start | bytes 196612
  678.8 8.5 %copy-start.23 = (f32[32,512]{1,0:T(8,128)}, f32[32,512]{1,0:T(8,128)S(1)}, u32[]{:S(2)}) copy-start(f32[32,512]{1,0:T(8,128)S(1)} %get-tuple-element.706) | copy-start | bytes 196612
  678.8 8.5 %copy-start.25 = (f32[32,512]{1,0:T(8,128)}, f32[32,512]{1,0:T(8,128)S(1)}, u32[]{:S(2)}) copy-start(f32[32,512]{1,0:T(8,128)S(1)} %get-tuple-element.707) | copy-start | bytes 196612
  687.2 2.9 copy-start.31
  687.2 2.9 copy-start.33
  687.2 2.9 copy-start.35
  687.2 2.9 copy-start.39
  687.2 2.9 copy-start.43
  687.3 2.9 copy-start.47
  690.2 96.5 %all-gather.39.cloned.1.call-start = ((), (), s32[]{:S(2)}) async-start(), calls=%async_computation.11 | async-start | bytes 1114112 | tf_op jit(solution)/shard_map/all_gather | solution.py:18
  803.0 1.0 copy-start.12
  803.0 1.0 copy-start.48
  803.0 1.0 copy-start.63
  803.0 1.0 copy-start.81
  806.9 1.1 copy-start.70
  806.9 1.2 copy-start.85
  806.9 1.9 copy-start.83
  806.9 0.9 copy-start.57
  807.0 1.0 copy-start.32
  807.0 1.0 copy-start.56
  807.9 1.0 copy-start.24
  807.9 2.3 copy-start.4
  807.9 2.3 copy-start.3
  810.2 1.5 copy-start.6
  (39 other events, 34.0 us)
Sparse Core Ops, SparseCore 0:
  52.1 51.1 all-gather.24
  105.8 47.0 all-gather.22
  155.3 47.0 all-gather.20
  204.6 47.0 all-gather.18
  253.9 47.0 all-gather.16
  303.8 47.0 all-gather.26
  409.2 47.0 all-gather.32
  458.7 47.0 all-gather.34
  543.1 48.5 all-gather.30
  594.6 47.0 all-gather.28
  690.3 47.0 all-gather.36
  739.6 47.0 all-gather.38
where the time goes:
time: 825 us; the launch traced here: 819 us
  waiting for transfers between devices  538 us (65%)
  other arithmetic  224 us (27%)
  local copies, waits for them, and re-layouts  25.9 us (3%)
  between operations  25.3 us (3%)
    all_gather x12, waiting for transfers between devices, prefix(): pieces = jax.tree.map(lambda part: lax.all_gather(part, axis), value)  535 us
    select_n x60, other arithmetic, lap(): jnp.where(position < mine, new, old)  69 us
    mul x2, other arithmetic, solve_lines(): current_slope = -eliminated_h_term[index_of_row] * current_slope  42 us
    mul x2, other arithmetic, compose_maps(): second_entry * inverse_norm  21.5 us
    div x2, other arithmetic, solve_lines(): (right_side[index_of_row] - lower_off[index_of_row] * running_g_term) / d...  16.7 us
  transfers between devices with their start and end apart: 16, of which 13 were waited for; matrix products, arithmetic and copies ran while one was open for 7% of the time, Pallas kernels for 0%

commit v1 on v0

v1 whole, which is shorter than its diff:
```python
import jax
import jax.numpy as jnp
from jax import lax
from jax.experimental import pallas as pl
from jax.experimental.pallas import tpu as pltpu
from jax.sharding import PartitionSpec as P

radial_weight = 8.0
azimuth_weight = 0.25
axial_weight = 0.25
flow_weight = 0.5
mass_weight = 1.0
heat_weight = 0.25
arrhenius_exponent = 2.0
slope_weight = 2.0

SUB, LANE = 8, 128
F32 = jnp.float32


def geometry(rows):
    total = rows * lax.axis_size("rad")
    stiffness = radial_weight * rows * rows
    first = (lax.axis_index("rad") * rows).astype(F32)
    links = [stiffness + (stiffness / total) * (first + float(i)) for i in range(rows + 1)]
    radii = [1.0 + (first + (i + 0.5)) * (1.0 / total) for i in range(rows)]
    return links, radii


def splat(scalar):
    return jnp.full((1, LANE), scalar, F32)


def wide(row, width):
    return jnp.concatenate([row] * (width // LANE), axis=1)


def tiles_of(ref, group, plane, width):
    per = width // LANE
    return jnp.concatenate([ref[group * per + t, plane] for t in range(per)], axis=1)


def put_tiles(ref, group, plane, value):
    per = value.shape[1] // LANE
    for t in range(per):
        ref[group * per + t, plane] = value[:, t * LANE : (t + 1) * LANE]


def lane_next(value):
    width = value.shape[1]
    lane = lax.broadcasted_iota(jnp.int32, value.shape, 1)
    return jnp.where(lane == width - 1, 0.0, pltpu.roll(value, width - 1, 1))


def lane_prev(value):
    lane = lax.broadcasted_iota(jnp.int32, value.shape, 1)
    return jnp.where(lane == 0, 0.0, pltpu.roll(value, 1, 1))


def matrix_kernel(heat, deform, flux, ratio, left_map, right_map, factor, condensed):
    rows, azimuths, width = heat.shape
    links, radii = geometry(rows)
    inverse_links = [wide(1.0 / splat(link), width) for link in links]
    shunts = []
    for radius in radii:
        r = splat(radius)
        shunts.append(wide(2.0 * azimuth_weight / (r * r) + (mass_weight + 2.0 * axial_weight), width))
    for group in range(azimuths // SUB):
        here = pl.ds(group * SUB, SUB)
        ratios, lefts = [], []
        pivot = None
        through = jnp.full((SUB, width), links[0], F32)
        for i in range(rows):
            hot = heat[i, here, :]
            size = deform[i, here, :]
            drag = jnp.exp(-arrhenius_exponent * (hot - 1.0)) * size
            shunt = radii[i] * (
                shunts[i]
                + flow_weight * flux[i, here, :]
                + (heat_weight * arrhenius_exponent) * (drag * size)
            )
            lane = lax.broadcasted_iota(jnp.int32, hot.shape, 1)
            rise = jnp.where(lane == width - 1, 0.0, pltpu.roll(hot, width - 1, 1) - hot)
            factor[i, here, :] = slope_weight * rise - (2.0 * heat_weight) * drag
            pivot = shunt + (links[0] if i == 0 else ratios[-1] * pivot)
            lefts.append(through)
            if i < rows - 1:
                step = links[i + 1] / (links[i + 1] + pivot)
                ratios.append(step)
                ratio[i, here, :] = step
                through = step * through
        put_tiles(condensed, group, 0, through)
        put_tiles(condensed, group, 2, pivot)
        from_left = jnp.zeros((SUB, width), F32)
        from_right = jnp.ones((SUB, width), F32)
        left_map[rows - 1, here, :] = from_left
        right_map[rows - 1, here, :] = from_right
        ratio[rows - 1, here, :] = from_left
        for i in range(rows - 2, -1, -1):
            from_left = ratios[i] * (lefts[i] * inverse_links[i + 1] + from_left)
            from_right = ratios[i] * from_right
            left_map[i, here, :] = from_left
            right_map[i, here, :] = from_right
        put_tiles(condensed, group, 1, links[0] * (1.0 - from_left))


def sources(group, old, below, above, flux, goal, radii, quarter):
    rows, azimuths, width = old.shape
    here = pl.ds(group * SUB, SUB)
    sub = lax.broadcasted_iota(jnp.int32, (SUB, width), 0)
    out = []
    for i in range(rows):
        centre = old[i, here, :]
        low = below[i : i + 1, :] if group == 0 else old[i, group * SUB - 1 : group * SUB, :]
        high = (
            above[i : i + 1, :]
            if group == azimuths // SUB - 1
            else old[i, (group + 1) * SUB : (group + 1) * SUB + 1, :]
        )
        side = jnp.where(sub == 0, low, pltpu.roll(centre, 1, 0)) + jnp.where(
            sub == SUB - 1, high, pltpu.roll(centre, SUB - 1, 0)
        )
        after = lane_next(centre)
        right = (
            goal[i, here, :]
            + axial_weight * (lane_prev(centre) + after)
            + flow_weight * flux[i, here, :] * after
            + mass_weight * centre
        )
        out.append(radii[i] * right + quarter[i] * side)
    return out


def local_solve(group, source, ratio, inverse_links, particular):
    rows = len(source)
    here = pl.ds(group * SUB, SUB)
    ratios = [ratio[i, here, :] for i in range(rows - 1)]
    currents = [source[0]]
    for i in range(1, rows):
        currents.append(source[i] + ratios[i - 1] * currents[-1])
    value = jnp.zeros_like(source[0])
    particular[rows - 1, here, :] = value
    for i in range(rows - 2, -1, -1):
        value = ratios[i] * (currents[i] * inverse_links[i + 1] + value)
        particular[i, here, :] = value
    return value, currents[-1]


def tables(rows, width):
    links, radii = geometry(rows)
    inverse_links = [wide(1.0 / splat(link), width) for link in links]
    quarter = [wide(azimuth_weight / splat(radius), width) for radius in radii]
    return links, radii, inverse_links, quarter


def first_kernel(old, below, above, flux, goal, ratio, condensed, particular, message):
    rows, azimuths, width = old.shape
    links, radii, inverse_links, quarter = tables(rows, width)
    message[:, 0:3] = condensed[...]
    for group in range(azimuths // SUB):
        source = sources(group, old, below, above, flux, goal, radii, quarter)
        inner, outer = local_solve(group, source, ratio, inverse_links, particular)
        put_tiles(message, group, 3, links[0] * inner)
        put_tiles(message, group, 4, outer)


def reduced_kernel(rows, got, sent):
    segments = got.shape[0]
    last_link = 2.0 * radial_weight * rows * rows
    inverses, ratios, offsets = [], [], []
    for s in range(segments):
        diagonal = got[s, 2] + (got[s + 1, 1] if s + 1 < segments else last_link)
        right = got[s, 4] + (got[s + 1, 3] if s + 1 < segments else 0.0)
        if s > 0:
            diagonal = diagonal - got[s, 0] * ratios[-1]
            right = right + ratios[-1] * carried
        carried = right
        inverse = 1.0 / diagonal
        inverses.append(inverse)
        offsets.append(right * inverse)
        if s + 1 < segments:
            ratios.append(got[s + 1, 0] * inverse)
    zero = jnp.zeros_like(inverses[0])
    for s in range(segments - 1, -1, -1):
        if s + 1 < segments:
            value = offsets[s] + ratios[s] * value
            green = inverses[s] + ratios[s] * ratios[s] * green
            rising = ratios[s] * rising
        else:
            value, green, rising = offsets[s], inverses[s], jnp.ones_like(zero)
        falling = green / rising
        for plane, item in enumerate((value, rising, falling)):
            sent[s, 2 * plane + 1] = item
            if s + 1 < segments:
                sent[s + 1, 2 * plane] = item
    for plane in range(3):
        sent[0, 2 * plane] = zero


def second_kernel(particular, left_map, right_map, got, new, low_edge, high_edge):
    rows, azimuths, width = particular.shape
    for group in range(azimuths // SUB):
        here = pl.ds(group * SUB, SUB)
        left = tiles_of(got, group, 0, width)
        right = tiles_of(got, group, 1, width)
        for i in range(rows):
            value = particular[i, here, :] + left_map[i, here, :] * left + right_map[i, here, :] * right
            new[i, here, :] = value
            if group == 0:
                low_edge[i : i + 1, :] = value[0:1, :]
            if group == azimuths // SUB - 1:
                high_edge[i : i + 1, :] = value[SUB - 1 : SUB, :]


def third_kernel(old, below, above, flux, goal, ratio, got, particular, message, own):
    rows, azimuths, width = old.shape
    links, radii, inverse_links, quarter = tables(rows, width)
    segments = message.shape[0]
    me = lax.axis_index("rad")
    for group in range(azimuths // SUB):
        here = pl.ds(group * SUB, SUB)
        source = sources(group, old, below, above, flux, goal, radii, quarter)
        inner, outer = local_solve(group, source, ratio, inverse_links, particular)
        inner = links[0] * inner
        upward = tiles_of(got, group, 2, width) * inner + tiles_of(got, group, 3, width) * outer
        downward = tiles_of(got, group, 4, width) * inner + tiles_of(got, group, 5, width) * outer
        own[0, here, :] = upward
        own[1, here, :] = downward
        for s in range(segments):
            message[s, here, :] = jnp.where(s > me, upward, downward)


def last_kernel(particular, left_map, right_map, factor, got, own, arrived, result, sensitivity):
    rows, azimuths, width = particular.shape
    segments = arrived.shape[0]
    me = lax.axis_index("rad")
    for group in range(azimuths // SUB):
        here = pl.ds(group * SUB, SUB)
        lower = jnp.zeros((SUB, width), F32)
        upper = jnp.zeros((SUB, width), F32)
        for s in range(segments):
            item = arrived[s, here, :]
            lower = lower + jnp.where(s < me, item, 0.0)
            upper = upper + jnp.where(s > me, item, 0.0)
        left = tiles_of(got, group, 4, width) * lower + tiles_of(got, group, 2, width) * (
            own[1, here, :] + upper
        )
        right = (
            tiles_of(got, group, 5, width) * (lower + own[0, here, :])
            + tiles_of(got, group, 3, width) * upper
        )
        for i in range(rows):
            value = particular[i, here, :] + left_map[i, here, :] * left + right_map[i, here, :] * right
            result[i, here, :] = value
            sensitivity[i, here, :] = value * factor[i, here, :]


def call(kernel, outs, *args, flops=1_000_000):
    moved = sum(4 * a.size for a in args) + sum(4 * o.size for o in outs)
    return pl.pallas_call(
        kernel,
        out_shape=outs,
        in_specs=[pl.BlockSpec(memory_space=pltpu.VMEM)] * len(args),
        out_specs=tuple([pl.BlockSpec(memory_space=pltpu.VMEM)] * len(outs)),
        compiler_params=pltpu.CompilerParams(vmem_limit_bytes=24 * 2**20),
        cost_estimate=pl.CostEstimate(flops=flops, bytes_accessed=moved, transcendentals=0),
    )(*args)


def swap_edges(low_edge, high_edge):
    count = lax.axis_size("azi")
    below = lax.ppermute(high_edge, "azi", [(i, (i + 1) % count) for i in range(count)])
    above = lax.ppermute(low_edge, "azi", [((i + 1) % count, i) for i in range(count)])
    return below, above


def exchange(value):
    return lax.all_to_all(value, "rad", 0, 0, tiled=True)


def body(heat, deform, flux, goal, start):
    rows, azimuths, width = heat.shape
    segments = lax.axis_size("rad")
    tiles = azimuths * width // (SUB * LANE)
    block = jax.ShapeDtypeStruct((rows, azimuths, width), F32)
    edge = jax.ShapeDtypeStruct((rows, width), F32)

    def planes(count):
        return jax.ShapeDtypeStruct((tiles, count, SUB, LANE), F32)

    below, above = swap_edges(start[:, 0, :], start[:, azimuths - 1, :])
    ratio, left_map, right_map, factor, condensed = call(
        matrix_kernel, (block, block, block, block, planes(3)), heat, deform, flux, flops=20_000_000
    )
    particular, message = call(
        first_kernel, (block, planes(5)), start, below, above, flux, goal, ratio, condensed
    )
    sent = call(
        lambda got, sent: reduced_kernel(rows, got, sent),
        (jax.ShapeDtypeStruct((segments, 6, SUB, LANE), F32),),
        exchange(message),
    )[0]
    got = exchange(sent)
    new, low_edge, high_edge = call(
        second_kernel, (block, edge, edge), particular, left_map, right_map, got
    )
    below, above = swap_edges(low_edge, high_edge)
    particular, message, own = call(
        third_kernel,
        (
            block,
            jax.ShapeDtypeStruct((segments, azimuths, width), F32),
            jax.ShapeDtypeStruct((2, azimuths, width), F32),
        ),
        new,
        below,
        above,
        flux,
        goal,
        ratio,
        got,
    )
    arrived = exchange(message)
    return call(
        last_kernel, (block, block), particular, left_map, right_map, factor, got, own, arrived
    )


def solution(mesh):
    spec = P("rad", "azi", None)
    return jax.shard_map(
        body, mesh=mesh, in_specs=(spec,) * 5, out_specs=(spec, spec), check_vma=False
    )
```

time: 825 us -> 68.8 us (0.08)
  the two profiles are of different devices: /device:TPU:64 before, /device:TPU:97 now
where the time goes in v1:
time: 68.8 us; the launch traced here: 68.5 us
  blocking collectives  46.3 us (67%)
  starting transfers between devices  6.47 us (9%)
  local copies, waits for them, and re-layouts  5.64 us (8%)
  Pallas kernels  4.8 us (7%)
  waiting for transfers between devices  4.55 us (7%)
  between operations  0.7 us (1%)
    all_to_all x3, blocking collectives, exchange(): return lax.all_to_all(value, 'rad', 0, 0, tiled=True)  46.3 us
    ppermute x2, starting transfers between devices, swap_edges(): lax.ppermute(high_edge, 'azi', [(i, (i + 1) % count) for i in range(count)])  6.46 us
    pallas_call x6, Pallas kernels, call(): pl.pallas_call(kernel, out_shape=outs, in_specs=[pl.BlockSpec(memory_spac...  4.8 us
    unnamed x14, local copies, waits for them, and re-layouts  4.55 us
    ppermute x2, waiting for transfers between devices, swap_edges(): lax.ppermute(low_edge, 'azi', [((i + 1) % count, i) for i in range(count)])  3.53 us
  transfers between devices with their start and end apart: 4, of which 2 were waited for; matrix products, arithmetic and copies ran while one was open for 0% of the time, Pallas kernels for 1%

profile of v1, /device:TPU:97, one launch (start us, length us, event | category | flops | bytes accessed | tf_op | source)
XLA Modules:
  0.0 68.5 jit_solution(8687120046262226838)
XLA Ops:
  0.6 1.1 %fusion = (f32[16,1,512]{2,1,0:T(1,128)S(1)}, f32[16,1,512]{2,1,0:T(1,128)S(1)}) fusion(f32[16,32,512]{2,1,0:T(8,128)} %old.1), kind=kLoop, calls=%fused_computation.2 | loop fusion | bytes 131072 | tf_op jit(solution)/shard_map/slice | solution.py:291
  1.7 3.4 %collective-permute-start = (f32[16,512]{1,0:T(8,128)S(1)}, f32[16,512]{1,0:T(8,128)S(1)}, u32[]{:S(2)}, u32[]{:S(2)}) collective-permute-start(f32[16,512]{1,0:T(8,128)S(1)} %bitcast.6), channel_id=1, source_target_pairs={{0,1},{1,2},{2,3},{3,4},{4,5},{5,6},{6,7},{7,8},{8,9},{9,10},{10,1... | collective-permute-start | bytes 98312 | tf_op jit(solution)/shard_map/ppermute | solution.py:272
  5.2 0.0 collective-permute-start.1
  5.2 0.0 copy-start
  5.2 1.2 %copy-done = f32[16,32,512]{2,1,0:T(8,128)S(1)} copy-done((f32[16,32,512]{2,1,0:T(8,128)S(1)}, f32[16,32,512]{2,1,0:T(8,128)}, u32[]{:S(2)}) %copy-start) | copy-done | bytes 1048600
  6.4 0.0 copy-start.4
  6.4 1.2 %copy-done.4 = f32[16,32,512]{2,1,0:T(8,128)S(1)} copy-done((f32[16,32,512]{2,1,0:T(8,128)S(1)}, f32[16,32,512]{2,1,0:T(8,128)}, u32[]{:S(2)}) %copy-start.4) | copy-done | bytes 1048600
  7.6 0.0 copy-start.5
  7.6 1.2 %copy-done.5 = f32[16,32,512]{2,1,0:T(8,128)S(1)} copy-done((f32[16,32,512]{2,1,0:T(8,128)S(1)}, f32[16,32,512]{2,1,0:T(8,128)}, u32[]{:S(2)}) %copy-start.5) | copy-done | bytes 1048600
  8.8 0.0 copy-start.1
  8.8 0.0 copy-start.2
  8.8 0.0 copy-start.3
  8.8 1.0 %shard_map.68 = (f32[16,32,512]{2,1,0:T(8,128)S(1)}, f32[16,32,512]{2,1,0:T(8,128)S(1)}, f32[16,32,512]{2,1,0:T(8,128)S(1)}, f32[16,32,512]{2,1,0:T(8,128)S(1)}, f32[16,3,8,128]{3,2,1,0:T(8,128)S(1)}) custom-call(f32[16,32,512]{2,1,0:T(8,128)S(1)} %copy-done.4, f32[16,32,512]{2,1,0:T(8,128)S(1)} %copy-done.5, f32[16,32,512]{2,1,0:T(8,128)S(1)} %copy-done), custom_call_target="tpu_custom_call" | custom-call | flops 20000000 | bytes 7536640 | tf_op jit(solution)/shard_map/pallas_call | solution.py:260
  9.8 0.0 collective-permute-done.below
  9.8 0.0 collective-permute-done.1.above
  9.8 0.2 copy-done.1
  10.1 0.3 copy-done.2
  10.4 0.3 copy-done.3
  10.7 0.8 %shard_map.69 = (f32[16,32,512]{2,1,0:T(8,128)S(1)}, f32[16,5,8,128]{3,2,1,0:T(8,128)S(1)}) custom-call(f32[16,32,512]{2,1,0:T(8,128)S(1)} %copy-done.3, f32[16,512]{1,0:T(8,128)S(1)} %collective-permute-done.below, f32[16,512]{1,0:T(8,128)S(1)} %collective-permute-done.1.above, f32[16,32,512]{2,1,0:T(8,128)S(1)} %copy-done.1, f32[16,32,512]{2,1,0:T(8,128)S(1)} %copy-done.2, ...), custom_call_target="tpu_custom_call" | custom-call | flops 1000000 | bytes 5832704 | tf_op jit(solution)/shard_map/pallas_call | solution.py:260
  11.5 16.0 %all_to_all.15.got = f32[16,5,8,128]{3,2,1,0:T(8,128)S(1)} all-to-all(f32[16,5,8,128]{3,2,1,0:T(8,128)S(1)} %get-tuple-element.20), channel_id=1, replica_groups=mesh['rad'=16,'azi'=16] {'rad'}, dimensions={0} | all-to-all | bytes 655360 | tf_op jit(solution)/shard_map/all_to_all | solution.py:278
  27.6 0.2 shard_map.70
  27.7 12.0 %all_to_all.16.got = f32[16,6,8,128]{3,2,1,0:T(8,128)S(1)} all-to-all(f32[16,6,8,128]{3,2,1,0:T(8,128)S(1)} %shard_map.70), channel_id=1, replica_groups=mesh['rad'=16,'azi'=16] {'rad'}, dimensions={0} | all-to-all | bytes 786432 | tf_op jit(solution)/shard_map/all_to_all | solution.py:278
  39.8 0.2 shard_map.71
  39.9 3.0 %collective-permute-start.2 = (f32[16,512]{1,0:T(8,128)S(1)}, f32[16,512]{1,0:T(8,128)S(1)}, u32[]{:S(2)}, u32[]{:S(2)}) collective-permute-start(f32[16,512]{1,0:T(8,128)S(1)} %get-tuple-element.22), channel_id=1, source_target_pairs={{0,1},{1,2},{2,3},{3,4},{4,5},{5,6},{6,7},{7,8},{8,9},{9,10},{10,1... | collective-permute-start | bytes 98312 | tf_op jit(solution)/shard_map/ppermute | solution.py:272
  43.0 0.0 collective-permute-start.3
  43.0 1.0 %collective-permute-done.2.below = f32[16,512]{1,0:T(8,128)S(1)} collective-permute-done((f32[16,512]{1,0:T(8,128)S(1)}, f32[16,512]{1,0:T(8,128)S(1)}, u32[]{:S(2)}, u32[]{:S(2)}) %collective-permute-start.2) | collective-permute-done | bytes 32800 | tf_op jit(solution)/shard_map/ppermute | solution.py:272
  44.0 3.5 %collective-permute-done.3.above = f32[16,512]{1,0:T(8,128)S(1)} collective-permute-done((f32[16,512]{1,0:T(8,128)S(1)}, f32[16,512]{1,0:T(8,128)S(1)}, u32[]{:S(2)}, u32[]{:S(2)}) %collective-permute-start.3) | collective-permute-done | bytes 32800 | tf_op jit(solution)/shard_map/ppermute | solution.py:273
  47.5 1.0 %shard_map.72 = (f32[16,32,512]{2,1,0:T(8,128)S(1)}, f32[16,32,512]{2,1,0:T(8,128)S(1)}, f32[2,32,512]{2,1,0:T(8,128)S(1)}) custom-call(f32[16,32,512]{2,1,0:T(8,128)S(1)} %get-tuple-element.21.old, f32[16,512]{1,0:T(8,128)S(1)} %collective-permute-done.2.below, f32[16,512]{1,0:T(8,128)S(1)} %collective-permute-done.3.above, f32[16,32,512]{2,1,0:T(8,128)S(1)} %copy-done.1, ...), custom_call_target="tpu_custom_call" | custom-call | flops 1000000 | bytes 6881280 | tf_op jit(solution)/shard_map/pallas_call | solution.py:260
  48.5 18.3 %all_to_all.17.arrived = f32[16,32,512]{2,1,0:T(8,128)S(1)} all-to-all(f32[16,32,512]{2,1,0:T(8,128)S(1)} %get-tuple-element.27), channel_id=1, replica_groups=mesh['rad'=16,'azi'=16] {'rad'}, dimensions={0} | all-to-all | bytes 2097152 | tf_op jit(solution)/shard_map/all_to_all | solution.py:278
  66.8 1.7 %shard_map.73 = (f32[16,32,512]{2,1,0:T(8,128)}, f32[16,32,512]{2,1,0:T(8,128)}) custom-call(f32[16,32,512]{2,1,0:T(8,128)S(1)} %get-tuple-element.24.particular, f32[16,32,512]{2,1,0:T(8,128)S(1)} %get-tuple-element.18.left_map, f32[16,32,512]{2,1,0:T(8,128)S(1)} %get-tuple-element.19.right_map, f32[16,32,512]{2,1,0:T(8,128)S(1)} %get-tuple-element.25.factor, ...), custom_call_target="tpu_custom_call" | custom-call | flops 1000000 | bytes 7864320 | tf_op jit(solution)/shard_map/pallas_call | solution.py:260
  (2 shorter events, 0.0 us)
Async XLA Ops:
  1.7 8.1 %collective-permute-start = (f32[16,512]{1,0:T(8,128)S(1)}, f32[16,512]{1,0:T(8,128)S(1)}, u32[]{:S(2)}, u32[]{:S(2)}) collective-permute-start(f32[16,512]{1,0:T(8,128)S(1)} %bitcast.6), channel_id=1, source_target_pairs={{0,1},{1,2},{2,3},{3,4},{4,5},{5,6},{6,7},{7,8},{8,9},{9,10},{10,1... | collective-permute-start | bytes 98312 | tf_op jit(solution)/shard_map/ppermute | solution.py:272
  5.2 4.7 %collective-permute-start.1 = (f32[16,512]{1,0:T(8,128)S(1)}, f32[16,512]{1,0:T(8,128)S(1)}, u32[]{:S(2)}, u32[]{:S(2)}) collective-permute-start(f32[16,512]{1,0:T(8,128)S(1)} %bitcast.7), channel_id=1, source_target_pairs={{1,0},{2,1},{3,2},{4,3},{5,4},{6,5},{7,6},{8,7},{9,8},{10,9},{11,1... | collective-permute-start | bytes 98312 | tf_op jit(solution)/shard_map/ppermute | solution.py:273
  5.2 1.2 %copy-start = (f32[16,32,512]{2,1,0:T(8,128)S(1)}, f32[16,32,512]{2,1,0:T(8,128)}, u32[]{:S(2)}) copy-start(f32[16,32,512]{2,1,0:T(8,128)} %flux.5) | copy-start | bytes 3145732
  6.4 1.2 %copy-start.4 = (f32[16,32,512]{2,1,0:T(8,128)S(1)}, f32[16,32,512]{2,1,0:T(8,128)}, u32[]{:S(2)}) copy-start(f32[16,32,512]{2,1,0:T(8,128)} %heat.1) | copy-start | bytes 3145732
  7.6 1.2 %copy-start.5 = (f32[16,32,512]{2,1,0:T(8,128)S(1)}, f32[16,32,512]{2,1,0:T(8,128)}, u32[]{:S(2)}) copy-start(f32[16,32,512]{2,1,0:T(8,128)} %deform.1) | copy-start | bytes 3145732
  8.8 1.2 %copy-start.1 = (f32[16,32,512]{2,1,0:T(8,128)S(1)}, f32[16,32,512]{2,1,0:T(8,128)}, u32[]{:S(2)}) copy-start(f32[16,32,512]{2,1,0:T(8,128)} %flux.5) | copy-start | bytes 3145732
  8.8 1.5 %copy-start.2 = (f32[16,32,512]{2,1,0:T(8,128)S(1)}, f32[16,32,512]{2,1,0:T(8,128)}, u32[]{:S(2)}) copy-start(f32[16,32,512]{2,1,0:T(8,128)} %goal.3) | copy-start | bytes 3145732
  8.8 1.9 %copy-start.3 = (f32[16,32,512]{2,1,0:T(8,128)S(1)}, f32[16,32,512]{2,1,0:T(8,128)}, u32[]{:S(2)}) copy-start(f32[16,32,512]{2,1,0:T(8,128)} %old.1) | copy-start | bytes 3145732
  39.9 4.1 %collective-permute-start.2 = (f32[16,512]{1,0:T(8,128)S(1)}, f32[16,512]{1,0:T(8,128)S(1)}, u32[]{:S(2)}, u32[]{:S(2)}) collective-permute-start(f32[16,512]{1,0:T(8,128)S(1)} %get-tuple-element.22), channel_id=1, source_target_pairs={{0,1},{1,2},{2,3},{3,4},{4,5},{5,6},{6,7},{7,8},{8,9},{9,10},{10,1... | collective-permute-start | bytes 98312 | tf_op jit(solution)/shard_map/ppermute | solution.py:272
  43.0 4.6 %collective-permute-start.3 = (f32[16,512]{1,0:T(8,128)S(1)}, f32[16,512]{1,0:T(8,128)S(1)}, u32[]{:S(2)}, u32[]{:S(2)}) collective-permute-start(f32[16,512]{1,0:T(8,128)S(1)} %get-tuple-element.23), channel_id=1, source_target_pairs={{1,0},{2,1},{3,2},{4,3},{5,4},{6,5},{7,6},{8,7},{9,8},{10,9},{11,1... | collective-permute-start | bytes 98312 | tf_op jit(solution)/shard_map/ppermute | solution.py:273

commit v2 on v1

--- a/solution.py
+++ b/solution.py
@@ -15,6 +15,7 @@
 slope_weight = 2.0
 
 SUB, LANE = 8, 128
+GROUP = 4
 F32 = jnp.float32
 
 
@@ -212,11 +213,9 @@
                 high_edge[i : i + 1, :] = value[SUB - 1 : SUB, :]
 
 
-def third_kernel(old, below, above, flux, goal, ratio, got, particular, message, own):
+def third_kernel(old, below, above, flux, goal, ratio, got, particular, own):
     rows, azimuths, width = old.shape
     links, radii, inverse_links, quarter = tables(rows, width)
-    segments = message.shape[0]
-    me = lax.axis_index("rad")
     for group in range(azimuths // SUB):
         here = pl.ds(group * SUB, SUB)
         source = sources(group, old, below, above, flux, goal, radii, quarter)
@@ -226,28 +225,45 @@
         downward = tiles_of(got, group, 4, width) * inner + tiles_of(got, group, 5, width) * outer
         own[0, here, :] = upward
         own[1, here, :] = downward
-        for s in range(segments):
-            message[s, here, :] = jnp.where(s > me, upward, downward)
-
-
-def last_kernel(particular, left_map, right_map, factor, got, own, arrived, result, sensitivity):
+
+
+def gather_kernel(own, first, second, third, near, message):
+    mine = lax.rem(lax.axis_index("rad"), GROUP)
+    block = lax.div(lax.axis_index("rad"), GROUP)
+    for group in range(own.shape[1] // SUB):
+        here = pl.ds(group * SUB, SUB)
+        upward, downward = own[0, here, :], own[1, here, :]
+        lower, upper = jnp.zeros_like(upward), downward
+        for flip, other in ((1, first), (2, second), (3, third)):
+            up, down = other[0, here, :], other[1, here, :]
+            upward = upward + up
+            downward = downward + down
+            below = (mine ^ flip) < mine
+            lower = lower + jnp.where(below, up, 0.0)
+            upper = upper + jnp.where(below, 0.0, down)
+        near[0, here, :] = lower
+        near[1, here, :] = upper
+        for slot, flip in ((0, 1), (1, 2)):
+            message[slot, here, :] = jnp.where((block ^ flip) > block, upward, downward)
+
+
+def last_kernel(
+    particular, left_map, right_map, factor, got, own, near, first, second, third, result, sensitivity
+):
     rows, azimuths, width = particular.shape
-    segments = arrived.shape[0]
-    me = lax.axis_index("rad")
-    for group in range(azimuths // SUB):
-        here = pl.ds(group * SUB, SUB)
-        lower = jnp.zeros((SUB, width), F32)
-        upper = jnp.zeros((SUB, width), F32)
-        for s in range(segments):
-            item = arrived[s, here, :]
-            lower = lower + jnp.where(s < me, item, 0.0)
-            upper = upper + jnp.where(s > me, item, 0.0)
-        left = tiles_of(got, group, 4, width) * lower + tiles_of(got, group, 2, width) * (
-            own[1, here, :] + upper
-        )
+    block = lax.div(lax.axis_index("rad"), GROUP)
+    for group in range(azimuths // SUB):
+        here = pl.ds(group * SUB, SUB)
+        lower, upper = near[0, here, :], near[1, here, :]
+        for flip, other in ((1, first), (2, second), (3, third)):
+            item = other[here, :]
+            below = (block ^ flip) < block
+            lower = lower + jnp.where(below, item, 0.0)
+            upper = upper + jnp.where(below, 0.0, item)
+        left = tiles_of(got, group, 4, width) * lower + tiles_of(got, group, 2, width) * upper
         right = (
             tiles_of(got, group, 5, width) * (lower + own[0, here, :])
-            + tiles_of(got, group, 3, width) * upper
+            + tiles_of(got, group, 3, width) * (upper - own[1, here, :])
         )
         for i in range(rows):
             value = particular[i, here, :] + left_map[i, here, :] * left + right_map[i, here, :] * right
@@ -274,6 +290,10 @@
     return below, above
 
 
+def flip_permute(value, flip):
+    return lax.ppermute(value, "rad", [(i, i ^ flip) for i in range(lax.axis_size("rad"))])
+
+
 def exchange(value):
     return lax.all_to_all(value, "rad", 0, 0, tiled=True)
 
@@ -305,24 +325,22 @@
         second_kernel, (block, edge, edge), particular, left_map, right_map, got
     )
     below, above = swap_edges(low_edge, high_edge)
-    particular, message, own = call(
-        third_kernel,
-        (
-            block,
-            jax.ShapeDtypeStruct((segments, azimuths, width), F32),
-            jax.ShapeDtypeStruct((2, azimuths, width), F32),
-        ),
-        new,
-        below,
-        above,
-        flux,
-        goal,
-        ratio,
+    pair = jax.ShapeDtypeStruct((2, azimuths, width), F32)
+    particular, own = call(third_kernel, (block, pair), new, below, above, flux, goal, ratio, got)
+    others = [flip_permute(own, flip) for flip in (1, 2, 3)]
+    near, message = call(gather_kernel, (pair, pair), own, *others)
+    far = [flip_permute(message[min(flip, 2) - 1], flip * GROUP) for flip in (1, 2, 3)]
+    return call(
+        last_kernel,
+        (block, block),
+        particular,
+        left_map,
+        right_map,
+        factor,
         got,
-    )
-    arrived = exchange(message)
-    return call(
-        last_kernel, (block, block), particular, left_map, right_map, factor, got, own, arrived
+        own,
+        near,
+        *far,
     )
 
 

time: 68.8 us -> 64.8 us (0.942)
  the two profiles are of different devices: /device:TPU:97 before, /device:TPU:64 now
where the time goes in v2:
time: 64.8 us; the launch traced here: 64 us
  blocking collectives  29.1 us (45%)
  waiting for transfers between devices  12.1 us (19%)
  starting transfers between devices  11.8 us (18%)
  local copies, waits for them, and re-layouts  5.65 us (9%)
  Pallas kernels  4.58 us (7%)
  between operations  0.74 us (1%)
    all_to_all x2, blocking collectives, exchange(): return lax.all_to_all(value, 'rad', 0, 0, tiled=True)  29.1 us
    ppermute x6, waiting for transfers between devices, flip_permute(): lax.ppermute(value, 'rad', [(i, i ^ flip) for i in range(lax.axis_size('r...  9.38 us
    ppermute x6, starting transfers between devices, flip_permute(): lax.ppermute(value, 'rad', [(i, i ^ flip) for i in range(lax.axis_size('r...  8.35 us
    pallas_call x7, Pallas kernels, call(): pl.pallas_call(kernel, out_shape=outs, in_specs=[pl.BlockSpec(memory_spac...  4.58 us
    unnamed x14, local copies, waits for them, and re-layouts  4.56 us
    ppermute x2, starting transfers between devices, swap_edges(): lax.ppermute(low_edge, 'azi', [((i + 1) % count, i) for i in range(count)])  3.46 us
    ppermute x2, waiting for transfers between devices, swap_edges(): lax.ppermute(high_edge, 'azi', [(i, (i + 1) % count) for i in range(count)])  1.6 us
  transfers between devices with their start and end apart: 10, of which 7 were waited for; matrix products, arithmetic and copies ran while one was open for 0% of the time, Pallas kernels for 1%

profile of v2, /device:TPU:64, one launch (start us, length us, event | category | flops | bytes accessed | tf_op | source)
XLA Modules:
  0.0 64.0 jit_solution(10121538008515573659)
XLA Ops:
  0.6 1.1 %fusion = (f32[16,1,512]{2,1,0:T(1,128)S(1)}, f32[16,1,512]{2,1,0:T(1,128)S(1)}) fusion(f32[16,32,512]{2,1,0:T(8,128)} %old.1), kind=kLoop, calls=%fused_computation.4 | loop fusion | bytes 131072 | tf_op jit(solution)/shard_map/slice | solution.py:311
  1.7 0.0 collective-permute-start
  1.8 1.7 %collective-permute-start.1 = (f32[16,512]{1,0:T(8,128)S(1)}, f32[16,512]{1,0:T(8,128)S(1)}, u32[]{:S(2)}, u32[]{:S(2)}) collective-permute-start(f32[16,512]{1,0:T(8,128)S(1)} %bitcast.11), channel_id=1, source_target_pairs={{1,0},{2,1},{3,2},{4,3},{5,4},{6,5},{7,6},{8,7},{9,8},{10,9},{11,1... | collective-permute-start | bytes 98312 | tf_op jit(solution)/shard_map/ppermute | solution.py:289
  3.5 0.0 copy-start
  3.5 1.2 %copy-done = f32[16,32,512]{2,1,0:T(8,128)S(1)} copy-done((f32[16,32,512]{2,1,0:T(8,128)S(1)}, f32[16,32,512]{2,1,0:T(8,128)}, u32[]{:S(2)}) %copy-start) | copy-done | bytes 1048600
  4.7 0.0 copy-start.4
  4.7 1.2 %copy-done.4 = f32[16,32,512]{2,1,0:T(8,128)S(1)} copy-done((f32[16,32,512]{2,1,0:T(8,128)S(1)}, f32[16,32,512]{2,1,0:T(8,128)}, u32[]{:S(2)}) %copy-start.4) | copy-done | bytes 1048600
  5.9 0.0 copy-start.5
  5.9 1.2 %copy-done.5 = f32[16,32,512]{2,1,0:T(8,128)S(1)} copy-done((f32[16,32,512]{2,1,0:T(8,128)S(1)}, f32[16,32,512]{2,1,0:T(8,128)}, u32[]{:S(2)}) %copy-start.5) | copy-done | bytes 1048600
  7.2 0.0 copy-start.1
  7.2 0.0 copy-start.2
  7.2 0.0 copy-start.3
  7.2 1.0 %shard_map.68 = (f32[16,32,512]{2,1,0:T(8,128)S(1)}, f32[16,32,512]{2,1,0:T(8,128)S(1)}, f32[16,32,512]{2,1,0:T(8,128)S(1)}, f32[16,32,512]{2,1,0:T(8,128)S(1)}, f32[16,3,8,128]{3,2,1,0:T(8,128)S(1)}) custom-call(f32[16,32,512]{2,1,0:T(8,128)S(1)} %copy-done.4, f32[16,32,512]{2,1,0:T(8,128)S(1)} %copy-done.5, f32[16,32,512]{2,1,0:T(8,128)S(1)} %copy-done), custom_call_target="tpu_custom_call" | custom-call | flops 20000000 | bytes 7536640 | tf_op jit(solution)/shard_map/pallas_call | solution.py:276
  8.1 0.0 collective-permute-done.below
  8.1 0.0 collective-permute-done.1.above
  8.2 0.2 copy-done.1
  8.4 0.3 copy-done.2
  8.7 0.3 copy-done.3
  9.0 0.8 %shard_map.69 = (f32[16,32,512]{2,1,0:T(8,128)S(1)}, f32[16,5,8,128]{3,2,1,0:T(8,128)S(1)}) custom-call(f32[16,32,512]{2,1,0:T(8,128)S(1)} %copy-done.3, f32[16,512]{1,0:T(8,128)S(1)} %collective-permute-done.below, f32[16,512]{1,0:T(8,128)S(1)} %collective-permute-done.1.above, f32[16,32,512]{2,1,0:T(8,128)S(1)} %copy-done.1, f32[16,32,512]{2,1,0:T(8,128)S(1)} %copy-done.2, ...), custom_call_target="tpu_custom_call" | custom-call | flops 1000000 | bytes 5832704 | tf_op jit(solution)/shard_map/pallas_call | solution.py:276
  9.9 16.7 %all_to_all.10.got = f32[16,5,8,128]{3,2,1,0:T(8,128)S(1)} all-to-all(f32[16,5,8,128]{3,2,1,0:T(8,128)S(1)} %get-tuple-element.21), channel_id=1, replica_groups=mesh['rad'=16,'azi'=16] {'rad'}, dimensions={0} | all-to-all | bytes 655360 | tf_op jit(solution)/shard_map/all_to_all | solution.py:298
  26.5 0.2 shard_map.70
  26.7 12.4 %all_to_all.11.got = f32[16,6,8,128]{3,2,1,0:T(8,128)S(1)} all-to-all(f32[16,6,8,128]{3,2,1,0:T(8,128)S(1)} %shard_map.70), channel_id=1, replica_groups=mesh['rad'=16,'azi'=16] {'rad'}, dimensions={0} | all-to-all | bytes 786432 | tf_op jit(solution)/shard_map/all_to_all | solution.py:298
  39.1 0.2 shard_map.71
  39.3 0.0 collective-permute-start.2
  39.3 1.7 %collective-permute-start.3 = (f32[16,512]{1,0:T(8,128)S(1)}, f32[16,512]{1,0:T(8,128)S(1)}, u32[]{:S(2)}, u32[]{:S(2)}) collective-permute-start(f32[16,512]{1,0:T(8,128)S(1)} %get-tuple-element.24), channel_id=1, source_target_pairs={{1,0},{2,1},{3,2},{4,3},{5,4},{6,5},{7,6},{8,7},{9,8},{10,9},{11,1... | collective-permute-start | bytes 98312 | tf_op jit(solution)/shard_map/ppermute | solution.py:289
  41.1 1.6 %collective-permute-done.2.below = f32[16,512]{1,0:T(8,128)S(1)} collective-permute-done((f32[16,512]{1,0:T(8,128)S(1)}, f32[16,512]{1,0:T(8,128)S(1)}, u32[]{:S(2)}, u32[]{:S(2)}) %collective-permute-start.2) | collective-permute-done | bytes 32800 | tf_op jit(solution)/shard_map/ppermute | solution.py:288
  42.6 1.1 %collective-permute-done.3.above = f32[16,512]{1,0:T(8,128)S(1)} collective-permute-done((f32[16,512]{1,0:T(8,128)S(1)}, f32[16,512]{1,0:T(8,128)S(1)}, u32[]{:S(2)}, u32[]{:S(2)}) %collective-permute-start.3) | collective-permute-done | bytes 32800 | tf_op jit(solution)/shard_map/ppermute | solution.py:289
  43.7 0.8 %shard_map.72 = (f32[16,32,512]{2,1,0:T(8,128)S(1)}, f32[2,32,512]{2,1,0:T(8,128)S(1)}) custom-call(f32[16,32,512]{2,1,0:T(8,128)S(1)} %get-tuple-element.22.old, f32[16,512]{1,0:T(8,128)S(1)} %collective-permute-done.2.below, f32[16,512]{1,0:T(8,128)S(1)} %collective-permute-done.3.above, f32[16,32,512]{2,1,0:T(8,128)S(1)} %copy-done.1, ...), custom_call_target="tpu_custom_call" | custom-call | flops 1000000 | bytes 5832704 | tf_op jit(solution)/shard_map/pallas_call | solution.py:276
  44.6 0.6 %collective-permute-start.6 = (f32[2,32,512]{2,1,0:T(8,128)S(1)}, f32[2,32,512]{2,1,0:T(8,128)S(1)}, u32[]{:S(2)}, u32[]{:S(2)}) collective-permute-start(f32[2,32,512]{2,1,0:T(8,128)S(1)} %get-tuple-element.27.own), channel_id=1, source_target_pairs={{0,48},{16,32},{32,16},{48,0},{64,112},{80,96},{96,80},{112,64},{1... | collective-permute-start | bytes 393224 | tf_op jit(solution)/shard_map/ppermute | solution.py:294
  45.2 2.1 %collective-permute-start.5 = (f32[2,32,512]{2,1,0:T(8,128)S(1)}, f32[2,32,512]{2,1,0:T(8,128)S(1)}, u32[]{:S(2)}, u32[]{:S(2)}) collective-permute-start(f32[2,32,512]{2,1,0:T(8,128)S(1)} %get-tuple-element.27.own), channel_id=1, source_target_pairs={{0,32},{16,48},{32,0},{48,16},{64,96},{80,112},{96,64},{112,80},{1... | collective-permute-start | bytes 393224 | tf_op jit(solution)/shard_map/ppermute | solution.py:294
  47.3 1.5 %collective-permute-start.4 = (f32[2,32,512]{2,1,0:T(8,128)S(1)}, f32[2,32,512]{2,1,0:T(8,128)S(1)}, u32[]{:S(2)}, u32[]{:S(2)}) collective-permute-start(f32[2,32,512]{2,1,0:T(8,128)S(1)} %get-tuple-element.27.own), channel_id=1, source_target_pairs={{0,16},{16,0},{32,48},{48,32},{64,80},{80,64},{96,112},{112,96},{1... | collective-permute-start | bytes 393224 | tf_op jit(solution)/shard_map/ppermute | solution.py:294
  48.8 4.8 %collective-permute-done.6.third = f32[2,32,512]{2,1,0:T(8,128)S(1)} collective-permute-done((f32[2,32,512]{2,1,0:T(8,128)S(1)}, f32[2,32,512]{2,1,0:T(8,128)S(1)}, u32[]{:S(2)}, u32[]{:S(2)}) %collective-permute-start.6) | collective-permute-done | bytes 131104 | tf_op jit(solution)/shard_map/ppermute | solution.py:294
  53.5 0.0 collective-permute-done.5.second
  53.5 1.0 %collective-permute-done.4.first = f32[2,32,512]{2,1,0:T(8,128)S(1)} collective-permute-done((f32[2,32,512]{2,1,0:T(8,128)S(1)}, f32[2,32,512]{2,1,0:T(8,128)S(1)}, u32[]{:S(2)}, u32[]{:S(2)}) %collective-permute-start.4) | collective-permute-done | bytes 131104 | tf_op jit(solution)/shard_map/ppermute | solution.py:294
  54.5 0.1 shard_map.73
  54.6 0.1 collective-permute-start.7
  54.7 1.4 %collective-permute-start.9 = (f32[32,512]{1,0:T(8,128)S(1)}, f32[32,512]{1,0:T(8,128)S(1)}, u32[]{:S(2)}, u32[]{:S(2)}) collective-permute-start(f32[32,512]{1,0:T(8,128)S(1)} %get-tuple-element.32), channel_id=1, source_target_pairs={{0,192},{16,208},{32,224},{48,240},{64,128},{80,144},{96,160},{112... | collective-permute-start | bytes 196616 | tf_op jit(solution)/shard_map/ppermute | solution.py:294
  56.1 2.7 %collective-permute-start.8 = (f32[32,512]{1,0:T(8,128)S(1)}, f32[32,512]{1,0:T(8,128)S(1)}, u32[]{:S(2)}, u32[]{:S(2)}) collective-permute-start(f32[32,512]{1,0:T(8,128)S(1)} %get-tuple-element.32), channel_id=1, source_target_pairs={{0,128},{16,144},{32,160},{48,176},{64,192},{80,208},{96,224},{112... | collective-permute-start | bytes 196616 | tf_op jit(solution)/shard_map/ppermute | solution.py:294
  58.8 0.6 collective-permute-done.7.first
  59.4 1.3 %collective-permute-done.9.third = f32[32,512]{1,0:T(8,128)S(1)} collective-permute-done((f32[32,512]{1,0:T(8,128)S(1)}, f32[32,512]{1,0:T(8,128)S(1)}, u32[]{:S(2)}, u32[]{:S(2)}) %collective-permute-start.9) | collective-permute-done | bytes 65568 | tf_op jit(solution)/shard_map/ppermute | solution.py:294
  60.7 1.7 %collective-permute-done.8.second = f32[32,512]{1,0:T(8,128)S(1)} collective-permute-done((f32[32,512]{1,0:T(8,128)S(1)}, f32[32,512]{1,0:T(8,128)S(1)}, u32[]{:S(2)}, u32[]{:S(2)}) %collective-permute-start.8) | collective-permute-done | bytes 65568 | tf_op jit(solution)/shard_map/ppermute | solution.py:294
  62.4 1.6 %shard_map.74 = (f32[16,32,512]{2,1,0:T(8,128)}, f32[16,32,512]{2,1,0:T(8,128)}) custom-call(f32[16,32,512]{2,1,0:T(8,128)S(1)} %get-tuple-element.25.particular, f32[16,32,512]{2,1,0:T(8,128)S(1)} %get-tuple-element.19.left_map, f32[16,32,512]{2,1,0:T(8,128)S(1)} %get-tuple-element.20.right_map, f32[16,32,512]{2,1,0:T(8,128)S(1)} %get-tuple-element.26.factor, ...), custom_call_target="tpu_custom_call" | custom-call | flops 1000000 | bytes 7143424 | tf_op jit(solution)/shard_map/pallas_call | solution.py:276
  (3 shorter events, 0.0 us)
Async XLA Ops:
  1.7 6.4 %collective-permute-start = (f32[16,512]{1,0:T(8,128)S(1)}, f32[16,512]{1,0:T(8,128)S(1)}, u32[]{:S(2)}, u32[]{:S(2)}) collective-permute-start(f32[16,512]{1,0:T(8,128)S(1)} %bitcast.10), channel_id=1, source_target_pairs={{0,1},{1,2},{2,3},{3,4},{4,5},{5,6},{6,7},{7,8},{8,9},{9,10},{10,1... | collective-permute-start | bytes 98312 | tf_op jit(solution)/shard_map/ppermute | solution.py:288
  1.8 6.4 %collective-permute-start.1 = (f32[16,512]{1,0:T(8,128)S(1)}, f32[16,512]{1,0:T(8,128)S(1)}, u32[]{:S(2)}, u32[]{:S(2)}) collective-permute-start(f32[16,512]{1,0:T(8,128)S(1)} %bitcast.11), channel_id=1, source_target_pairs={{1,0},{2,1},{3,2},{4,3},{5,4},{6,5},{7,6},{8,7},{9,8},{10,9},{11,1... | collective-permute-start | bytes 98312 | tf_op jit(solution)/shard_map/ppermute | solution.py:289
  3.5 1.2 %copy-start = (f32[16,32,512]{2,1,0:T(8,128)S(1)}, f32[16,32,512]{2,1,0:T(8,128)}, u32[]{:S(2)}) copy-start(f32[16,32,512]{2,1,0:T(8,128)} %flux.5) | copy-start | bytes 3145732
  4.7 1.2 %copy-start.4 = (f32[16,32,512]{2,1,0:T(8,128)S(1)}, f32[16,32,512]{2,1,0:T(8,128)}, u32[]{:S(2)}) copy-start(f32[16,32,512]{2,1,0:T(8,128)} %heat.1) | copy-start | bytes 3145732
  5.9 1.2 %copy-start.5 = (f32[16,32,512]{2,1,0:T(8,128)S(1)}, f32[16,32,512]{2,1,0:T(8,128)}, u32[]{:S(2)}) copy-start(f32[16,32,512]{2,1,0:T(8,128)} %deform.1) | copy-start | bytes 3145732
  7.2 1.2 %copy-start.1 = (f32[16,32,512]{2,1,0:T(8,128)S(1)}, f32[16,32,512]{2,1,0:T(8,128)}, u32[]{:S(2)}) copy-start(f32[16,32,512]{2,1,0:T(8,128)} %flux.5) | copy-start | bytes 3145732
  7.2 1.5 %copy-start.2 = (f32[16,32,512]{2,1,0:T(8,128)S(1)}, f32[16,32,512]{2,1,0:T(8,128)}, u32[]{:S(2)}) copy-start(f32[16,32,512]{2,1,0:T(8,128)} %goal.3) | copy-start | bytes 3145732
  7.2 1.9 %copy-start.3 = (f32[16,32,512]{2,1,0:T(8,128)S(1)}, f32[16,32,512]{2,1,0:T(8,128)}, u32[]{:S(2)}) copy-start(f32[16,32,512]{2,1,0:T(8,128)} %old.1) | copy-start | bytes 3145732
  39.3 3.4 %collective-permute-start.2 = (f32[16,512]{1,0:T(8,128)S(1)}, f32[16,512]{1,0:T(8,128)S(1)}, u32[]{:S(2)}, u32[]{:S(2)}) collective-permute-start(f32[16,512]{1,0:T(8,128)S(1)} %get-tuple-element.23), channel_id=1, source_target_pairs={{0,1},{1,2},{2,3},{3,4},{4,5},{5,6},{6,7},{7,8},{8,9},{9,10},{10,1... | collective-permute-start | bytes 98312 | tf_op jit(solution)/shard_map/ppermute | solution.py:288
  39.3 4.4 %collective-permute-start.3 = (f32[16,512]{1,0:T(8,128)S(1)}, f32[16,512]{1,0:T(8,128)S(1)}, u32[]{:S(2)}, u32[]{:S(2)}) collective-permute-start(f32[16,512]{1,0:T(8,128)S(1)} %get-tuple-element.24), channel_id=1, source_target_pairs={{1,0},{2,1},{3,2},{4,3},{5,4},{6,5},{7,6},{8,7},{9,8},{10,9},{11,1... | collective-permute-start | bytes 98312 | tf_op jit(solution)/shard_map/ppermute | solution.py:289
  44.6 8.9 %collective-permute-start.6 = (f32[2,32,512]{2,1,0:T(8,128)S(1)}, f32[2,32,512]{2,1,0:T(8,128)S(1)}, u32[]{:S(2)}, u32[]{:S(2)}) collective-permute-start(f32[2,32,512]{2,1,0:T(8,128)S(1)} %get-tuple-element.27.own), channel_id=1, source_target_pairs={{0,48},{16,32},{32,16},{48,0},{64,112},{80,96},{96,80},{112,64},{1... | collective-permute-start | bytes 393224 | tf_op jit(solution)/shard_map/ppermute | solution.py:294
  45.2 8.3 %collective-permute-start.5 = (f32[2,32,512]{2,1,0:T(8,128)S(1)}, f32[2,32,512]{2,1,0:T(8,128)S(1)}, u32[]{:S(2)}, u32[]{:S(2)}) collective-permute-start(f32[2,32,512]{2,1,0:T(8,128)S(1)} %get-tuple-element.27.own), channel_id=1, source_target_pairs={{0,32},{16,48},{32,0},{48,16},{64,96},{80,112},{96,64},{112,80},{1... | collective-permute-start | bytes 393224 | tf_op jit(solution)/shard_map/ppermute | solution.py:294
  47.3 7.3 %collective-permute-start.4 = (f32[2,32,512]{2,1,0:T(8,128)S(1)}, f32[2,32,512]{2,1,0:T(8,128)S(1)}, u32[]{:S(2)}, u32[]{:S(2)}) collective-permute-start(f32[2,32,512]{2,1,0:T(8,128)S(1)} %get-tuple-element.27.own), channel_id=1, source_target_pairs={{0,16},{16,0},{32,48},{48,32},{64,80},{80,64},{96,112},{112,96},{1... | collective-permute-start | bytes 393224 | tf_op jit(solution)/shard_map/ppermute | solution.py:294
  54.6 4.8 %collective-permute-start.7 = (f32[32,512]{1,0:T(8,128)S(1)}, f32[32,512]{1,0:T(8,128)S(1)}, u32[]{:S(2)}, u32[]{:S(2)}) collective-permute-start(f32[32,512]{1,0:T(8,128)S(1)} %get-tuple-element.33), channel_id=1, source_target_pairs={{0,64},{16,80},{32,96},{48,112},{64,0},{80,16},{96,32},{112,48},{1... | collective-permute-start | bytes 196616 | tf_op jit(solution)/shard_map/ppermute | solution.py:294
  54.7 6.0 %collective-permute-start.9 = (f32[32,512]{1,0:T(8,128)S(1)}, f32[32,512]{1,0:T(8,128)S(1)}, u32[]{:S(2)}, u32[]{:S(2)}) collective-permute-start(f32[32,512]{1,0:T(8,128)S(1)} %get-tuple-element.32), channel_id=1, source_target_pairs={{0,192},{16,208},{32,224},{48,240},{64,128},{80,144},{96,160},{112... | collective-permute-start | bytes 196616 | tf_op jit(solution)/shard_map/ppermute | solution.py:294
  56.1 6.3 %collective-permute-start.8 = (f32[32,512]{1,0:T(8,128)S(1)}, f32[32,512]{1,0:T(8,128)S(1)}, u32[]{:S(2)}, u32[]{:S(2)}) collective-permute-start(f32[32,512]{1,0:T(8,128)S(1)} %get-tuple-element.32), channel_id=1, source_target_pairs={{0,128},{16,144},{32,160},{48,176},{64,192},{80,208},{96,224},{112... | collective-permute-start | bytes 196616 | tf_op jit(solution)/shard_map/ppermute | solution.py:294

commit v3 on v2

v3 whole, which is shorter than its diff:
```python
import jax
import jax.numpy as jnp
from jax import lax
from jax.experimental import pallas as pl
from jax.experimental.pallas import tpu as pltpu
from jax.sharding import PartitionSpec as P

radial_weight = 8.0
azimuth_weight = 0.25
axial_weight = 0.25
flow_weight = 0.5
mass_weight = 1.0
heat_weight = 0.25
arrhenius_exponent = 2.0
slope_weight = 2.0

SUB, LANE = 8, 128
GROUP = 4
F32 = jnp.float32


def geometry(rows):
    total = rows * lax.axis_size("rad")
    stiffness = radial_weight * rows * rows
    first = (lax.axis_index("rad") * rows).astype(F32)
    links = [stiffness + (stiffness / total) * (first + float(i)) for i in range(rows + 1)]
    radii = [1.0 + (first + (i + 0.5)) * (1.0 / total) for i in range(rows)]
    return links, radii


def splat(scalar):
    return jnp.full((1, LANE), scalar, F32)


def wide(row, width):
    return jnp.concatenate([row] * (width // LANE), axis=1)


def tiles_of(ref, group, plane, width):
    per = width // LANE
    return jnp.concatenate([ref[group * per + t, plane] for t in range(per)], axis=1)


def put_tiles(ref, group, plane, value):
    per = value.shape[1] // LANE
    for t in range(per):
        ref[group * per + t, plane] = value[:, t * LANE : (t + 1) * LANE]


def lane_next(value):
    width = value.shape[1]
    lane = lax.broadcasted_iota(jnp.int32, value.shape, 1)
    return jnp.where(lane == width - 1, 0.0, pltpu.roll(value, width - 1, 1))


def lane_prev(value):
    lane = lax.broadcasted_iota(jnp.int32, value.shape, 1)
    return jnp.where(lane == 0, 0.0, pltpu.roll(value, 1, 1))


def shunt_of(hot, size, drag_flux, radius, base):
    drag = jnp.exp(-arrhenius_exponent * (hot - 1.0)) * size
    heating = (heat_weight * arrhenius_exponent) * (drag * size)
    return drag, radius * (base + flow_weight * drag_flux + heating)


def ladder(shunts, links, inverse_links):
    rows = len(shunts)
    ratios, lefts = [], []
    through = jnp.full(shunts[0].shape, links[0], F32)
    pivot = shunts[0] + links[0]
    for i in range(rows):
        if i > 0:
            pivot = shunts[i] + ratios[-1] * pivot
        lefts.append(through)
        if i < rows - 1:
            step = links[i + 1] / (links[i + 1] + pivot)
            ratios.append(step)
            through = step * through
    from_left = jnp.zeros_like(through)
    from_right = jnp.ones_like(through)
    left_maps, right_maps = [from_left], [from_right]
    for i in range(rows - 2, -1, -1):
        from_left = ratios[i] * (lefts[i] * inverse_links[i + 1] + from_left)
        from_right = ratios[i] * from_right
        left_maps.append(from_left)
        right_maps.append(from_right)
    inner = links[0] * (1.0 - from_left)
    return ratios, left_maps[::-1], right_maps[::-1], (through, inner, pivot)


def base_shunts(radii):
    out = []
    for radius in radii:
        r = splat(radius)
        out.append(2.0 * azimuth_weight / (r * r) + (mass_weight + 2.0 * axial_weight))
    return out


def matrix_kernel(
    heat, deform, flux, ratio, left_map, right_map, factor, condensed, hot_in, size_in, flux_in, ready
):
    rows, azimuths, width = heat.shape
    groups = azimuths // SUB
    copies = []
    for group in range(groups):
        here = pl.ds(group * SUB, SUB)
        for k, (source, target) in enumerate(((heat, hot_in), (deform, size_in), (flux, flux_in))):
            copy = pltpu.make_async_copy(
                source.at[:, here, :], target.at[:, here, :], ready.at[group, k]
            )
            copy.start()
            copies.append(copy)
    links, radii = geometry(rows)
    inverse_links = [wide(1.0 / splat(link), width) for link in links]
    bases = [wide(base, width) for base in base_shunts(radii)]
    for group in range(groups):
        here = pl.ds(group * SUB, SUB)
        for copy in copies[3 * group : 3 * group + 3]:
            copy.wait()
        shunts = []
        for i in range(rows):
            hot = hot_in[i, here, :]
            drag, shunt = shunt_of(hot, size_in[i, here, :], flux_in[i, here, :], radii[i], bases[i])
            shunts.append(shunt)
            lane = lax.broadcasted_iota(jnp.int32, hot.shape, 1)
            rise = jnp.where(lane == width - 1, 0.0, pltpu.roll(hot, width - 1, 1) - hot)
            factor[i, here, :] = slope_weight * rise - (2.0 * heat_weight) * drag
        ratios, lefts, rights, ports = ladder(shunts, links, inverse_links)
        for i in range(rows):
            ratio[i, here, :] = ratios[i] if i < rows - 1 else jnp.zeros_like(hot)
            left_map[i, here, :] = lefts[i]
            right_map[i, here, :] = rights[i]
        for plane, port in enumerate(ports):
            put_tiles(condensed, group, plane, port)


def edge_kernel(heat, deform, flux, goal, old, low_edge, high_edge, held, ready):
    rows, azimuths, width = heat.shape
    spans = (pl.ds(0, SUB), pl.ds(azimuths - SUB, SUB))
    copies = []
    for k, source in enumerate((heat, deform, flux, goal, old)):
        for e in range(2):
            copy = pltpu.make_async_copy(source.at[:, spans[e], :], held.at[k, e], ready.at[k, e])
            copy.start()
            copies.append(copy)
    total = rows * lax.axis_size("rad")
    first = (lax.axis_index("rad") * rows).astype(F32)
    row = lax.broadcasted_iota(jnp.int32, (rows, width), 0).astype(F32)
    radius = 1.0 + (first + (row + 0.5)) * (1.0 / total)
    base = 2.0 * azimuth_weight / (radius * radius) + (mass_weight + 2.0 * axial_weight)
    quarter = azimuth_weight / radius
    for copy in copies:
        copy.wait()

    def line(k, e, at):
        return jnp.concatenate([held[k, e, i, at : at + 1, :] for i in range(rows)], axis=0)

    for e, (at, inner, out) in enumerate(((0, 1, low_edge), (SUB - 1, SUB - 2, high_edge))):
        moving = line(2, e, at)
        centre = line(4, e, at)
        _, shunt = shunt_of(line(0, e, at), line(1, e, at), moving, radius, base)
        out[0] = shunt
        out[1] = radius * explicit(centre, moving, line(3, e, at)) + quarter * line(4, e, inner)
        out[2] = centre


def explicit(centre, moving, given):
    after = lane_next(centre)
    return (
        given
        + axial_weight * (lane_prev(centre) + after)
        + flow_weight * moving * after
        + mass_weight * centre
    )


def sources(group, old, below, above, flux, goal, radii, quarter):
    rows, azimuths, width = old.shape
    here = pl.ds(group * SUB, SUB)
    sub = lax.broadcasted_iota(jnp.int32, (SUB, width), 0)
    out = []
    for i in range(rows):
        centre = old[i, here, :]
        low = below(i) if group == 0 else old[i, group * SUB - 1 : group * SUB, :]
        high = (
            above(i)
            if group == azimuths // SUB - 1
            else old[i, (group + 1) * SUB : (group + 1) * SUB + 1, :]
        )
        side = jnp.where(sub == 0, low, pltpu.roll(centre, 1, 0)) + jnp.where(
            sub == SUB - 1, high, pltpu.roll(centre, SUB - 1, 0)
        )
        right = explicit(centre, flux[i, here, :], goal[i, here, :])
        out.append(radii[i] * right + quarter[i] * side)
    return out


def substitute(source, ratios, inverse_links):
    rows = len(source)
    currents = [source[0]]
    for i in range(1, rows):
        currents.append(source[i] + ratios[i - 1] * currents[-1])
    value = jnp.zeros_like(source[0])
    values = [value]
    for i in range(rows - 2, -1, -1):
        value = ratios[i] * (currents[i] * inverse_links[i + 1] + value)
        values.append(value)
    return values[::-1], currents[-1]


def local_solve(group, source, ratio, inverse_links, particular):
    rows = len(source)
    here = pl.ds(group * SUB, SUB)
    ratios = [ratio[i, here, :] for i in range(rows - 1)]
    values, outer = substitute(source, ratios, inverse_links)
    for i in range(rows):
        particular[i, here, :] = values[i]
    return values[0], outer


def tables(rows, width):
    links, radii = geometry(rows)
    inverse_links = [wide(1.0 / splat(link), width) for link in links]
    quarter = [wide(azimuth_weight / splat(radius), width) for radius in radii]
    return links, radii, inverse_links, quarter


def pair_of(below, above):
    return jnp.concatenate([below, above], axis=0)


def first_kernel(
    old, below, above, flux, goal, ratio, condensed, particular, message, outside
):
    rows, azimuths, width = old.shape
    links, radii, inverse_links, quarter = tables(rows, width)
    tiles = message.shape[0]
    per = width // LANE
    message[:, 0:3] = condensed[...]
    message[:, 5] = jnp.ones((tiles, SUB, LANE), F32)

    shunts, source = [], []
    for i in range(rows):
        row = pl.ds(i, 1)
        shunts.append(pair_of(below[0, row, :], above[0, row, :]))
        beside = pair_of(old[i, 0:1, :], old[i, azimuths - 1 : azimuths, :])
        source.append(pair_of(below[1, row, :], above[1, row, :]) + quarter[i] * beside)
    ratios, lefts, rights, ports = ladder(shunts, links, inverse_links)
    values, outer = substitute(source, ratios, inverse_links)
    for i in range(rows):
        outside[0, i] = values[i]
        outside[1, i] = lefts[i]
        outside[2, i] = rights[i]
    for plane, port in enumerate((*ports, links[0] * values[0], outer)):
        for e in range(2):
            for t in range(per):
                message[e * per + t, 5, plane : plane + 1, :] = port[
                    e : e + 1, t * LANE : (t + 1) * LANE
                ]

    for group in range(azimuths // SUB):
        source = sources(
            group,
            old,
            lambda i: below[2, i : i + 1, :],
            lambda i: above[2, i : i + 1, :],
            flux,
            goal,
            radii,
            quarter,
        )
        inner, outer = local_solve(group, source, ratio, inverse_links, particular)
        put_tiles(message, group, 3, links[0] * inner)
        put_tiles(message, group, 4, outer)


def reduced_solve(last_link, through, inner, pivot, left, right):
    segments = len(through)
    inverses, ratios, offsets = [], [], []
    for s in range(segments):
        diagonal = pivot[s] + (inner[s + 1] if s + 1 < segments else last_link)
        given = right[s] + (left[s + 1] if s + 1 < segments else 0.0)
        if s > 0:
            diagonal = diagonal - through[s] * ratios[-1]
            given = given + ratios[-1] * carried
        carried = given
        inverse = 1.0 / diagonal
        inverses.append(inverse)
        offsets.append(given * inverse)
        if s + 1 < segments:
            ratios.append(through[s + 1] * inverse)
    out = []
    for s in range(segments - 1, -1, -1):
        if s + 1 < segments:
            value = offsets[s] + ratios[s] * value
            green = inverses[s] + ratios[s] * ratios[s] * green
            rising = ratios[s] * rising
        else:
            value, green, rising = offsets[s], inverses[s], jnp.ones_like(offsets[s])
        out.append((value, green, rising))
    return out[::-1]


def reduced_kernel(rows, got, sent):
    segments = got.shape[0]
    last_link = 2.0 * radial_weight * rows * rows
    main = reduced_solve(last_link, *[[got[s, p] for s in range(segments)] for p in range(5)])
    extra = reduced_solve(
        last_link, *[[got[s, 5, p : p + 1, :] for s in range(segments)] for p in range(5)]
    )
    zero = jnp.zeros((SUB, LANE), F32)
    for plane in range(3):
        sent[0, 2 * plane] = zero
    for s in range(segments):
        sent[s, 6] = zero
    for s in range(segments):
        value, green, rising = main[s]
        for plane, item in enumerate((value, rising, green / rising)):
            sent[s, 2 * plane + 1] = item
            if s + 1 < segments:
                sent[s + 1, 2 * plane] = item
        sent[s, 6, 1:2, :] = extra[s][0]
        if s + 1 < segments:
            sent[s + 1, 6, 0:1, :] = extra[s][0]


def third_kernel(
    before, left_map, right_map, outside, flux, goal, ratio, got, particular, own, new
):
    rows, azimuths, width = before.shape
    links, radii, inverse_links, quarter = tables(rows, width)
    per = width // LANE
    for group in range(azimuths // SUB):
        here = pl.ds(group * SUB, SUB)
        left = tiles_of(got, group, 0, width)
        right = tiles_of(got, group, 1, width)
        for i in range(rows):
            new[i, here, :] = (
                before[i, here, :] + left_map[i, here, :] * left + right_map[i, here, :] * right
            )

    def beyond(end):
        return pair_of(
            *[
                jnp.concatenate([got[e * per + t, 6, end : end + 1, :] for t in range(per)], axis=1)
                for e in range(2)
            ]
        )

    left, right = beyond(0), beyond(1)
    halo = [outside[0, i] + outside[1, i] * left + outside[2, i] * right for i in range(rows)]
    for group in range(azimuths // SUB):
        here = pl.ds(group * SUB, SUB)
        source = sources(
            group,
            new,
            lambda i: halo[i][0:1, :],
            lambda i: halo[i][1:2, :],
            flux,
            goal,
            radii,
            quarter,
        )
        inner, outer = local_solve(group, source, ratio, inverse_links, particular)
        inner = links[0] * inner
        own[0, here, :] = (
            tiles_of(got, group, 2, width) * inner + tiles_of(got, group, 3, width) * outer
        )
        own[1, here, :] = (
            tiles_of(got, group, 4, width) * inner + tiles_of(got, group, 5, width) * outer
        )


def gather_kernel(own, first, second, third, near, message):
    mine = lax.rem(lax.axis_index("rad"), GROUP)
    block = lax.div(lax.axis_index("rad"), GROUP)
    for group in range(own.shape[1] // SUB):
        here = pl.ds(group * SUB, SUB)
        upward, downward = own[0, here, :], own[1, here, :]
        lower, upper = jnp.zeros_like(upward), downward
        for flip, other in ((1, first), (2, second), (3, third)):
            up, down = other[0, here, :], other[1, here, :]
            upward = upward + up
            downward = downward + down
            below = (mine ^ flip) < mine
            lower = lower + jnp.where(below, up, 0.0)
            upper = upper + jnp.where(below, 0.0, down)
        near[0, here, :] = lower
        near[1, here, :] = upper
        for slot, flip in ((0, 1), (1, 2)):
            message[slot, here, :] = jnp.where((block ^ flip) > block, upward, downward)


def last_kernel(
    particular,
    left_map,
    right_map,
    factor,
    got,
    own,
    near,
    first,
    second,
    third,
    result,
    sensitivity,
    result_out,
    sensitivity_out,
    done,
):
    rows, azimuths, width = particular.shape
    block = lax.div(lax.axis_index("rad"), GROUP)
    copies = []
    for group in range(azimuths // SUB):
        here = pl.ds(group * SUB, SUB)
        lower, upper = near[0, here, :], near[1, here, :]
        for flip, other in ((1, first), (2, second), (3, third)):
            item = other[here, :]
            below = (block ^ flip) < block
            lower = lower + jnp.where(below, item, 0.0)
            upper = upper + jnp.where(below, 0.0, item)
        left = tiles_of(got, group, 4, width) * lower + tiles_of(got, group, 2, width) * upper
        right = (
            tiles_of(got, group, 5, width) * (lower + own[0, here, :])
            + tiles_of(got, group, 3, width) * (upper - own[1, here, :])
        )
        for i in range(rows):
            value = particular[i, here, :] + left_map[i, here, :] * left + right_map[i, here, :] * right
            result_out[i, here, :] = value
            sensitivity_out[i, here, :] = value * factor[i, here, :]
        for k, (source, target) in enumerate(((result_out, result), (sensitivity_out, sensitivity))):
            copy = pltpu.make_async_copy(
                source.at[:, here, :], target.at[:, here, :], done.at[group, k]
            )
            copy.start()
            copies.append(copy)
    for copy in copies:
        copy.wait()


def call(kernel, outs, *args, flops=1_000_000, remote=(), remote_outs=False, scratch=(), room=24):
    moved = sum(4 * a.size for a in args) + sum(4 * o.size for o in outs)
    near, away = pl.BlockSpec(memory_space=pltpu.VMEM), pl.BlockSpec(memory_space=pltpu.HBM)
    return pl.pallas_call(
        kernel,
        out_shape=outs,
        in_specs=[away if k in remote else near for k in range(len(args))],
        out_specs=tuple([away if remote_outs else near] * len(outs)),
        scratch_shapes=list(scratch),
        compiler_params=pltpu.CompilerParams(vmem_limit_bytes=room * 2**20),
        cost_estimate=pl.CostEstimate(flops=flops, bytes_accessed=moved, transcendentals=0),
    )(*args)


def swap_edges(low_edge, high_edge):
    count = lax.axis_size("azi")
    below = lax.ppermute(high_edge, "azi", [(i, (i + 1) % count) for i in range(count)])
    above = lax.ppermute(low_edge, "azi", [((i + 1) % count, i) for i in range(count)])
    return below, above


def flip_permute(value, flip):
    return lax.ppermute(value, "rad", [(i, i ^ flip) for i in range(lax.axis_size("rad"))])


def exchange(value):
    return lax.all_to_all(value, "rad", 0, 0, tiled=True)


def body(heat, deform, flux, goal, start):
    rows, azimuths, width = heat.shape
    segments = lax.axis_size("rad")
    groups = azimuths // SUB
    tiles = azimuths * width // (SUB * LANE)
    block = jax.ShapeDtypeStruct((rows, azimuths, width), F32)
    pair = jax.ShapeDtypeStruct((2, azimuths, width), F32)
    edge = jax.ShapeDtypeStruct((3, rows, width), F32)
    held = pltpu.VMEM((rows, azimuths, width), F32)

    def planes(count):
        return jax.ShapeDtypeStruct((tiles, count, SUB, LANE), F32)

    edges = call(
        edge_kernel,
        (edge, edge),
        heat,
        deform,
        flux,
        goal,
        start,
        remote=range(5),
        room=54,
scratch=(pltpu.VMEM((5, 2, rows, SUB, width), F32), pltpu.SemaphoreType.DMA((5, 2))),
    )
    below, above = swap_edges(*edges)
    ratio, left_map, right_map, factor, condensed = call(
        matrix_kernel,
        (block, block, block, block, planes(3)),
        heat,
        deform,
        flux,
        flops=20_000_000,
        remote=range(3),
        room=49,
        scratch=(held, held, held, pltpu.SemaphoreType.DMA((groups, 3))),
    )
    particular, message, outside = call(
        first_kernel,
        (block, planes(6), jax.ShapeDtypeStruct((3, rows, 2, width), F32)),
        start,
        below,
        above,
        flux,
        goal,
        ratio,
        condensed,
    )
    sent = call(
        lambda got, sent: reduced_kernel(rows, got, sent),
        (jax.ShapeDtypeStruct((segments, 7, SUB, LANE), F32),),
        exchange(message),
    )[0]
    got = exchange(sent)
    particular, own = call(
        third_kernel,
        (block, pair),
        particular,
        left_map,
        right_map,
        outside,
        flux,
        goal,
        ratio,
        got,
        scratch=(held,),
    )
    others = [flip_permute(own, flip) for flip in (1, 2, 3)]
    near, message = call(gather_kernel, (pair, pair), own, *others)
    far = [flip_permute(message[min(flip, 2) - 1], flip * GROUP) for flip in (1, 2, 3)]
    return call(
        last_kernel,
        (block, block),
        particular,
        left_map,
        right_map,
        factor,
        got,
        own,
        near,
        *far,
        remote_outs=True,
        scratch=(held, held, pltpu.SemaphoreType.DMA((groups, 2))),
    )


def solution(mesh):
    spec = P("rad", "azi", None)
    return jax.shard_map(
        body, mesh=mesh, in_specs=(spec,) * 5, out_specs=(spec, spec), check_vma=False
    )
```

time: 64.8 us -> 60.1 us (0.927)
  local copies, waits for them, and re-layouts: 5.65 us -> 0.03 us
  Pallas kernels: 4.58 us -> 8.58 us
  waiting for transfers between devices: 12.1 us -> 8.45 us
  blocking collectives: 29.1 us -> 32 us
  starting transfers between devices: 11.8 us -> 10.1 us
    unnamed x14 -> x6, local copies, waits for them, and re-layouts: 4.56 us -> 0.02 us
    pallas_call x7, Pallas kernels: 4.58 us -> 8.58 us  [call(): pl.pallas_call(kernel, out_shape=outs, in_specs=[away if k in remote else...]
    all_to_all x2, blocking collectives: 29.1 us -> 32 us  [exchange(): return lax.all_to_all(value, 'rad', 0, 0, tiled=True)]
    ppermute x2 -> x1, starting transfers between devices: 3.46 us -> 1.7 us  [swap_edges(): lax.ppermute(low_edge, 'azi', [((i + 1) % count, i) for i in range(count)])]
    ppermute x2 -> x1, waiting for transfers between devices: 1.6 us -> 0.26 us  [swap_edges(): lax.ppermute(high_edge, 'azi', [(i, (i + 1) % count) for i in range(count)])]
    ppermute x6, waiting for transfers between devices: 9.38 us -> 8.16 us  [flip_permute(): lax.ppermute(value, 'rad', [(i, i ^ flip) for i in range(lax.axis_size('r...]
    slice x1 -> x0, local copies, waits for them, and re-layouts: 1.08 us -> none  [body(): below, above = swap_edges(start[:, 0, :], start[:, azimuths - 1, :])]
    ppermute x2 -> x1, waiting for transfers between devices: 1.08 us -> 0.03 us  [swap_edges(): lax.ppermute(low_edge, 'azi', [((i + 1) % count, i) for i in range(count)])]
  transfers between devices with their start and end apart: 10 -> 8, of which waited for: 7 -> 6; matrix products, arithmetic and copies ran while one was open for 0% -> 0% of each run, Pallas kernels for 1% -> 4%
where the time goes in v3:
time: 60.1 us; the launch traced here: 59.9 us
  blocking collectives  32 us (53%)
  starting transfers between devices  10.1 us (17%)
  Pallas kernels  8.58 us (14%)
  waiting for transfers between devices  8.45 us (14%)
  between operations  0.72 us (1%)
    all_to_all x2, blocking collectives, exchange(): return lax.all_to_all(value, 'rad', 0, 0, tiled=True)  32 us
    pallas_call x7, Pallas kernels, call(): pl.pallas_call(kernel, out_shape=outs, in_specs=[away if k in remote else...  8.58 us
    ppermute x6, starting transfers between devices, flip_permute(): lax.ppermute(value, 'rad', [(i, i ^ flip) for i in range(lax.axis_size('r...  8.35 us
    ppermute x6, waiting for transfers between devices, flip_permute(): lax.ppermute(value, 'rad', [(i, i ^ flip) for i in range(lax.axis_size('r...  8.16 us
    ppermute x1, starting transfers between devices, swap_edges(): lax.ppermute(low_edge, 'azi', [((i + 1) % count, i) for i in range(count)])  1.7 us
  transfers between devices with their start and end apart: 8, of which 6 were waited for; matrix products, arithmetic and copies ran while one was open for 0% of the time, Pallas kernels for 4%

profile of v3, /device:TPU:64, one launch (start us, length us, event | category | flops | bytes accessed | tf_op | source)
XLA Modules:
  0.0 59.9 jit_solution(6193316810341175443)
XLA Ops:
  0.6 2.6 %shard_map.68 = (f32[3,16,512]{2,1,0:T(8,128)}, f32[3,16,512]{2,1,0:T(8,128)}) custom-call(f32[16,32,512]{2,1,0:T(8,128)} %heat.3, f32[16,32,512]{2,1,0:T(8,128)} %deform.3, f32[16,32,512]{2,1,0:T(8,128)} %flux.7, f32[16,32,512]{2,1,0:T(8,128)} %goal.5, f32[16,32,512]{2,1,0:T(8,128)} %old.3), custom_call_target="tpu_custom_call" | custom-call | flops 1000000 | bytes 5439488 | tf_op jit(solution)/shard_map/pallas_call | solution.py:445
  3.3 0.0 collective-permute-start
  3.3 0.0 copy-start
  3.3 0.0 copy-start.1
  3.3 0.0 copy-start.2
  3.3 1.7 %collective-permute-start.1 = (f32[3,16,512]{2,1,0:T(8,128)}, f32[3,16,512]{2,1,0:T(8,128)S(1)}, u32[]{:S(2)}, u32[]{:S(2)}) collective-permute-start(f32[3,16,512]{2,1,0:T(8,128)} %get-tuple-element.17), channel_id=1, source_target_pairs={{1,0},{2,1},{3,2},{4,3},{5,4},{6,5},{7,6},{8,7},{9,8},{10,9},{11,1... | collective-permute-start | bytes 294920 | tf_op jit(solution)/shard_map/ppermute | solution.py:459
  5.0 2.2 %shard_map.69 = (f32[16,32,512]{2,1,0:T(8,128)S(1)}, f32[16,32,512]{2,1,0:T(8,128)S(1)}, f32[16,32,512]{2,1,0:T(8,128)S(1)}, f32[16,32,512]{2,1,0:T(8,128)S(1)}, f32[16,3,8,128]{3,2,1,0:T(8,128)S(1)}) custom-call(f32[16,32,512]{2,1,0:T(8,128)} %heat.3, f32[16,32,512]{2,1,0:T(8,128)} %deform.3, f32[16,32,512]{2,1,0:T(8,128)} %flux.7), custom_call_target="tpu_custom_call" | custom-call | flops 20000000 | bytes 7536640 | tf_op jit(solution)/shard_map/pallas_call | solution.py:445
  7.3 0.3 collective-permute-done.below
  7.5 0.0 collective-permute-done.1.above
  7.6 0.0 copy-done
  7.6 0.0 copy-done.1
  7.6 0.0 copy-done.2
  7.6 1.1 %shard_map.70 = (f32[16,32,512]{2,1,0:T(8,128)S(1)}, f32[16,6,8,128]{3,2,1,0:T(8,128)S(1)}, f32[3,16,2,512]{3,2,1,0:T(2,128)S(1)}) custom-call(f32[16,32,512]{2,1,0:T(8,128)S(1)} %copy-done.2, f32[3,16,512]{2,1,0:T(8,128)S(1)} %collective-permute-done.below, f32[3,16,512]{2,1,0:T(8,128)S(1)} %collective-permute-done.1.above, f32[16,32,512]{2,1,0:T(8,128)S(1)} %copy-done, ...), custom_call_target="tpu_custom_call" | custom-call | flops 1000000 | bytes 6225920 | tf_op jit(solution)/shard_map/pallas_call | solution.py:445
  8.6 17.6 %all_to_all.10.got = f32[16,6,8,128]{3,2,1,0:T(8,128)S(1)} all-to-all(f32[16,6,8,128]{3,2,1,0:T(8,128)S(1)} %get-tuple-element.24), channel_id=1, replica_groups=mesh['rad'=16,'azi'=16] {'rad'}, dimensions={0} | all-to-all | bytes 786432 | tf_op jit(solution)/shard_map/all_to_all | solution.py:468
  26.2 0.2 shard_map.71
  26.4 14.4 %all_to_all.11.got = f32[16,7,8,128]{3,2,1,0:T(8,128)S(1)} all-to-all(f32[16,7,8,128]{3,2,1,0:T(8,128)S(1)} %shard_map.71), channel_id=1, replica_groups=mesh['rad'=16,'azi'=16] {'rad'}, dimensions={0} | all-to-all | bytes 917504 | tf_op jit(solution)/shard_map/all_to_all | solution.py:468
  40.8 1.0 %shard_map.72 = (f32[16,32,512]{2,1,0:T(8,128)S(1)}, f32[2,32,512]{2,1,0:T(8,128)S(1)}) custom-call(f32[16,32,512]{2,1,0:T(8,128)S(1)} %get-tuple-element.20.before, f32[16,32,512]{2,1,0:T(8,128)S(1)} %get-tuple-element.21.left_map, f32[16,32,512]{2,1,0:T(8,128)S(1)} %get-tuple-element.22.right_map, f32[3,16,2,512]{3,2,1,0:T(2,128)S(1)} %get-tuple-element.23.outside, ...), custom_call_target="tpu_custom_call" | custom-call | flops 1000000 | bytes 8126464 | tf_op jit(solution)/shard_map/pallas_call | solution.py:445
  41.8 0.6 %collective-permute-start.4 = (f32[2,32,512]{2,1,0:T(8,128)S(1)}, f32[2,32,512]{2,1,0:T(8,128)S(1)}, u32[]{:S(2)}, u32[]{:S(2)}) collective-permute-start(f32[2,32,512]{2,1,0:T(8,128)S(1)} %get-tuple-element.27.own), channel_id=1, source_target_pairs={{0,48},{16,32},{32,16},{48,0},{64,112},{80,96},{96,80},{112,64},{1... | collective-permute-start | bytes 393224 | tf_op jit(solution)/shard_map/ppermute | solution.py:464
  42.5 2.1 %collective-permute-start.3 = (f32[2,32,512]{2,1,0:T(8,128)S(1)}, f32[2,32,512]{2,1,0:T(8,128)S(1)}, u32[]{:S(2)}, u32[]{:S(2)}) collective-permute-start(f32[2,32,512]{2,1,0:T(8,128)S(1)} %get-tuple-element.27.own), channel_id=1, source_target_pairs={{0,32},{16,48},{32,0},{48,16},{64,96},{80,112},{96,64},{112,80},{1... | collective-permute-start | bytes 393224 | tf_op jit(solution)/shard_map/ppermute | solution.py:464
  44.5 1.5 %collective-permute-start.2 = (f32[2,32,512]{2,1,0:T(8,128)S(1)}, f32[2,32,512]{2,1,0:T(8,128)S(1)}, u32[]{:S(2)}, u32[]{:S(2)}) collective-permute-start(f32[2,32,512]{2,1,0:T(8,128)S(1)} %get-tuple-element.27.own), channel_id=1, source_target_pairs={{0,16},{16,0},{32,48},{48,32},{64,80},{80,64},{96,112},{112,96},{1... | collective-permute-start | bytes 393224 | tf_op jit(solution)/shard_map/ppermute | solution.py:464
  46.0 4.1 %collective-permute-done.4.third = f32[2,32,512]{2,1,0:T(8,128)S(1)} collective-permute-done((f32[2,32,512]{2,1,0:T(8,128)S(1)}, f32[2,32,512]{2,1,0:T(8,128)S(1)}, u32[]{:S(2)}, u32[]{:S(2)}) %collective-permute-start.4) | collective-permute-done | bytes 131104 | tf_op jit(solution)/shard_map/ppermute | solution.py:464
  50.1 0.0 collective-permute-done.3.second
  50.1 0.6 %collective-permute-done.2.first = f32[2,32,512]{2,1,0:T(8,128)S(1)} collective-permute-done((f32[2,32,512]{2,1,0:T(8,128)S(1)}, f32[2,32,512]{2,1,0:T(8,128)S(1)}, u32[]{:S(2)}, u32[]{:S(2)}) %collective-permute-start.2) | collective-permute-done | bytes 131104 | tf_op jit(solution)/shard_map/ppermute | solution.py:464
  50.7 0.1 shard_map.73
  50.8 0.1 collective-permute-start.5
  50.9 1.7 %collective-permute-start.7 = (f32[32,512]{1,0:T(8,128)S(1)}, f32[32,512]{1,0:T(8,128)S(1)}, u32[]{:S(2)}, u32[]{:S(2)}) collective-permute-start(f32[32,512]{1,0:T(8,128)S(1)} %get-tuple-element.30), channel_id=1, source_target_pairs={{0,192},{16,208},{32,224},{48,240},{64,128},{80,144},{96,160},{112... | collective-permute-start | bytes 196616 | tf_op jit(solution)/shard_map/ppermute | solution.py:464
  52.6 2.3 %collective-permute-start.6 = (f32[32,512]{1,0:T(8,128)S(1)}, f32[32,512]{1,0:T(8,128)S(1)}, u32[]{:S(2)}, u32[]{:S(2)}) collective-permute-start(f32[32,512]{1,0:T(8,128)S(1)} %get-tuple-element.30), channel_id=1, source_target_pairs={{0,128},{16,144},{32,160},{48,176},{64,192},{80,208},{96,224},{112... | collective-permute-start | bytes 196616 | tf_op jit(solution)/shard_map/ppermute | solution.py:464
  55.0 0.2 collective-permute-done.5.first
  55.2 1.3 %collective-permute-done.7.third = f32[32,512]{1,0:T(8,128)S(1)} collective-permute-done((f32[32,512]{1,0:T(8,128)S(1)}, f32[32,512]{1,0:T(8,128)S(1)}, u32[]{:S(2)}, u32[]{:S(2)}) %collective-permute-start.7) | collective-permute-done | bytes 65568 | tf_op jit(solution)/shard_map/ppermute | solution.py:464
  56.5 2.0 %collective-permute-done.6.second = f32[32,512]{1,0:T(8,128)S(1)} collective-permute-done((f32[32,512]{1,0:T(8,128)S(1)}, f32[32,512]{1,0:T(8,128)S(1)}, u32[]{:S(2)}, u32[]{:S(2)}) %collective-permute-start.6) | collective-permute-done | bytes 65568 | tf_op jit(solution)/shard_map/ppermute | solution.py:464
  58.4 1.4 %shard_map.74 = (f32[16,32,512]{2,1,0:T(8,128)}, f32[16,32,512]{2,1,0:T(8,128)}) custom-call(f32[16,32,512]{2,1,0:T(8,128)S(1)} %get-tuple-element.25.particular, f32[16,32,512]{2,1,0:T(8,128)S(1)} %get-tuple-element.21.left_map, f32[16,32,512]{2,1,0:T(8,128)S(1)} %get-tuple-element.22.right_map, f32[16,32,512]{2,1,0:T(8,128)S(1)} %get-tuple-element.26.factor, ...), custom_call_target="tpu_custom_call" | custom-call | flops 1000000 | bytes 7208960 | tf_op jit(solution)/shard_map/pallas_call | solution.py:445
  (1 shorter events, 0.0 us)
Async XLA Ops:
  3.3 4.3 %collective-permute-start = (f32[3,16,512]{2,1,0:T(8,128)}, f32[3,16,512]{2,1,0:T(8,128)S(1)}, u32[]{:S(2)}, u32[]{:S(2)}) collective-permute-start(f32[3,16,512]{2,1,0:T(8,128)} %get-tuple-element.16), channel_id=1, source_target_pairs={{0,1},{1,2},{2,3},{3,4},{4,5},{5,6},{6,7},{7,8},{8,9},{9,10},{10,1... | collective-permute-start | bytes 294920 | tf_op jit(solution)/shard_map/ppermute | solution.py:458
  3.3 4.3 %copy-start = (f32[16,32,512]{2,1,0:T(8,128)S(1)}, f32[16,32,512]{2,1,0:T(8,128)}, u32[]{:S(2)}) copy-start(f32[16,32,512]{2,1,0:T(8,128)} %flux.7) | copy-start | bytes 3145732
  3.3 4.3 %copy-start.1 = (f32[16,32,512]{2,1,0:T(8,128)S(1)}, f32[16,32,512]{2,1,0:T(8,128)}, u32[]{:S(2)}) copy-start(f32[16,32,512]{2,1,0:T(8,128)} %goal.5) | copy-start | bytes 3145732
  3.3 4.3 %copy-start.2 = (f32[16,32,512]{2,1,0:T(8,128)S(1)}, f32[16,32,512]{2,1,0:T(8,128)}, u32[]{:S(2)}) copy-start(f32[16,32,512]{2,1,0:T(8,128)} %old.3) | copy-start | bytes 3145732
  3.3 4.2 %collective-permute-start.1 = (f32[3,16,512]{2,1,0:T(8,128)}, f32[3,16,512]{2,1,0:T(8,128)S(1)}, u32[]{:S(2)}, u32[]{:S(2)}) collective-permute-start(f32[3,16,512]{2,1,0:T(8,128)} %get-tuple-element.17), channel_id=1, source_target_pairs={{1,0},{2,1},{3,2},{4,3},{5,4},{6,5},{7,6},{8,7},{9,8},{10,9},{11,1... | collective-permute-start | bytes 294920 | tf_op jit(solution)/shard_map/ppermute | solution.py:459
  41.8 8.3 %collective-permute-start.4 = (f32[2,32,512]{2,1,0:T(8,128)S(1)}, f32[2,32,512]{2,1,0:T(8,128)S(1)}, u32[]{:S(2)}, u32[]{:S(2)}) collective-permute-start(f32[2,32,512]{2,1,0:T(8,128)S(1)} %get-tuple-element.27.own), channel_id=1, source_target_pairs={{0,48},{16,32},{32,16},{48,0},{64,112},{80,96},{96,80},{112,64},{1... | collective-permute-start | bytes 393224 | tf_op jit(solution)/shard_map/ppermute | solution.py:464
  42.5 7.6 %collective-permute-start.3 = (f32[2,32,512]{2,1,0:T(8,128)S(1)}, f32[2,32,512]{2,1,0:T(8,128)S(1)}, u32[]{:S(2)}, u32[]{:S(2)}) collective-permute-start(f32[2,32,512]{2,1,0:T(8,128)S(1)} %get-tuple-element.27.own), channel_id=1, source_target_pairs={{0,32},{16,48},{32,0},{48,16},{64,96},{80,112},{96,64},{112,80},{1... | collective-permute-start | bytes 393224 | tf_op jit(solution)/shard_map/ppermute | solution.py:464
  44.5 6.2 %collective-permute-start.2 = (f32[2,32,512]{2,1,0:T(8,128)S(1)}, f32[2,32,512]{2,1,0:T(8,128)S(1)}, u32[]{:S(2)}, u32[]{:S(2)}) collective-permute-start(f32[2,32,512]{2,1,0:T(8,128)S(1)} %get-tuple-element.27.own), channel_id=1, source_target_pairs={{0,16},{16,0},{32,48},{48,32},{64,80},{80,64},{96,112},{112,96},{1... | collective-permute-start | bytes 393224 | tf_op jit(solution)/shard_map/ppermute | solution.py:464
  50.8 4.4 %collective-permute-start.5 = (f32[32,512]{1,0:T(8,128)S(1)}, f32[32,512]{1,0:T(8,128)S(1)}, u32[]{:S(2)}, u32[]{:S(2)}) collective-permute-start(f32[32,512]{1,0:T(8,128)S(1)} %get-tuple-element.31), channel_id=1, source_target_pairs={{0,64},{16,80},{32,96},{48,112},{64,0},{80,16},{96,32},{112,48},{1... | collective-permute-start | bytes 196616 | tf_op jit(solution)/shard_map/ppermute | solution.py:464
  50.9 5.6 %collective-permute-start.7 = (f32[32,512]{1,0:T(8,128)S(1)}, f32[32,512]{1,0:T(8,128)S(1)}, u32[]{:S(2)}, u32[]{:S(2)}) collective-permute-start(f32[32,512]{1,0:T(8,128)S(1)} %get-tuple-element.30), channel_id=1, source_target_pairs={{0,192},{16,208},{32,224},{48,240},{64,128},{80,144},{96,160},{112... | collective-permute-start | bytes 196616 | tf_op jit(solution)/shard_map/ppermute | solution.py:464
  52.6 5.8 %collective-permute-start.6 = (f32[32,512]{1,0:T(8,128)S(1)}, f32[32,512]{1,0:T(8,128)S(1)}, u32[]{:S(2)}, u32[]{:S(2)}) collective-permute-start(f32[32,512]{1,0:T(8,128)S(1)} %get-tuple-element.30), channel_id=1, source_target_pairs={{0,128},{16,144},{32,160},{48,176},{64,192},{80,208},{96,224},{112... | collective-permute-start | bytes 196616 | tf_op jit(solution)/shard_map/ppermute | solution.py:464

commit v4 on v3

--- a/solution.py
+++ b/solution.py
@@ -16,6 +16,7 @@
 
 SUB, LANE = 8, 128
 GROUP = 4
+PIECE = 16
 F32 = jnp.float32
 
 
@@ -98,33 +99,37 @@
 
 
 def matrix_kernel(
-    heat, deform, flux, ratio, left_map, right_map, factor, condensed, hot_in, size_in, flux_in, ready
+    heat,
+    deform,
+    flux,
+    goal,
+    ratio,
+    left_map,
+    right_map,
+    factor,
+    ahead,
+    given,
+    condensed,
 ):
     rows, azimuths, width = heat.shape
-    groups = azimuths // SUB
-    copies = []
-    for group in range(groups):
-        here = pl.ds(group * SUB, SUB)
-        for k, (source, target) in enumerate(((heat, hot_in), (deform, size_in), (flux, flux_in))):
-            copy = pltpu.make_async_copy(
-                source.at[:, here, :], target.at[:, here, :], ready.at[group, k]
-            )
-            copy.start()
-            copies.append(copy)
     links, radii = geometry(rows)
     inverse_links = [wide(1.0 / splat(link), width) for link in links]
     bases = [wide(base, width) for base in base_shunts(radii)]
-    for group in range(groups):
+    for group in range(azimuths // SUB):
         here = pl.ds(group * SUB, SUB)
-        for copy in copies[3 * group : 3 * group + 3]:
-            copy.wait()
         shunts = []
         for i in range(rows):
-            hot = hot_in[i, here, :]
-            drag, shunt = shunt_of(hot, size_in[i, here, :], flux_in[i, here, :], radii[i], bases[i])
+            hot = heat[i, here, :]
+            moving = flux[i, here, :]
+            drag, shunt = shunt_of(hot, deform[i, here, :], moving, radii[i], bases[i])
             shunts.append(shunt)
             lane = lax.broadcasted_iota(jnp.int32, hot.shape, 1)
-            rise = jnp.where(lane == width - 1, 0.0, pltpu.roll(hot, width - 1, 1) - hot)
+            last = lane == width - 1
+            rise = jnp.where(last, 0.0, pltpu.roll(hot, width - 1, 1) - hot)
+            ahead[i, here, :] = jnp.where(
+                last, 0.0, radii[i] * axial_weight + (radii[i] * flow_weight) * moving
+            )
+            given[i, here, :] = radii[i] * goal[i, here, :]
             factor[i, here, :] = slope_weight * rise - (2.0 * heat_weight) * drag
         ratios, lefts, rights, ports = ladder(shunts, links, inverse_links)
         for i in range(rows):
@@ -137,11 +142,13 @@
 
 def edge_kernel(heat, deform, flux, goal, old, low_edge, high_edge, held, ready):
     rows, azimuths, width = heat.shape
-    spans = (pl.ds(0, SUB), pl.ds(azimuths - SUB, SUB))
+    ends = ((0, 1, low_edge), (azimuths - 1, azimuths - 2, high_edge))
     copies = []
-    for k, source in enumerate((heat, deform, flux, goal, old)):
-        for e in range(2):
-            copy = pltpu.make_async_copy(source.at[:, spans[e], :], held.at[k, e], ready.at[k, e])
+    for e, (at, inner, _) in enumerate(ends):
+        for k, (source, line) in enumerate(
+            ((heat, at), (deform, at), (flux, at), (goal, at), (old, at), (old, inner))
+        ):
+            copy = pltpu.make_async_copy(source.at[:, line, :], held.at[e, k], ready.at[e, k])
             copy.start()
             copies.append(copy)
     total = rows * lax.axis_size("rad")
@@ -150,18 +157,13 @@
     radius = 1.0 + (first + (row + 0.5)) * (1.0 / total)
     base = 2.0 * azimuth_weight / (radius * radius) + (mass_weight + 2.0 * axial_weight)
     quarter = azimuth_weight / radius
-    for copy in copies:
-        copy.wait()
-
-    def line(k, e, at):
-        return jnp.concatenate([held[k, e, i, at : at + 1, :] for i in range(rows)], axis=0)
-
-    for e, (at, inner, out) in enumerate(((0, 1, low_edge), (SUB - 1, SUB - 2, high_edge))):
-        moving = line(2, e, at)
-        centre = line(4, e, at)
-        _, shunt = shunt_of(line(0, e, at), line(1, e, at), moving, radius, base)
+    for e, (_, _, out) in enumerate(ends):
+        for copy in copies[6 * e : 6 * e + 6]:
+            copy.wait()
+        hot, size, moving, given, centre, beside = [held[e, k] for k in range(6)]
+        _, shunt = shunt_of(hot, size, moving, radius, base)
         out[0] = shunt
-        out[1] = radius * explicit(centre, moving, line(3, e, at)) + quarter * line(4, e, inner)
+        out[1] = radius * explicit(centre, moving, given) + quarter * beside
         out[2] = centre
 
 
@@ -175,24 +177,32 @@
     )
 
 
-def sources(group, old, below, above, flux, goal, radii, quarter):
-    rows, azimuths, width = old.shape
+def place(padded, group, i, value):
+    for t in range(value.shape[1] // LANE):
+        padded[i, t, pl.ds((group + 1) * SUB, SUB), :] = value[:, t * LANE : (t + 1) * LANE]
+
+
+def place_row(padded, at, i, value):
+    for t in range(value.shape[1] // LANE):
+        padded[i, t, at : at + 1, :] = value[:, t * LANE : (t + 1) * LANE]
+
+
+def sources(group, padded, ahead, given, behind, radii, quarter):
+    rows, tiles = padded.shape[:2]
     here = pl.ds(group * SUB, SUB)
-    sub = lax.broadcasted_iota(jnp.int32, (SUB, width), 0)
+
+    def lines(i, shift):
+        at = pl.ds((group + 1) * SUB + shift, SUB)
+        return jnp.concatenate([padded[i, t, at, :] for t in range(tiles)], axis=1)
+
     out = []
     for i in range(rows):
-        centre = old[i, here, :]
-        low = below(i) if group == 0 else old[i, group * SUB - 1 : group * SUB, :]
-        high = (
-            above(i)
-            if group == azimuths // SUB - 1
-            else old[i, (group + 1) * SUB : (group + 1) * SUB + 1, :]
-        )
-        side = jnp.where(sub == 0, low, pltpu.roll(centre, 1, 0)) + jnp.where(
-            sub == SUB - 1, high, pltpu.roll(centre, SUB - 1, 0)
-        )
-        right = explicit(centre, flux[i, here, :], goal[i, here, :])
-        out.append(radii[i] * right + quarter[i] * side)
+        centre = lines(i, 0)
+        width = centre.shape[1]
+        value = given[i, here, :] + ahead[i, here, :] * pltpu.roll(centre, width - 1, 1)
+        value = value + behind[i] * pltpu.roll(centre, 1, 1)
+        value = value + (radii[i] * mass_weight) * centre
+        out.append(value + quarter[i] * (lines(i, -1) + lines(i, 1)))
     return out
 
 
@@ -223,56 +233,65 @@
     links, radii = geometry(rows)
     inverse_links = [wide(1.0 / splat(link), width) for link in links]
     quarter = [wide(azimuth_weight / splat(radius), width) for radius in radii]
-    return links, radii, inverse_links, quarter
+    first = lax.broadcasted_iota(jnp.int32, (1, width), 1) == 0
+    behind = [jnp.where(first, 0.0, radius * axial_weight) for radius in radii]
+    return links, radii, inverse_links, quarter, behind
+
+
+def first_kernel(old, ahead, given, ratio, particular, ports, padded):
+    rows, azimuths, width = old.shape
+    links, radii, inverse_links, quarter, behind = tables(rows, width)
+    for i in range(rows):
+        place_row(padded, SUB - 1, i, jnp.zeros((1, width), F32))
+        place_row(padded, SUB + azimuths, i, jnp.zeros((1, width), F32))
+        for group in range(azimuths // SUB):
+            place(padded, group, i, old[i, pl.ds(group * SUB, SUB), :])
+    for group in range(azimuths // SUB):
+        source = sources(group, padded, ahead, given, behind, radii, quarter)
+        inner, outer = local_solve(group, source, ratio, inverse_links, particular)
+        put_tiles(ports, group, 0, links[0] * inner)
+        put_tiles(ports, group, 1, outer)
 
 
 def pair_of(below, above):
     return jnp.concatenate([below, above], axis=0)
 
 
-def first_kernel(
-    old, below, above, flux, goal, ratio, condensed, particular, message, outside
-):
+def edge_rows(ref, i):
+    last = ref.shape[1] - 1
+    return pair_of(ref[i, 0:1, :], ref[i, last : last + 1, :])
+
+
+def join_kernel(old, below, above, ratio, condensed, ports, message, outside):
     rows, azimuths, width = old.shape
-    links, radii, inverse_links, quarter = tables(rows, width)
+    links, radii, inverse_links, quarter, _ = tables(rows, width)
     tiles = message.shape[0]
     per = width // LANE
     message[:, 0:3] = condensed[...]
+    message[:, 3:5] = ports[...]
     message[:, 5] = jnp.ones((tiles, SUB, LANE), F32)
 
-    shunts, source = [], []
+    shunts, source, added = [], [], []
     for i in range(rows):
         row = pl.ds(i, 1)
         shunts.append(pair_of(below[0, row, :], above[0, row, :]))
-        beside = pair_of(old[i, 0:1, :], old[i, azimuths - 1 : azimuths, :])
-        source.append(pair_of(below[1, row, :], above[1, row, :]) + quarter[i] * beside)
-    ratios, lefts, rights, ports = ladder(shunts, links, inverse_links)
+        source.append(pair_of(below[1, row, :], above[1, row, :]) + quarter[i] * edge_rows(old, i))
+        added.append(quarter[i] * pair_of(below[2, row, :], above[2, row, :]))
+    ratios, lefts, rights, extra = ladder(shunts, links, inverse_links)
     values, outer = substitute(source, ratios, inverse_links)
-    for i in range(rows):
-        outside[0, i] = values[i]
-        outside[1, i] = lefts[i]
-        outside[2, i] = rights[i]
-    for plane, port in enumerate((*ports, links[0] * values[0], outer)):
-        for e in range(2):
-            for t in range(per):
-                message[e * per + t, 5, plane : plane + 1, :] = port[
-                    e : e + 1, t * LANE : (t + 1) * LANE
-                ]
-
-    for group in range(azimuths // SUB):
-        source = sources(
-            group,
-            old,
-            lambda i: below[2, i : i + 1, :],
-            lambda i: above[2, i : i + 1, :],
-            flux,
-            goal,
-            radii,
-            quarter,
-        )
-        inner, outer = local_solve(group, source, ratio, inverse_links, particular)
-        put_tiles(message, group, 3, links[0] * inner)
-        put_tiles(message, group, 4, outer)
+    changes, change = substitute(added, [edge_rows(ratio, i) for i in range(rows - 1)], inverse_links)
+    for i in range(rows):
+        for slot, item in enumerate((values, lefts, rights, changes)):
+            outside[slot, i] = item[i]
+    for e, (at, row) in enumerate(((0, 0), (tiles - per, SUB - 1))):
+        for t in range(per):
+            lanes = slice(t * LANE, (t + 1) * LANE)
+            for plane, port in enumerate((*extra, links[0] * values[0], outer)):
+                message[e * per + t, 5, plane : plane + 1, :] = port[e : e + 1, lanes]
+            for plane, port in ((3, links[0] * changes[0]), (4, change)):
+                message[at + t, plane, row : row + 1, :] = (
+                    ports[at + t, plane - 3, row : row + 1, :] + port[e : e + 1, lanes]
+                )
 
 
 def reduced_solve(last_link, through, inner, pivot, left, right):
@@ -326,19 +345,13 @@
 
 
 def third_kernel(
-    before, left_map, right_map, outside, flux, goal, ratio, got, particular, own, new
+    before, left_map, right_map, outside, ahead, given, ratio, got, particular, own, padded
 ):
     rows, azimuths, width = before.shape
-    links, radii, inverse_links, quarter = tables(rows, width)
+    links, radii, inverse_links, quarter, behind = tables(rows, width)
     per = width // LANE
-    for group in range(azimuths // SUB):
-        here = pl.ds(group * SUB, SUB)
-        left = tiles_of(got, group, 0, width)
-        right = tiles_of(got, group, 1, width)
-        for i in range(rows):
-            new[i, here, :] = (
-                before[i, here, :] + left_map[i, here, :] * left + right_map[i, here, :] * right
-            )
+    groups = azimuths // SUB
+    sub = lax.broadcasted_iota(jnp.int32, (SUB, width), 0)
 
     def beyond(end):
         return pair_of(
@@ -349,19 +362,24 @@
         )
 
     left, right = beyond(0), beyond(1)
-    halo = [outside[0, i] + outside[1, i] * left + outside[2, i] * right for i in range(rows)]
-    for group in range(azimuths // SUB):
+    for i in range(rows):
+        halo = outside[0, i] + outside[1, i] * left + outside[2, i] * right
+        place_row(padded, SUB - 1, i, halo[0:1, :])
+        place_row(padded, SUB + azimuths, i, halo[1:2, :])
+    for group in range(groups):
         here = pl.ds(group * SUB, SUB)
-        source = sources(
-            group,
-            new,
-            lambda i: halo[i][0:1, :],
-            lambda i: halo[i][1:2, :],
-            flux,
-            goal,
-            radii,
-            quarter,
-        )
+        left = tiles_of(got, group, 0, width)
+        right = tiles_of(got, group, 1, width)
+        for i in range(rows):
+            value = before[i, here, :] + left_map[i, here, :] * left + right_map[i, here, :] * right
+            if group == 0:
+                value = value + jnp.where(sub == 0, outside[3, i, 0:1, :], 0.0)
+            if group == groups - 1:
+                value = value + jnp.where(sub == SUB - 1, outside[3, i, 1:2, :], 0.0)
+            place(padded, group, i, value)
+    for group in range(groups):
+        here = pl.ds(group * SUB, SUB)
+        source = sources(group, padded, ahead, given, behind, radii, quarter)
         inner, outer = local_solve(group, source, ratio, inverse_links, particular)
         inner = links[0] * inner
         own[0, here, :] = (
@@ -429,12 +447,17 @@
             value = particular[i, here, :] + left_map[i, here, :] * left + right_map[i, here, :] * right
             result_out[i, here, :] = value
             sensitivity_out[i, here, :] = value * factor[i, here, :]
-        for k, (source, target) in enumerate(((result_out, result), (sensitivity_out, sensitivity))):
-            copy = pltpu.make_async_copy(
-                source.at[:, here, :], target.at[:, here, :], done.at[group, k]
-            )
-            copy.start()
-            copies.append(copy)
+            if (i + 1) % PIECE:
+                continue
+            part = pl.ds(i + 1 - PIECE, PIECE)
+            for k, (source, target) in enumerate(
+                ((result_out, result), (sensitivity_out, sensitivity))
+            ):
+                copy = pltpu.make_async_copy(
+                    source.at[part, here, :], target.at[part, here, :], done.at[group, i // PIECE, k]
+                )
+                copy.start()
+                copies.append(copy)
     for copy in copies:
         copy.wait()
 
@@ -477,6 +500,7 @@
     pair = jax.ShapeDtypeStruct((2, azimuths, width), F32)
     edge = jax.ShapeDtypeStruct((3, rows, width), F32)
     held = pltpu.VMEM((rows, azimuths, width), F32)
+    padded = pltpu.VMEM((rows, width // LANE, azimuths + 2 * SUB, LANE), F32)
 
     def planes(count):
         return jax.ShapeDtypeStruct((tiles, count, SUB, LANE), F32)
@@ -491,30 +515,30 @@
         start,
         remote=range(5),
         room=54,
-scratch=(pltpu.VMEM((5, 2, rows, SUB, width), F32), pltpu.SemaphoreType.DMA((5, 2))),
+        scratch=(pltpu.VMEM((2, 6, rows, width), F32), pltpu.SemaphoreType.DMA((2, 6))),
     )
     below, above = swap_edges(*edges)
-    ratio, left_map, right_map, factor, condensed = call(
+    ratio, left_map, right_map, factor, ahead, given, condensed = call(
         matrix_kernel,
-        (block, block, block, block, planes(3)),
+        (block, block, block, block, block, block, planes(3)),
         heat,
         deform,
         flux,
+        goal,
         flops=20_000_000,
-        remote=range(3),
-        room=49,
-        scratch=(held, held, held, pltpu.SemaphoreType.DMA((groups, 3))),
-    )
-    particular, message, outside = call(
-        first_kernel,
-        (block, planes(6), jax.ShapeDtypeStruct((3, rows, 2, width), F32)),
+    )
+    particular, ports = call(
+        first_kernel, (block, planes(2)), start, ahead, given, ratio, scratch=(padded,)
+    )
+    message, outside = call(
+        join_kernel,
+        (planes(6), jax.ShapeDtypeStruct((4, rows, 2, width), F32)),
         start,
         below,
         above,
-        flux,
-        goal,
         ratio,
         condensed,
+        ports,
     )
     sent = call(
         lambda got, sent: reduced_kernel(rows, got, sent),
@@ -529,11 +553,11 @@
         left_map,
         right_map,
         outside,
-        flux,
-        goal,
+        ahead,
+        given,
         ratio,
         got,
-        scratch=(held,),
+        scratch=(padded,),
     )
     others = [flip_permute(own, flip) for flip in (1, 2, 3)]
     near, message = call(gather_kernel, (pair, pair), own, *others)
@@ -550,7 +574,7 @@
         near,
         *far,
         remote_outs=True,
-        scratch=(held, held, pltpu.SemaphoreType.DMA((groups, 2))),
+        scratch=(held, held, pltpu.SemaphoreType.DMA((groups, rows // PIECE, 2))),
     )
 
 

time: 60.1 us -> 58.7 us (0.977)
  Pallas kernels: 8.58 us -> 6.74 us
    pallas_call x7 -> x8, Pallas kernels: 8.58 us -> 6.74 us  [call(): pl.pallas_call(kernel, out_shape=outs, in_specs=[away if k in remote else...]
  transfers between devices with their start and end apart: 8 -> 8, of which waited for: 6 -> 6; matrix products, arithmetic and copies ran while one was open for 0% -> 0% of each run, Pallas kernels for 4% -> 3%
where the time goes in v4:
time: 58.7 us; the launch traced here: 58.5 us
  blocking collectives  32 us (55%)
  starting transfers between devices  10.1 us (17%)
  waiting for transfers between devices  8.86 us (15%)
  Pallas kernels  6.74 us (11%)
  between operations  0.75 us (1%)
    all_to_all x2, blocking collectives, exchange(): return lax.all_to_all(value, 'rad', 0, 0, tiled=True)  32 us
    ppermute x6, starting transfers between devices, flip_permute(): lax.ppermute(value, 'rad', [(i, i ^ flip) for i in range(lax.axis_size('r...  8.35 us
    ppermute x6, waiting for transfers between devices, flip_permute(): lax.ppermute(value, 'rad', [(i, i ^ flip) for i in range(lax.axis_size('r...  8.15 us
    pallas_call x8, Pallas kernels, call(): pl.pallas_call(kernel, out_shape=outs, in_specs=[away if k in remote else...  6.74 us
    ppermute x1, starting transfers between devices, swap_edges(): lax.ppermute(low_edge, 'azi', [((i + 1) % count, i) for i in range(count)])  1.72 us
  transfers between devices with their start and end apart: 8, of which 6 were waited for; matrix products, arithmetic and copies ran while one was open for 0% of the time, Pallas kernels for 3%

profile of v4, /device:TPU:64, one launch (start us, length us, event | category | flops | bytes accessed | tf_op | source)
XLA Modules:
  0.0 58.5 jit_solution(13197387655679530219)
XLA Ops:
  0.6 0.0 copy-start.4
  0.6 0.0 copy-start.3
  0.7 0.0 copy-start.2
  0.7 0.0 copy-start.1
  0.7 2.0 %shard_map.70 = (f32[3,16,512]{2,1,0:T(8,128)}, f32[3,16,512]{2,1,0:T(8,128)}) custom-call(f32[16,32,512]{2,1,0:T(8,128)} %heat.3, f32[16,32,512]{2,1,0:T(8,128)} %deform.3, f32[16,32,512]{2,1,0:T(8,128)} %flux.3, f32[16,32,512]{2,1,0:T(8,128)} %goal.3, f32[16,32,512]{2,1,0:T(8,128)} %old.5), custom_call_target="tpu_custom_call" | custom-call | flops 1000000 | bytes 5439488 | tf_op jit(solution)/shard_map/pallas_call | solution.py:468
  2.7 0.0 collective-permute-start
  2.7 0.0 copy-start
  2.7 1.7 %collective-permute-start.1 = (f32[3,16,512]{2,1,0:T(8,128)}, f32[3,16,512]{2,1,0:T(8,128)S(1)}, u32[]{:S(2)}, u32[]{:S(2)}) collective-permute-start(f32[3,16,512]{2,1,0:T(8,128)} %get-tuple-element.26), channel_id=1, source_target_pairs={{1,0},{2,1},{3,2},{4,3},{5,4},{6,5},{7,6},{8,7},{9,8},{10,9},{11,1... | collective-permute-start | bytes 294920 | tf_op jit(solution)/shard_map/ppermute | solution.py:482
  4.4 0.0 copy-done.4
  4.4 0.0 copy-done.3
  4.4 0.0 copy-done.2
  4.4 0.0 copy-done.1
  4.4 1.1 %shard_map.68 = (f32[16,32,512]{2,1,0:T(8,128)S(1)}, f32[16,32,512]{2,1,0:T(8,128)S(1)}, f32[16,32,512]{2,1,0:T(8,128)S(1)}, f32[16,32,512]{2,1,0:T(8,128)S(1)},...) custom-call(f32[16,32,512]{2,1,0:T(8,128)S(1)} %copy-done.1, ...), custom_call_target="tpu_custom_call" | custom-call | flops 20000000 | bytes 10682368 | tf_op jit(solution)/shard_map/pallas_call | solution.py:468
  5.5 0.0 copy-done
  5.5 0.7 %shard_map.69 = (f32[16,32,512]{2,1,0:T(8,128)S(1)}, f32[16,2,8,128]{3,2,1,0:T(8,128)S(1)}) custom-call(f32[16,32,512]{2,1,0:T(8,128)S(1)} %copy-done, f32[16,32,512]{2,1,0:T(8,128)S(1)} %get-tuple-element.19.ahead, f32[16,32,512]{2,1,0:T(8,128)S(1)} %get-tuple-element.20.given, f32[16,32,512]{2,1,0:T(8,128)S(1)} %get-tuple-element.21.ratio), custom_call_target="tpu_custom_call" | custom-call | flops 1000000 | bytes 5373952 | tf_op jit(solution)/shard_map/pallas_call | solution.py:468
  6.2 0.7 %collective-permute-done.below = f32[3,16,512]{2,1,0:T(8,128)S(1)} collective-permute-done((f32[3,16,512]{2,1,0:T(8,128)}, f32[3,16,512]{2,1,0:T(8,128)S(1)}, u32[]{:S(2)}, u32[]{:S(2)}) %collective-permute-start) | collective-permute-done | bytes 98336 | tf_op jit(solution)/shard_map/ppermute | solution.py:481
  6.9 0.0 collective-permute-done.1.above
  6.9 0.4 shard_map.71
  7.3 17.6 %all_to_all.10.got = f32[16,6,8,128]{3,2,1,0:T(8,128)S(1)} all-to-all(f32[16,6,8,128]{3,2,1,0:T(8,128)S(1)} %get-tuple-element.30), channel_id=1, replica_groups=mesh['rad'=16,'azi'=16] {'rad'}, dimensions={0} | all-to-all | bytes 786432 | tf_op jit(solution)/shard_map/all_to_all | solution.py:491
  24.9 0.2 shard_map.72
  25.1 14.4 %all_to_all.11.got = f32[16,7,8,128]{3,2,1,0:T(8,128)S(1)} all-to-all(f32[16,7,8,128]{3,2,1,0:T(8,128)S(1)} %shard_map.72), channel_id=1, replica_groups=mesh['rad'=16,'azi'=16] {'rad'}, dimensions={0} | all-to-all | bytes 917504 | tf_op jit(solution)/shard_map/all_to_all | solution.py:491
  39.5 0.9 %shard_map.73 = (f32[16,32,512]{2,1,0:T(8,128)S(1)}, f32[2,32,512]{2,1,0:T(8,128)S(1)}) custom-call(f32[16,32,512]{2,1,0:T(8,128)S(1)} %get-tuple-element.22.before, f32[16,32,512]{2,1,0:T(8,128)S(1)} %get-tuple-element.23.left_map, f32[16,32,512]{2,1,0:T(8,128)S(1)} %get-tuple-element.24.right_map, f32[4,16,2,512]{3,2,1,0:T(2,128)S(1)} %get-tuple-element.29.outside, ...), custom_call_target="tpu_custom_call" | custom-call | flops 1000000 | bytes 8192000 | tf_op jit(solution)/shard_map/pallas_call | solution.py:468
  40.5 0.6 %collective-permute-start.4 = (f32[2,32,512]{2,1,0:T(8,128)S(1)}, f32[2,32,512]{2,1,0:T(8,128)S(1)}, u32[]{:S(2)}, u32[]{:S(2)}) collective-permute-start(f32[2,32,512]{2,1,0:T(8,128)S(1)} %get-tuple-element.33.own), channel_id=1, source_target_pairs={{0,48},{16,32},{32,16},{48,0},{64,112},{80,96},{96,80},{112,64},{1... | collective-permute-start | bytes 393224 | tf_op jit(solution)/shard_map/ppermute | solution.py:487
  41.1 2.1 %collective-permute-start.3 = (f32[2,32,512]{2,1,0:T(8,128)S(1)}, f32[2,32,512]{2,1,0:T(8,128)S(1)}, u32[]{:S(2)}, u32[]{:S(2)}) collective-permute-start(f32[2,32,512]{2,1,0:T(8,128)S(1)} %get-tuple-element.33.own), channel_id=1, source_target_pairs={{0,32},{16,48},{32,0},{48,16},{64,96},{80,112},{96,64},{112,80},{1... | collective-permute-start | bytes 393224 | tf_op jit(solution)/shard_map/ppermute | solution.py:487
  43.2 1.5 %collective-permute-start.2 = (f32[2,32,512]{2,1,0:T(8,128)S(1)}, f32[2,32,512]{2,1,0:T(8,128)S(1)}, u32[]{:S(2)}, u32[]{:S(2)}) collective-permute-start(f32[2,32,512]{2,1,0:T(8,128)S(1)} %get-tuple-element.33.own), channel_id=1, source_target_pairs={{0,16},{16,0},{32,48},{48,32},{64,80},{80,64},{96,112},{112,96},{1... | collective-permute-start | bytes 393224 | tf_op jit(solution)/shard_map/ppermute | solution.py:487
  44.6 4.1 %collective-permute-done.4.third = f32[2,32,512]{2,1,0:T(8,128)S(1)} collective-permute-done((f32[2,32,512]{2,1,0:T(8,128)S(1)}, f32[2,32,512]{2,1,0:T(8,128)S(1)}, u32[]{:S(2)}, u32[]{:S(2)}) %collective-permute-start.4) | collective-permute-done | bytes 131104 | tf_op jit(solution)/shard_map/ppermute | solution.py:487
  48.8 0.0 collective-permute-done.3.second
  48.8 0.6 %collective-permute-done.2.first = f32[2,32,512]{2,1,0:T(8,128)S(1)} collective-permute-done((f32[2,32,512]{2,1,0:T(8,128)S(1)}, f32[2,32,512]{2,1,0:T(8,128)S(1)}, u32[]{:S(2)}, u32[]{:S(2)}) %collective-permute-start.2) | collective-permute-done | bytes 131104 | tf_op jit(solution)/shard_map/ppermute | solution.py:487
  49.4 0.1 shard_map.74
  49.5 0.1 collective-permute-start.5
  49.6 1.7 %collective-permute-start.7 = (f32[32,512]{1,0:T(8,128)S(1)}, f32[32,512]{1,0:T(8,128)S(1)}, u32[]{:S(2)}, u32[]{:S(2)}) collective-permute-start(f32[32,512]{1,0:T(8,128)S(1)} %get-tuple-element.36), channel_id=1, source_target_pairs={{0,192},{16,208},{32,224},{48,240},{64,128},{80,144},{96,160},{112... | collective-permute-start | bytes 196616 | tf_op jit(solution)/shard_map/ppermute | solution.py:487
  51.3 2.4 %collective-permute-start.6 = (f32[32,512]{1,0:T(8,128)S(1)}, f32[32,512]{1,0:T(8,128)S(1)}, u32[]{:S(2)}, u32[]{:S(2)}) collective-permute-start(f32[32,512]{1,0:T(8,128)S(1)} %get-tuple-element.36), channel_id=1, source_target_pairs={{0,128},{16,144},{32,160},{48,176},{64,192},{80,208},{96,224},{112... | collective-permute-start | bytes 196616 | tf_op jit(solution)/shard_map/ppermute | solution.py:487
  53.6 0.2 collective-permute-done.5.first
  53.8 1.3 %collective-permute-done.7.third = f32[32,512]{1,0:T(8,128)S(1)} collective-permute-done((f32[32,512]{1,0:T(8,128)S(1)}, f32[32,512]{1,0:T(8,128)S(1)}, u32[]{:S(2)}, u32[]{:S(2)}) %collective-permute-start.7) | collective-permute-done | bytes 65568 | tf_op jit(solution)/shard_map/ppermute | solution.py:487
  55.1 1.9 %collective-permute-done.6.second = f32[32,512]{1,0:T(8,128)S(1)} collective-permute-done((f32[32,512]{1,0:T(8,128)S(1)}, f32[32,512]{1,0:T(8,128)S(1)}, u32[]{:S(2)}, u32[]{:S(2)}) %collective-permute-start.6) | collective-permute-done | bytes 65568 | tf_op jit(solution)/shard_map/ppermute | solution.py:487
  57.0 1.4 %shard_map.75 = (f32[16,32,512]{2,1,0:T(8,128)}, f32[16,32,512]{2,1,0:T(8,128)}) custom-call(f32[16,32,512]{2,1,0:T(8,128)S(1)} %get-tuple-element.31.particular, f32[16,32,512]{2,1,0:T(8,128)S(1)} %get-tuple-element.23.left_map, f32[16,32,512]{2,1,0:T(8,128)S(1)} %get-tuple-element.24.right_map, f32[16,32,512]{2,1,0:T(8,128)S(1)} %get-tuple-element.32.factor, ...), custom_call_target="tpu_custom_call" | custom-call | flops 1000000 | bytes 7208960 | tf_op jit(solution)/shard_map/pallas_call | solution.py:468
  (1 shorter events, 0.0 us)
Async XLA Ops:
  0.6 3.8 %copy-start.4 = (f32[16,32,512]{2,1,0:T(8,128)S(1)}, f32[16,32,512]{2,1,0:T(8,128)}, u32[]{:S(2)}) copy-start(f32[16,32,512]{2,1,0:T(8,128)} %goal.3) | copy-start | bytes 3145732
  0.6 3.8 %copy-start.3 = (f32[16,32,512]{2,1,0:T(8,128)S(1)}, f32[16,32,512]{2,1,0:T(8,128)}, u32[]{:S(2)}) copy-start(f32[16,32,512]{2,1,0:T(8,128)} %flux.3) | copy-start | bytes 3145732
  0.7 3.8 %copy-start.2 = (f32[16,32,512]{2,1,0:T(8,128)S(1)}, f32[16,32,512]{2,1,0:T(8,128)}, u32[]{:S(2)}) copy-start(f32[16,32,512]{2,1,0:T(8,128)} %deform.3) | copy-start | bytes 3145732
  0.7 3.8 %copy-start.1 = (f32[16,32,512]{2,1,0:T(8,128)S(1)}, f32[16,32,512]{2,1,0:T(8,128)}, u32[]{:S(2)}) copy-start(f32[16,32,512]{2,1,0:T(8,128)} %heat.3) | copy-start | bytes 3145732
  2.7 4.3 %collective-permute-start = (f32[3,16,512]{2,1,0:T(8,128)}, f32[3,16,512]{2,1,0:T(8,128)S(1)}, u32[]{:S(2)}, u32[]{:S(2)}) collective-permute-start(f32[3,16,512]{2,1,0:T(8,128)} %get-tuple-element.25), channel_id=1, source_target_pairs={{0,1},{1,2},{2,3},{3,4},{4,5},{5,6},{6,7},{7,8},{8,9},{9,10},{10,1... | collective-permute-start | bytes 294920 | tf_op jit(solution)/shard_map/ppermute | solution.py:481
  2.7 2.8 %copy-start = (f32[16,32,512]{2,1,0:T(8,128)S(1)}, f32[16,32,512]{2,1,0:T(8,128)}, u32[]{:S(2)}) copy-start(f32[16,32,512]{2,1,0:T(8,128)} %old.5) | copy-start | bytes 3145732
  2.7 4.3 %collective-permute-start.1 = (f32[3,16,512]{2,1,0:T(8,128)}, f32[3,16,512]{2,1,0:T(8,128)S(1)}, u32[]{:S(2)}, u32[]{:S(2)}) collective-permute-start(f32[3,16,512]{2,1,0:T(8,128)} %get-tuple-element.26), channel_id=1, source_target_pairs={{1,0},{2,1},{3,2},{4,3},{5,4},{6,5},{7,6},{8,7},{9,8},{10,9},{11,1... | collective-permute-start | bytes 294920 | tf_op jit(solution)/shard_map/ppermute | solution.py:482
  40.5 8.3 %collective-permute-start.4 = (f32[2,32,512]{2,1,0:T(8,128)S(1)}, f32[2,32,512]{2,1,0:T(8,128)S(1)}, u32[]{:S(2)}, u32[]{:S(2)}) collective-permute-start(f32[2,32,512]{2,1,0:T(8,128)S(1)} %get-tuple-element.33.own), channel_id=1, source_target_pairs={{0,48},{16,32},{32,16},{48,0},{64,112},{80,96},{96,80},{112,64},{1... | collective-permute-start | bytes 393224 | tf_op jit(solution)/shard_map/ppermute | solution.py:487
  41.1 7.7 %collective-permute-start.3 = (f32[2,32,512]{2,1,0:T(8,128)S(1)}, f32[2,32,512]{2,1,0:T(8,128)S(1)}, u32[]{:S(2)}, u32[]{:S(2)}) collective-permute-start(f32[2,32,512]{2,1,0:T(8,128)S(1)} %get-tuple-element.33.own), channel_id=1, source_target_pairs={{0,32},{16,48},{32,0},{48,16},{64,96},{80,112},{96,64},{112,80},{1... | collective-permute-start | bytes 393224 | tf_op jit(solution)/shard_map/ppermute | solution.py:487
  43.2 6.2 %collective-permute-start.2 = (f32[2,32,512]{2,1,0:T(8,128)S(1)}, f32[2,32,512]{2,1,0:T(8,128)S(1)}, u32[]{:S(2)}, u32[]{:S(2)}) collective-permute-start(f32[2,32,512]{2,1,0:T(8,128)S(1)} %get-tuple-element.33.own), channel_id=1, source_target_pairs={{0,16},{16,0},{32,48},{48,32},{64,80},{80,64},{96,112},{112,96},{1... | collective-permute-start | bytes 393224 | tf_op jit(solution)/shard_map/ppermute | solution.py:487
  49.5 4.4 %collective-permute-start.5 = (f32[32,512]{1,0:T(8,128)S(1)}, f32[32,512]{1,0:T(8,128)S(1)}, u32[]{:S(2)}, u32[]{:S(2)}) collective-permute-start(f32[32,512]{1,0:T(8,128)S(1)} %get-tuple-element.37), channel_id=1, source_target_pairs={{0,64},{16,80},{32,96},{48,112},{64,0},{80,16},{96,32},{112,48},{1... | collective-permute-start | bytes 196616 | tf_op jit(solution)/shard_map/ppermute | solution.py:487
  49.6 5.6 %collective-permute-start.7 = (f32[32,512]{1,0:T(8,128)S(1)}, f32[32,512]{1,0:T(8,128)S(1)}, u32[]{:S(2)}, u32[]{:S(2)}) collective-permute-start(f32[32,512]{1,0:T(8,128)S(1)} %get-tuple-element.36), channel_id=1, source_target_pairs={{0,192},{16,208},{32,224},{48,240},{64,128},{80,144},{96,160},{112... | collective-permute-start | bytes 196616 | tf_op jit(solution)/shard_map/ppermute | solution.py:487
  51.3 5.8 %collective-permute-start.6 = (f32[32,512]{1,0:T(8,128)S(1)}, f32[32,512]{1,0:T(8,128)S(1)}, u32[]{:S(2)}, u32[]{:S(2)}) collective-permute-start(f32[32,512]{1,0:T(8,128)S(1)} %get-tuple-element.36), channel_id=1, source_target_pairs={{0,128},{16,144},{32,160},{48,176},{64,192},{80,208},{96,224},{112... | collective-permute-start | bytes 196616 | tf_op jit(solution)/shard_map/ppermute | solution.py:487

commit v5 on v4

--- a/solution.py
+++ b/solution.py
@@ -329,23 +329,36 @@
         last_link, *[[got[s, 5, p : p + 1, :] for s in range(segments)] for p in range(5)]
     )
     zero = jnp.zeros((SUB, LANE), F32)
-    for plane in range(3):
-        sent[0, 2 * plane] = zero
+    for plane in (0, 2):
+        sent[0, plane] = zero
     for s in range(segments):
-        sent[s, 6] = zero
+        sent[s, 5] = zero
     for s in range(segments):
         value, green, rising = main[s]
-        for plane, item in enumerate((value, rising, green / rising)):
-            sent[s, 2 * plane + 1] = item
-            if s + 1 < segments:
-                sent[s + 1, 2 * plane] = item
-        sent[s, 6, 1:2, :] = extra[s][0]
+        sent[s, 1] = value
+        sent[s, 3] = rising
+        sent[s, 4] = green / rising
+        sent[s, 5, 1:2, :] = extra[s][0]
         if s + 1 < segments:
-            sent[s + 1, 6, 0:1, :] = extra[s][0]
+            sent[s + 1, 0] = value
+            sent[s + 1, 2] = rising
+            sent[s + 1, 5, 0:1, :] = extra[s][0]
 
 
 def third_kernel(
-    before, left_map, right_map, outside, ahead, given, ratio, got, particular, own, padded
+    before,
+    left_map,
+    right_map,
+    outside,
+    ahead,
+    given,
+    ratio,
+    condensed,
+    got,
+    particular,
+    own,
+    fall,
+    padded,
 ):
     rows, azimuths, width = before.shape
     links, radii, inverse_links, quarter, behind = tables(rows, width)
@@ -356,7 +369,7 @@
     def beyond(end):
         return pair_of(
             *[
-                jnp.concatenate([got[e * per + t, 6, end : end + 1, :] for t in range(per)], axis=1)
+                jnp.concatenate([got[e * per + t, 5, end : end + 1, :] for t in range(per)], axis=1)
                 for e in range(2)
             ]
         )
@@ -382,12 +395,13 @@
         source = sources(group, padded, ahead, given, behind, radii, quarter)
         inner, outer = local_solve(group, source, ratio, inverse_links, particular)
         inner = links[0] * inner
-        own[0, here, :] = (
-            tiles_of(got, group, 2, width) * inner + tiles_of(got, group, 3, width) * outer
-        )
-        own[1, here, :] = (
-            tiles_of(got, group, 4, width) * inner + tiles_of(got, group, 5, width) * outer
-        )
+        rise_left, rise_right, fall_right = [tiles_of(got, group, plane, width) for plane in (2, 3, 4)]
+        through = tiles_of(condensed, group, 0, width)
+        fall_left = (1.0 / through + rise_left * fall_right) / rise_right
+        fall_left = jnp.where(lax.axis_index("rad") == 0, 0.0, fall_left)
+        fall[here, :] = fall_left
+        own[0, here, :] = rise_left * inner + rise_right * outer
+        own[1, here, :] = fall_left * inner + fall_right * outer
 
 
 def gather_kernel(own, first, second, third, near, message):
@@ -417,6 +431,7 @@
     factor,
     got,
     own,
+    fall,
     near,
     first,
     second,
@@ -438,9 +453,9 @@
             below = (block ^ flip) < block
             lower = lower + jnp.where(below, item, 0.0)
             upper = upper + jnp.where(below, 0.0, item)
-        left = tiles_of(got, group, 4, width) * lower + tiles_of(got, group, 2, width) * upper
+        left = fall[here, :] * lower + tiles_of(got, group, 2, width) * upper
         right = (
-            tiles_of(got, group, 5, width) * (lower + own[0, here, :])
+            tiles_of(got, group, 4, width) * (lower + own[0, here, :])
             + tiles_of(got, group, 3, width) * (upper - own[1, here, :])
         )
         for i in range(rows):
@@ -542,13 +557,13 @@
     )
     sent = call(
         lambda got, sent: reduced_kernel(rows, got, sent),
-        (jax.ShapeDtypeStruct((segments, 7, SUB, LANE), F32),),
+        (jax.ShapeDtypeStruct((segments, 6, SUB, LANE), F32),),
         exchange(message),
     )[0]
     got = exchange(sent)
-    particular, own = call(
+    particular, own, fall = call(
         third_kernel,
-        (block, pair),
+        (block, pair, jax.ShapeDtypeStruct((azimuths, width), F32)),
         particular,
         left_map,
         right_map,
@@ -556,6 +571,7 @@
         ahead,
         given,
         ratio,
+        condensed,
         got,
         scratch=(padded,),
     )
@@ -571,6 +587,7 @@
         factor,
         got,
         own,
+        fall,
         near,
         *far,
         remote_outs=True,

time: 58.7 us -> 57.8 us (0.985)
  blocking collectives: 32 us -> 31.3 us
    all_to_all x2, blocking collectives: 32 us -> 31.3 us  [exchange(): return lax.all_to_all(value, 'rad', 0, 0, tiled=True)]
where the time goes in v5:
time: 57.8 us; the launch traced here: 57.6 us
  blocking collectives  31.3 us (54%)
  starting transfers between devices  10.1 us (17%)
  waiting for transfers between devices  8.69 us (15%)
  Pallas kernels  6.75 us (12%)
  between operations  0.75 us (1%)
    all_to_all x2, blocking collectives, exchange(): return lax.all_to_all(value, 'rad', 0, 0, tiled=True)  31.3 us
    ppermute x6, starting transfers between devices, flip_permute(): lax.ppermute(value, 'rad', [(i, i ^ flip) for i in range(lax.axis_size('r...  8.35 us
    ppermute x6, waiting for transfers between devices, flip_permute(): lax.ppermute(value, 'rad', [(i, i ^ flip) for i in range(lax.axis_size('r...  7.98 us
    pallas_call x8, Pallas kernels, call(): pl.pallas_call(kernel, out_shape=outs, in_specs=[away if k in remote else...  6.75 us
    ppermute x1, starting transfers between devices, swap_edges(): lax.ppermute(low_edge, 'azi', [((i + 1) % count, i) for i in range(count)])  1.72 us
  transfers between devices with their start and end apart: 8, of which 6 were waited for; matrix products, arithmetic and copies ran while one was open for 0% of the time, Pallas kernels for 3%

profile of v5, /device:TPU:64, one launch (start us, length us, event | category | flops | bytes accessed | tf_op | source)
XLA Modules:
  0.0 57.6 jit_solution(2016558783898618836)
XLA Ops:
  0.6 0.0 copy-start.4
  0.6 0.0 copy-start.3
  0.7 0.0 copy-start.2
  0.7 0.0 copy-start.1
  0.7 2.0 %shard_map.70 = (f32[3,16,512]{2,1,0:T(8,128)}, f32[3,16,512]{2,1,0:T(8,128)}) custom-call(f32[16,32,512]{2,1,0:T(8,128)} %heat.3, f32[16,32,512]{2,1,0:T(8,128)} %deform.3, f32[16,32,512]{2,1,0:T(8,128)} %flux.3, f32[16,32,512]{2,1,0:T(8,128)} %goal.3, f32[16,32,512]{2,1,0:T(8,128)} %old.5), custom_call_target="tpu_custom_call" | custom-call | flops 1000000 | bytes 5439488 | tf_op jit(solution)/shard_map/pallas_call | solution.py:483
  2.7 0.0 collective-permute-start
  2.7 0.0 copy-start
  2.7 1.7 %collective-permute-start.1 = (f32[3,16,512]{2,1,0:T(8,128)}, f32[3,16,512]{2,1,0:T(8,128)S(1)}, u32[]{:S(2)}, u32[]{:S(2)}) collective-permute-start(f32[3,16,512]{2,1,0:T(8,128)} %get-tuple-element.27), channel_id=1, source_target_pairs={{1,0},{2,1},{3,2},{4,3},{5,4},{6,5},{7,6},{8,7},{9,8},{10,9},{11,1... | collective-permute-start | bytes 294920 | tf_op jit(solution)/shard_map/ppermute | solution.py:497
  4.4 0.0 copy-done.4
  4.4 0.0 copy-done.3
  4.4 0.0 copy-done.2
  4.4 0.0 copy-done.1
  4.4 1.1 %shard_map.68 = (f32[16,32,512]{2,1,0:T(8,128)S(1)}, f32[16,32,512]{2,1,0:T(8,128)S(1)}, f32[16,32,512]{2,1,0:T(8,128)S(1)}, f32[16,32,512]{2,1,0:T(8,128)S(1)},...) custom-call(f32[16,32,512]{2,1,0:T(8,128)S(1)} %copy-done.1, ...), custom_call_target="tpu_custom_call" | custom-call | flops 20000000 | bytes 10682368 | tf_op jit(solution)/shard_map/pallas_call | solution.py:483
  5.5 0.0 copy-done
  5.5 0.7 %shard_map.69 = (f32[16,32,512]{2,1,0:T(8,128)S(1)}, f32[16,2,8,128]{3,2,1,0:T(8,128)S(1)}) custom-call(f32[16,32,512]{2,1,0:T(8,128)S(1)} %copy-done, f32[16,32,512]{2,1,0:T(8,128)S(1)} %get-tuple-element.20.ahead, f32[16,32,512]{2,1,0:T(8,128)S(1)} %get-tuple-element.21.given, f32[16,32,512]{2,1,0:T(8,128)S(1)} %get-tuple-element.22.ratio), custom_call_target="tpu_custom_call" | custom-call | flops 1000000 | bytes 5373952 | tf_op jit(solution)/shard_map/pallas_call | solution.py:483
  6.2 0.7 %collective-permute-done.below = f32[3,16,512]{2,1,0:T(8,128)S(1)} collective-permute-done((f32[3,16,512]{2,1,0:T(8,128)}, f32[3,16,512]{2,1,0:T(8,128)S(1)}, u32[]{:S(2)}, u32[]{:S(2)}) %collective-permute-start) | collective-permute-done | bytes 98336 | tf_op jit(solution)/shard_map/ppermute | solution.py:496
  6.9 0.0 collective-permute-done.1.above
  6.9 0.4 shard_map.71
  7.3 17.6 %all_to_all.10.got = f32[16,6,8,128]{3,2,1,0:T(8,128)S(1)} all-to-all(f32[16,6,8,128]{3,2,1,0:T(8,128)S(1)} %get-tuple-element.31), channel_id=1, replica_groups=mesh['rad'=16,'azi'=16] {'rad'}, dimensions={0} | all-to-all | bytes 786432 | tf_op jit(solution)/shard_map/all_to_all | solution.py:506
  24.9 0.2 shard_map.72
  25.1 13.7 %all_to_all.11.got = f32[16,6,8,128]{3,2,1,0:T(8,128)S(1)} all-to-all(f32[16,6,8,128]{3,2,1,0:T(8,128)S(1)} %shard_map.72), channel_id=1, replica_groups=mesh['rad'=16,'azi'=16] {'rad'}, dimensions={0} | all-to-all | bytes 786432 | tf_op jit(solution)/shard_map/all_to_all | solution.py:506
  38.8 0.9 %shard_map.73 = (f32[16,32,512]{2,1,0:T(8,128)S(1)}, f32[2,32,512]{2,1,0:T(8,128)S(1)}, f32[32,512]{1,0:T(8,128)S(1)}) custom-call(f32[16,32,512]{2,1,0:T(8,128)S(1)} %get-tuple-element.23.before, f32[16,32,512]{2,1,0:T(8,128)S(1)} %get-tuple-element.24.left_map, f32[16,32,512]{2,1,0:T(8,128)S(1)} %get-tuple-element.25.right_map, ...), custom_call_target="tpu_custom_call" | custom-call | flops 1000000 | bytes 8388608 | tf_op jit(solution)/shard_map/pallas_call | solution.py:483
  39.8 0.6 %collective-permute-start.4 = (f32[2,32,512]{2,1,0:T(8,128)S(1)}, f32[2,32,512]{2,1,0:T(8,128)S(1)}, u32[]{:S(2)}, u32[]{:S(2)}) collective-permute-start(f32[2,32,512]{2,1,0:T(8,128)S(1)} %get-tuple-element.34.own), channel_id=1, source_target_pairs={{0,48},{16,32},{32,16},{48,0},{64,112},{80,96},{96,80},{112,64},{1... | collective-permute-start | bytes 393224 | tf_op jit(solution)/shard_map/ppermute | solution.py:502
  40.4 2.1 %collective-permute-start.3 = (f32[2,32,512]{2,1,0:T(8,128)S(1)}, f32[2,32,512]{2,1,0:T(8,128)S(1)}, u32[]{:S(2)}, u32[]{:S(2)}) collective-permute-start(f32[2,32,512]{2,1,0:T(8,128)S(1)} %get-tuple-element.34.own), channel_id=1, source_target_pairs={{0,32},{16,48},{32,0},{48,16},{64,96},{80,112},{96,64},{112,80},{1... | collective-permute-start | bytes 393224 | tf_op jit(solution)/shard_map/ppermute | solution.py:502
  42.5 1.5 %collective-permute-start.2 = (f32[2,32,512]{2,1,0:T(8,128)S(1)}, f32[2,32,512]{2,1,0:T(8,128)S(1)}, u32[]{:S(2)}, u32[]{:S(2)}) collective-permute-start(f32[2,32,512]{2,1,0:T(8,128)S(1)} %get-tuple-element.34.own), channel_id=1, source_target_pairs={{0,16},{16,0},{32,48},{48,32},{64,80},{80,64},{96,112},{112,96},{1... | collective-permute-start | bytes 393224 | tf_op jit(solution)/shard_map/ppermute | solution.py:502
  43.9 4.3 %collective-permute-done.4.third = f32[2,32,512]{2,1,0:T(8,128)S(1)} collective-permute-done((f32[2,32,512]{2,1,0:T(8,128)S(1)}, f32[2,32,512]{2,1,0:T(8,128)S(1)}, u32[]{:S(2)}, u32[]{:S(2)}) %collective-permute-start.4) | collective-permute-done | bytes 131104 | tf_op jit(solution)/shard_map/ppermute | solution.py:502
  48.3 0.0 collective-permute-done.3.second
  48.3 0.6 %collective-permute-done.2.first = f32[2,32,512]{2,1,0:T(8,128)S(1)} collective-permute-done((f32[2,32,512]{2,1,0:T(8,128)S(1)}, f32[2,32,512]{2,1,0:T(8,128)S(1)}, u32[]{:S(2)}, u32[]{:S(2)}) %collective-permute-start.2) | collective-permute-done | bytes 131104 | tf_op jit(solution)/shard_map/ppermute | solution.py:502
  48.9 0.1 shard_map.74
  49.0 0.1 collective-permute-start.5
  49.1 1.3 %collective-permute-start.7 = (f32[32,512]{1,0:T(8,128)S(1)}, f32[32,512]{1,0:T(8,128)S(1)}, u32[]{:S(2)}, u32[]{:S(2)}) collective-permute-start(f32[32,512]{1,0:T(8,128)S(1)} %get-tuple-element.38), channel_id=1, source_target_pairs={{0,192},{16,208},{32,224},{48,240},{64,128},{80,144},{96,160},{112... | collective-permute-start | bytes 196616 | tf_op jit(solution)/shard_map/ppermute | solution.py:502
  50.4 2.8 %collective-permute-start.6 = (f32[32,512]{1,0:T(8,128)S(1)}, f32[32,512]{1,0:T(8,128)S(1)}, u32[]{:S(2)}, u32[]{:S(2)}) collective-permute-start(f32[32,512]{1,0:T(8,128)S(1)} %get-tuple-element.38), channel_id=1, source_target_pairs={{0,128},{16,144},{32,160},{48,176},{64,192},{80,208},{96,224},{112... | collective-permute-start | bytes 196616 | tf_op jit(solution)/shard_map/ppermute | solution.py:502
  53.2 0.7 %collective-permute-done.5.first = f32[32,512]{1,0:T(8,128)S(1)} collective-permute-done((f32[32,512]{1,0:T(8,128)S(1)}, f32[32,512]{1,0:T(8,128)S(1)}, u32[]{:S(2)}, u32[]{:S(2)}) %collective-permute-start.5) | collective-permute-done | bytes 65568 | tf_op jit(solution)/shard_map/ppermute | solution.py:502
  53.8 0.8 %collective-permute-done.7.third = f32[32,512]{1,0:T(8,128)S(1)} collective-permute-done((f32[32,512]{1,0:T(8,128)S(1)}, f32[32,512]{1,0:T(8,128)S(1)}, u32[]{:S(2)}, u32[]{:S(2)}) %collective-permute-start.7) | collective-permute-done | bytes 65568 | tf_op jit(solution)/shard_map/ppermute | solution.py:502
  54.6 1.5 %collective-permute-done.6.second = f32[32,512]{1,0:T(8,128)S(1)} collective-permute-done((f32[32,512]{1,0:T(8,128)S(1)}, f32[32,512]{1,0:T(8,128)S(1)}, u32[]{:S(2)}, u32[]{:S(2)}) %collective-permute-start.6) | collective-permute-done | bytes 65568 | tf_op jit(solution)/shard_map/ppermute | solution.py:502
  56.2 1.4 %shard_map.75 = (f32[16,32,512]{2,1,0:T(8,128)}, f32[16,32,512]{2,1,0:T(8,128)}) custom-call(f32[16,32,512]{2,1,0:T(8,128)S(1)} %get-tuple-element.32.particular, f32[16,32,512]{2,1,0:T(8,128)S(1)} %get-tuple-element.24.left_map, f32[16,32,512]{2,1,0:T(8,128)S(1)} %get-tuple-element.25.right_map, f32[16,32,512]{2,1,0:T(8,128)S(1)} %get-tuple-element.33.factor, ...), custom_call_target="tpu_custom_call" | custom-call | flops 1000000 | bytes 7208960 | tf_op jit(solution)/shard_map/pallas_call | solution.py:483
  (1 shorter events, 0.0 us)
Async XLA Ops:
  0.6 3.8 %copy-start.4 = (f32[16,32,512]{2,1,0:T(8,128)S(1)}, f32[16,32,512]{2,1,0:T(8,128)}, u32[]{:S(2)}) copy-start(f32[16,32,512]{2,1,0:T(8,128)} %goal.3) | copy-start | bytes 3145732
  0.6 3.8 %copy-start.3 = (f32[16,32,512]{2,1,0:T(8,128)S(1)}, f32[16,32,512]{2,1,0:T(8,128)}, u32[]{:S(2)}) copy-start(f32[16,32,512]{2,1,0:T(8,128)} %flux.3) | copy-start | bytes 3145732
  0.7 3.8 %copy-start.2 = (f32[16,32,512]{2,1,0:T(8,128)S(1)}, f32[16,32,512]{2,1,0:T(8,128)}, u32[]{:S(2)}) copy-start(f32[16,32,512]{2,1,0:T(8,128)} %deform.3) | copy-start | bytes 3145732
  0.7 3.8 %copy-start.1 = (f32[16,32,512]{2,1,0:T(8,128)S(1)}, f32[16,32,512]{2,1,0:T(8,128)}, u32[]{:S(2)}) copy-start(f32[16,32,512]{2,1,0:T(8,128)} %heat.3) | copy-start | bytes 3145732
  2.7 4.3 %collective-permute-start = (f32[3,16,512]{2,1,0:T(8,128)}, f32[3,16,512]{2,1,0:T(8,128)S(1)}, u32[]{:S(2)}, u32[]{:S(2)}) collective-permute-start(f32[3,16,512]{2,1,0:T(8,128)} %get-tuple-element.26), channel_id=1, source_target_pairs={{0,1},{1,2},{2,3},{3,4},{4,5},{5,6},{6,7},{7,8},{8,9},{9,10},{10,1... | collective-permute-start | bytes 294920 | tf_op jit(solution)/shard_map/ppermute | solution.py:496
  2.7 2.8 %copy-start = (f32[16,32,512]{2,1,0:T(8,128)S(1)}, f32[16,32,512]{2,1,0:T(8,128)}, u32[]{:S(2)}) copy-start(f32[16,32,512]{2,1,0:T(8,128)} %old.5) | copy-start | bytes 3145732
  2.7 4.3 %collective-permute-start.1 = (f32[3,16,512]{2,1,0:T(8,128)}, f32[3,16,512]{2,1,0:T(8,128)S(1)}, u32[]{:S(2)}, u32[]{:S(2)}) collective-permute-start(f32[3,16,512]{2,1,0:T(8,128)} %get-tuple-element.27), channel_id=1, source_target_pairs={{1,0},{2,1},{3,2},{4,3},{5,4},{6,5},{7,6},{8,7},{9,8},{10,9},{11,1... | collective-permute-start | bytes 294920 | tf_op jit(solution)/shard_map/ppermute | solution.py:497
  39.8 8.5 %collective-permute-start.4 = (f32[2,32,512]{2,1,0:T(8,128)S(1)}, f32[2,32,512]{2,1,0:T(8,128)S(1)}, u32[]{:S(2)}, u32[]{:S(2)}) collective-permute-start(f32[2,32,512]{2,1,0:T(8,128)S(1)} %get-tuple-element.34.own), channel_id=1, source_target_pairs={{0,48},{16,32},{32,16},{48,0},{64,112},{80,96},{96,80},{112,64},{1... | collective-permute-start | bytes 393224 | tf_op jit(solution)/shard_map/ppermute | solution.py:502
  40.4 7.9 %collective-permute-start.3 = (f32[2,32,512]{2,1,0:T(8,128)S(1)}, f32[2,32,512]{2,1,0:T(8,128)S(1)}, u32[]{:S(2)}, u32[]{:S(2)}) collective-permute-start(f32[2,32,512]{2,1,0:T(8,128)S(1)} %get-tuple-element.34.own), channel_id=1, source_target_pairs={{0,32},{16,48},{32,0},{48,16},{64,96},{80,112},{96,64},{112,80},{1... | collective-permute-start | bytes 393224 | tf_op jit(solution)/shard_map/ppermute | solution.py:502
  42.5 6.4 %collective-permute-start.2 = (f32[2,32,512]{2,1,0:T(8,128)S(1)}, f32[2,32,512]{2,1,0:T(8,128)S(1)}, u32[]{:S(2)}, u32[]{:S(2)}) collective-permute-start(f32[2,32,512]{2,1,0:T(8,128)S(1)} %get-tuple-element.34.own), channel_id=1, source_target_pairs={{0,16},{16,0},{32,48},{48,32},{64,80},{80,64},{96,112},{112,96},{1... | collective-permute-start | bytes 393224 | tf_op jit(solution)/shard_map/ppermute | solution.py:502
  49.0 4.9 %collective-permute-start.5 = (f32[32,512]{1,0:T(8,128)S(1)}, f32[32,512]{1,0:T(8,128)S(1)}, u32[]{:S(2)}, u32[]{:S(2)}) collective-permute-start(f32[32,512]{1,0:T(8,128)S(1)} %get-tuple-element.39), channel_id=1, source_target_pairs={{0,64},{16,80},{32,96},{48,112},{64,0},{80,16},{96,32},{112,48},{1... | collective-permute-start | bytes 196616 | tf_op jit(solution)/shard_map/ppermute | solution.py:502
  49.1 5.6 %collective-permute-start.7 = (f32[32,512]{1,0:T(8,128)S(1)}, f32[32,512]{1,0:T(8,128)S(1)}, u32[]{:S(2)}, u32[]{:S(2)}) collective-permute-start(f32[32,512]{1,0:T(8,128)S(1)} %get-tuple-element.38), channel_id=1, source_target_pairs={{0,192},{16,208},{32,224},{48,240},{64,128},{80,144},{96,160},{112... | collective-permute-start | bytes 196616 | tf_op jit(solution)/shard_map/ppermute | solution.py:502
  50.4 5.8 %collective-permute-start.6 = (f32[32,512]{1,0:T(8,128)S(1)}, f32[32,512]{1,0:T(8,128)S(1)}, u32[]{:S(2)}, u32[]{:S(2)}) collective-permute-start(f32[32,512]{1,0:T(8,128)S(1)} %get-tuple-element.38), channel_id=1, source_target_pairs={{0,128},{16,144},{32,160},{48,176},{64,192},{80,208},{96,224},{112... | collective-permute-start | bytes 196616 | tf_op jit(solution)/shard_map/ppermute | solution.py:502

commit v6 on v5

--- a/solution.py
+++ b/solution.py
@@ -486,7 +486,7 @@
         in_specs=[away if k in remote else near for k in range(len(args))],
         out_specs=tuple([away if remote_outs else near] * len(outs)),
         scratch_shapes=list(scratch),
-        compiler_params=pltpu.CompilerParams(vmem_limit_bytes=room * 2**20),
+        compiler_params=pltpu.CompilerParams(vmem_limit_bytes=int(room * 2**20)),
         cost_estimate=pl.CostEstimate(flops=flops, bytes_accessed=moved, transcendentals=0),
     )(*args)
 
@@ -529,7 +529,7 @@
         goal,
         start,
         remote=range(5),
-        room=54,
+        room=53,
         scratch=(pltpu.VMEM((2, 6, rows, width), F32), pltpu.SemaphoreType.DMA((2, 6))),
     )
     below, above = swap_edges(*edges)

time: 57.8 us -> 56.9 us (0.984)
  Pallas kernels: 6.75 us -> 6.11 us
    pallas_call x8, Pallas kernels: 6.75 us -> 6.11 us  [call(): pl.pallas_call(kernel, out_shape=outs, in_specs=[away if k in remote else...]
where the time goes in v6:
time: 56.9 us; the launch traced here: 56.7 us
  blocking collectives  31.3 us (55%)
  starting transfers between devices  10.1 us (18%)
  waiting for transfers between devices  8.44 us (15%)
  Pallas kernels  6.11 us (11%)
  between operations  0.75 us (1%)
    all_to_all x2, blocking collectives, exchange(): return lax.all_to_all(value, 'rad', 0, 0, tiled=True)  31.3 us
    ppermute x6, starting transfers between devices, flip_permute(): lax.ppermute(value, 'rad', [(i, i ^ flip) for i in range(lax.axis_size('r...  8.35 us
    ppermute x6, waiting for transfers between devices, flip_permute(): lax.ppermute(value, 'rad', [(i, i ^ flip) for i in range(lax.axis_size('r...  7.96 us
    pallas_call x8, Pallas kernels, call(): pl.pallas_call(kernel, out_shape=outs, in_specs=[away if k in remote else...  6.11 us
    ppermute x1, starting transfers between devices, swap_edges(): lax.ppermute(low_edge, 'azi', [((i + 1) % count, i) for i in range(count)])  1.72 us
  transfers between devices with their start and end apart: 8, of which 6 were waited for; matrix products, arithmetic and copies ran while one was open for 0% of the time, Pallas kernels for 3%

profile of v6, /device:TPU:64, one launch (start us, length us, event | category | flops | bytes accessed | tf_op | source)
XLA Modules:
  0.0 56.7 jit_solution(10655842176079231397)
XLA Ops:
  0.6 0.0 copy-start.4
  0.6 0.0 copy-start.3
  0.7 0.0 copy-start.2
  0.7 0.0 copy-start.1
  0.7 1.3 %shard_map.70 = (f32[3,16,512]{2,1,0:T(8,128)S(1)}, f32[3,16,512]{2,1,0:T(8,128)S(1)}) custom-call(f32[16,32,512]{2,1,0:T(8,128)} %heat.3, f32[16,32,512]{2,1,0:T(8,128)} %deform.3, f32[16,32,512]{2,1,0:T(8,128)} %flux.3, f32[16,32,512]{2,1,0:T(8,128)} %goal.3, f32[16,32,512]{2,1,0:T(8,128)} %old.5), custom_call_target="tpu_custom_call" | custom-call | flops 1000000 | bytes 5439488 | tf_op jit(solution)/shard_map/pallas_call | solution.py:483
  2.0 0.0 collective-permute-start
  2.0 0.0 copy-start
  2.1 1.7 %collective-permute-start.1 = (f32[3,16,512]{2,1,0:T(8,128)S(1)}, f32[3,16,512]{2,1,0:T(8,128)S(1)}, u32[]{:S(2)}, u32[]{:S(2)}) collective-permute-start(f32[3,16,512]{2,1,0:T(8,128)S(1)} %get-tuple-element.27), channel_id=1, source_target_pairs={{1,0},{2,1},{3,2},{4,3},{5,4},{6,5},{7,6},{8,7},{9,8},{10,9},{11,1... | collective-permute-start | bytes 294920 | tf_op jit(solution)/shard_map/ppermute | solution.py:497
  3.8 0.0 copy-done.4
  3.8 0.0 copy-done.3
  3.8 0.0 copy-done.2
  3.8 0.0 copy-done.1
  3.8 1.1 %shard_map.68 = (f32[16,32,512]{2,1,0:T(8,128)S(1)}, f32[16,32,512]{2,1,0:T(8,128)S(1)}, f32[16,32,512]{2,1,0:T(8,128)S(1)}, f32[16,32,512]{2,1,0:T(8,128)S(1)},...) custom-call(f32[16,32,512]{2,1,0:T(8,128)S(1)} %copy-done.1, ...), custom_call_target="tpu_custom_call" | custom-call | flops 20000000 | bytes 10682368 | tf_op jit(solution)/shard_map/pallas_call | solution.py:483
  4.9 0.0 copy-done
  4.9 0.7 %shard_map.69 = (f32[16,32,512]{2,1,0:T(8,128)S(1)}, f32[16,2,8,128]{3,2,1,0:T(8,128)S(1)}) custom-call(f32[16,32,512]{2,1,0:T(8,128)S(1)} %copy-done, f32[16,32,512]{2,1,0:T(8,128)S(1)} %get-tuple-element.20.ahead, f32[16,32,512]{2,1,0:T(8,128)S(1)} %get-tuple-element.21.given, f32[16,32,512]{2,1,0:T(8,128)S(1)} %get-tuple-element.22.ratio), custom_call_target="tpu_custom_call" | custom-call | flops 1000000 | bytes 5373952 | tf_op jit(solution)/shard_map/pallas_call | solution.py:483
  5.6 0.5 collective-permute-done.below
  6.1 0.0 collective-permute-done.1.above
  6.1 0.4 shard_map.71
  6.5 17.6 %all_to_all.10.got = f32[16,6,8,128]{3,2,1,0:T(8,128)S(1)} all-to-all(f32[16,6,8,128]{3,2,1,0:T(8,128)S(1)} %get-tuple-element.31), channel_id=1, replica_groups=mesh['rad'=16,'azi'=16] {'rad'}, dimensions={0} | all-to-all | bytes 786432 | tf_op jit(solution)/shard_map/all_to_all | solution.py:506
  24.0 0.2 shard_map.72
  24.2 13.7 %all_to_all.11.got = f32[16,6,8,128]{3,2,1,0:T(8,128)S(1)} all-to-all(f32[16,6,8,128]{3,2,1,0:T(8,128)S(1)} %shard_map.72), channel_id=1, replica_groups=mesh['rad'=16,'azi'=16] {'rad'}, dimensions={0} | all-to-all | bytes 786432 | tf_op jit(solution)/shard_map/all_to_all | solution.py:506
  38.0 0.9 %shard_map.73 = (f32[16,32,512]{2,1,0:T(8,128)S(1)}, f32[2,32,512]{2,1,0:T(8,128)S(1)}, f32[32,512]{1,0:T(8,128)S(1)}) custom-call(f32[16,32,512]{2,1,0:T(8,128)S(1)} %get-tuple-element.23.before, f32[16,32,512]{2,1,0:T(8,128)S(1)} %get-tuple-element.24.left_map, f32[16,32,512]{2,1,0:T(8,128)S(1)} %get-tuple-element.25.right_map, ...), custom_call_target="tpu_custom_call" | custom-call | flops 1000000 | bytes 8388608 | tf_op jit(solution)/shard_map/pallas_call | solution.py:483
  38.9 0.6 %collective-permute-start.4 = (f32[2,32,512]{2,1,0:T(8,128)S(1)}, f32[2,32,512]{2,1,0:T(8,128)S(1)}, u32[]{:S(2)}, u32[]{:S(2)}) collective-permute-start(f32[2,32,512]{2,1,0:T(8,128)S(1)} %get-tuple-element.34.own), channel_id=1, source_target_pairs={{0,48},{16,32},{32,16},{48,0},{64,112},{80,96},{96,80},{112,64},{1... | collective-permute-start | bytes 393224 | tf_op jit(solution)/shard_map/ppermute | solution.py:502
  39.6 2.1 %collective-permute-start.3 = (f32[2,32,512]{2,1,0:T(8,128)S(1)}, f32[2,32,512]{2,1,0:T(8,128)S(1)}, u32[]{:S(2)}, u32[]{:S(2)}) collective-permute-start(f32[2,32,512]{2,1,0:T(8,128)S(1)} %get-tuple-element.34.own), channel_id=1, source_target_pairs={{0,32},{16,48},{32,0},{48,16},{64,96},{80,112},{96,64},{112,80},{1... | collective-permute-start | bytes 393224 | tf_op jit(solution)/shard_map/ppermute | solution.py:502
  41.6 1.5 %collective-permute-start.2 = (f32[2,32,512]{2,1,0:T(8,128)S(1)}, f32[2,32,512]{2,1,0:T(8,128)S(1)}, u32[]{:S(2)}, u32[]{:S(2)}) collective-permute-start(f32[2,32,512]{2,1,0:T(8,128)S(1)} %get-tuple-element.34.own), channel_id=1, source_target_pairs={{0,16},{16,0},{32,48},{48,32},{64,80},{80,64},{96,112},{112,96},{1... | collective-permute-start | bytes 393224 | tf_op jit(solution)/shard_map/ppermute | solution.py:502
  43.1 4.3 %collective-permute-done.4.third = f32[2,32,512]{2,1,0:T(8,128)S(1)} collective-permute-done((f32[2,32,512]{2,1,0:T(8,128)S(1)}, f32[2,32,512]{2,1,0:T(8,128)S(1)}, u32[]{:S(2)}, u32[]{:S(2)}) %collective-permute-start.4) | collective-permute-done | bytes 131104 | tf_op jit(solution)/shard_map/ppermute | solution.py:502
  47.4 0.0 collective-permute-done.3.second
  47.4 0.6 %collective-permute-done.2.first = f32[2,32,512]{2,1,0:T(8,128)S(1)} collective-permute-done((f32[2,32,512]{2,1,0:T(8,128)S(1)}, f32[2,32,512]{2,1,0:T(8,128)S(1)}, u32[]{:S(2)}, u32[]{:S(2)}) %collective-permute-start.2) | collective-permute-done | bytes 131104 | tf_op jit(solution)/shard_map/ppermute | solution.py:502
  48.0 0.1 shard_map.74
  48.1 0.1 collective-permute-start.5
  48.2 1.3 %collective-permute-start.7 = (f32[32,512]{1,0:T(8,128)S(1)}, f32[32,512]{1,0:T(8,128)S(1)}, u32[]{:S(2)}, u32[]{:S(2)}) collective-permute-start(f32[32,512]{1,0:T(8,128)S(1)} %get-tuple-element.38), channel_id=1, source_target_pairs={{0,192},{16,208},{32,224},{48,240},{64,128},{80,144},{96,160},{112... | collective-permute-start | bytes 196616 | tf_op jit(solution)/shard_map/ppermute | solution.py:502
  49.5 2.7 %collective-permute-start.6 = (f32[32,512]{1,0:T(8,128)S(1)}, f32[32,512]{1,0:T(8,128)S(1)}, u32[]{:S(2)}, u32[]{:S(2)}) collective-permute-start(f32[32,512]{1,0:T(8,128)S(1)} %get-tuple-element.38), channel_id=1, source_target_pairs={{0,128},{16,144},{32,160},{48,176},{64,192},{80,208},{96,224},{112... | collective-permute-start | bytes 196616 | tf_op jit(solution)/shard_map/ppermute | solution.py:502
  52.3 0.6 %collective-permute-done.5.first = f32[32,512]{1,0:T(8,128)S(1)} collective-permute-done((f32[32,512]{1,0:T(8,128)S(1)}, f32[32,512]{1,0:T(8,128)S(1)}, u32[]{:S(2)}, u32[]{:S(2)}) %collective-permute-start.5) | collective-permute-done | bytes 65568 | tf_op jit(solution)/shard_map/ppermute | solution.py:502
  52.9 0.8 %collective-permute-done.7.third = f32[32,512]{1,0:T(8,128)S(1)} collective-permute-done((f32[32,512]{1,0:T(8,128)S(1)}, f32[32,512]{1,0:T(8,128)S(1)}, u32[]{:S(2)}, u32[]{:S(2)}) %collective-permute-start.7) | collective-permute-done | bytes 65568 | tf_op jit(solution)/shard_map/ppermute | solution.py:502
  53.8 1.5 %collective-permute-done.6.second = f32[32,512]{1,0:T(8,128)S(1)} collective-permute-done((f32[32,512]{1,0:T(8,128)S(1)}, f32[32,512]{1,0:T(8,128)S(1)}, u32[]{:S(2)}, u32[]{:S(2)}) %collective-permute-start.6) | collective-permute-done | bytes 65568 | tf_op jit(solution)/shard_map/ppermute | solution.py:502
  55.3 1.4 %shard_map.75 = (f32[16,32,512]{2,1,0:T(8,128)}, f32[16,32,512]{2,1,0:T(8,128)}) custom-call(f32[16,32,512]{2,1,0:T(8,128)S(1)} %get-tuple-element.32.particular, f32[16,32,512]{2,1,0:T(8,128)S(1)} %get-tuple-element.24.left_map, f32[16,32,512]{2,1,0:T(8,128)S(1)} %get-tuple-element.25.right_map, f32[16,32,512]{2,1,0:T(8,128)S(1)} %get-tuple-element.33.factor, ...), custom_call_target="tpu_custom_call" | custom-call | flops 1000000 | bytes 7208960 | tf_op jit(solution)/shard_map/pallas_call | solution.py:483
  (1 shorter events, 0.0 us)
Async XLA Ops:
  0.6 3.1 %copy-start.4 = (f32[16,32,512]{2,1,0:T(8,128)S(1)}, f32[16,32,512]{2,1,0:T(8,128)}, u32[]{:S(2)}) copy-start(f32[16,32,512]{2,1,0:T(8,128)} %goal.3) | copy-start | bytes 3145732
  0.6 3.1 %copy-start.3 = (f32[16,32,512]{2,1,0:T(8,128)S(1)}, f32[16,32,512]{2,1,0:T(8,128)}, u32[]{:S(2)}) copy-start(f32[16,32,512]{2,1,0:T(8,128)} %flux.3) | copy-start | bytes 3145732
  0.7 3.1 %copy-start.2 = (f32[16,32,512]{2,1,0:T(8,128)S(1)}, f32[16,32,512]{2,1,0:T(8,128)}, u32[]{:S(2)}) copy-start(f32[16,32,512]{2,1,0:T(8,128)} %deform.3) | copy-start | bytes 3145732
  0.7 3.1 %copy-start.1 = (f32[16,32,512]{2,1,0:T(8,128)S(1)}, f32[16,32,512]{2,1,0:T(8,128)}, u32[]{:S(2)}) copy-start(f32[16,32,512]{2,1,0:T(8,128)} %heat.3) | copy-start | bytes 3145732
  2.0 4.1 %collective-permute-start = (f32[3,16,512]{2,1,0:T(8,128)S(1)}, f32[3,16,512]{2,1,0:T(8,128)S(1)}, u32[]{:S(2)}, u32[]{:S(2)}) collective-permute-start(f32[3,16,512]{2,1,0:T(8,128)S(1)} %get-tuple-element.26), channel_id=1, source_target_pairs={{0,1},{1,2},{2,3},{3,4},{4,5},{5,6},{6,7},{7,8},{8,9},{9,10},{10,1... | collective-permute-start | bytes 294920 | tf_op jit(solution)/shard_map/ppermute | solution.py:496
  2.0 2.8 %copy-start = (f32[16,32,512]{2,1,0:T(8,128)S(1)}, f32[16,32,512]{2,1,0:T(8,128)}, u32[]{:S(2)}) copy-start(f32[16,32,512]{2,1,0:T(8,128)} %old.5) | copy-start | bytes 3145732
  2.1 4.0 %collective-permute-start.1 = (f32[3,16,512]{2,1,0:T(8,128)S(1)}, f32[3,16,512]{2,1,0:T(8,128)S(1)}, u32[]{:S(2)}, u32[]{:S(2)}) collective-permute-start(f32[3,16,512]{2,1,0:T(8,128)S(1)} %get-tuple-element.27), channel_id=1, source_target_pairs={{1,0},{2,1},{3,2},{4,3},{5,4},{6,5},{7,6},{8,7},{9,8},{10,9},{11,1... | collective-permute-start | bytes 294920 | tf_op jit(solution)/shard_map/ppermute | solution.py:497
  38.9 8.5 %collective-permute-start.4 = (f32[2,32,512]{2,1,0:T(8,128)S(1)}, f32[2,32,512]{2,1,0:T(8,128)S(1)}, u32[]{:S(2)}, u32[]{:S(2)}) collective-permute-start(f32[2,32,512]{2,1,0:T(8,128)S(1)} %get-tuple-element.34.own), channel_id=1, source_target_pairs={{0,48},{16,32},{32,16},{48,0},{64,112},{80,96},{96,80},{112,64},{1... | collective-permute-start | bytes 393224 | tf_op jit(solution)/shard_map/ppermute | solution.py:502
  39.6 7.8 %collective-permute-start.3 = (f32[2,32,512]{2,1,0:T(8,128)S(1)}, f32[2,32,512]{2,1,0:T(8,128)S(1)}, u32[]{:S(2)}, u32[]{:S(2)}) collective-permute-start(f32[2,32,512]{2,1,0:T(8,128)S(1)} %get-tuple-element.34.own), channel_id=1, source_target_pairs={{0,32},{16,48},{32,0},{48,16},{64,96},{80,112},{96,64},{112,80},{1... | collective-permute-start | bytes 393224 | tf_op jit(solution)/shard_map/ppermute | solution.py:502
  41.6 6.4 %collective-permute-start.2 = (f32[2,32,512]{2,1,0:T(8,128)S(1)}, f32[2,32,512]{2,1,0:T(8,128)S(1)}, u32[]{:S(2)}, u32[]{:S(2)}) collective-permute-start(f32[2,32,512]{2,1,0:T(8,128)S(1)} %get-tuple-element.34.own), channel_id=1, source_target_pairs={{0,16},{16,0},{32,48},{48,32},{64,80},{80,64},{96,112},{112,96},{1... | collective-permute-start | bytes 393224 | tf_op jit(solution)/shard_map/ppermute | solution.py:502
  48.1 4.8 %collective-permute-start.5 = (f32[32,512]{1,0:T(8,128)S(1)}, f32[32,512]{1,0:T(8,128)S(1)}, u32[]{:S(2)}, u32[]{:S(2)}) collective-permute-start(f32[32,512]{1,0:T(8,128)S(1)} %get-tuple-element.39), channel_id=1, source_target_pairs={{0,64},{16,80},{32,96},{48,112},{64,0},{80,16},{96,32},{112,48},{1... | collective-permute-start | bytes 196616 | tf_op jit(solution)/shard_map/ppermute | solution.py:502
  48.2 5.6 %collective-permute-start.7 = (f32[32,512]{1,0:T(8,128)S(1)}, f32[32,512]{1,0:T(8,128)S(1)}, u32[]{:S(2)}, u32[]{:S(2)}) collective-permute-start(f32[32,512]{1,0:T(8,128)S(1)} %get-tuple-element.38), channel_id=1, source_target_pairs={{0,192},{16,208},{32,224},{48,240},{64,128},{80,144},{96,160},{112... | collective-permute-start | bytes 196616 | tf_op jit(solution)/shard_map/ppermute | solution.py:502
  49.5 5.8 %collective-permute-start.6 = (f32[32,512]{1,0:T(8,128)S(1)}, f32[32,512]{1,0:T(8,128)S(1)}, u32[]{:S(2)}, u32[]{:S(2)}) collective-permute-start(f32[32,512]{1,0:T(8,128)S(1)} %get-tuple-element.38), channel_id=1, source_target_pairs={{0,128},{16,144},{32,160},{48,176},{64,192},{80,208},{96,224},{112... | collective-permute-start | bytes 196616 | tf_op jit(solution)/shard_map/ppermute | solution.py:502

commit v7 on v6

--- a/solution.py
+++ b/solution.py
@@ -16,7 +16,6 @@
 
 SUB, LANE = 8, 128
 GROUP = 4
-PIECE = 16
 F32 = jnp.float32
 
 
@@ -352,10 +351,9 @@
     outside,
     ahead,
     given,
-    ratio,
     condensed,
     got,
-    particular,
+    source,
     own,
     fall,
     padded,
@@ -392,9 +390,14 @@
             place(padded, group, i, value)
     for group in range(groups):
         here = pl.ds(group * SUB, SUB)
-        source = sources(group, padded, ahead, given, behind, radii, quarter)
-        inner, outer = local_solve(group, source, ratio, inverse_links, particular)
-        inner = links[0] * inner
+        values = sources(group, padded, ahead, given, behind, radii, quarter)
+        inner = jnp.zeros((SUB, width), F32)
+        outer = values[rows - 1]
+        for i in range(rows):
+            source[i, here, :] = values[i]
+            if i < rows - 1:
+                inner = inner + left_map[i, here, :] * values[i]
+                outer = outer + right_map[i, here, :] * values[i]
         rise_left, rise_right, fall_right = [tiles_of(got, group, plane, width) for plane in (2, 3, 4)]
         through = tiles_of(condensed, group, 0, width)
         fall_left = (1.0 / through + rise_left * fall_right) / rise_right
@@ -404,7 +407,16 @@
         own[1, here, :] = fall_left * inner + fall_right * outer
 
 
-def gather_kernel(own, first, second, third, near, message):
+def inner_kernel(source, ratio, particular):
+    rows, azimuths, width = source.shape
+    _, _, inverse_links, _, _ = tables(rows, width)
+    for group in range(azimuths // SUB):
+        here = pl.ds(group * SUB, SUB)
+        values = [source[i, here, :] for i in range(rows)]
+        local_solve(group, values, ratio, inverse_links, particular)
+
+
+def gather_kernel(own, first, second, third, near, message_far, message_near):
     mine = lax.rem(lax.axis_index("rad"), GROUP)
     block = lax.div(lax.axis_index("rad"), GROUP)
     for group in range(own.shape[1] // SUB):
@@ -420,8 +432,8 @@
             upper = upper + jnp.where(below, 0.0, down)
         near[0, here, :] = lower
         near[1, here, :] = upper
-        for slot, flip in ((0, 1), (1, 2)):
-            message[slot, here, :] = jnp.where((block ^ flip) > block, upward, downward)
+        for message, flip in ((message_far, 2), (message_near, 1)):
+            message[here, :] = jnp.where((block ^ flip) > block, upward, downward)
 
 
 def last_kernel(
@@ -462,14 +474,15 @@
             value = particular[i, here, :] + left_map[i, here, :] * left + right_map[i, here, :] * right
             result_out[i, here, :] = value
             sensitivity_out[i, here, :] = value * factor[i, here, :]
-            if (i + 1) % PIECE:
+            piece = rows // 2 if group == azimuths // SUB - 1 else rows
+            if (i + 1) % piece:
                 continue
-            part = pl.ds(i + 1 - PIECE, PIECE)
+            part = pl.ds(i + 1 - piece, piece)
             for k, (source, target) in enumerate(
                 ((result_out, result), (sensitivity_out, sensitivity))
             ):
                 copy = pltpu.make_async_copy(
-                    source.at[part, here, :], target.at[part, here, :], done.at[group, i // PIECE, k]
+                    source.at[part, here, :], target.at[part, here, :], done.at[group, i // piece, k]
                 )
                 copy.start()
                 copies.append(copy)
@@ -561,7 +574,7 @@
         exchange(message),
     )[0]
     got = exchange(sent)
-    particular, own, fall = call(
+    source, own, fall = call(
         third_kernel,
         (block, pair, jax.ShapeDtypeStruct((azimuths, width), F32)),
         particular,
@@ -570,14 +583,16 @@
         outside,
         ahead,
         given,
-        ratio,
         condensed,
         got,
         scratch=(padded,),
     )
+    (particular,) = call(inner_kernel, (block,), source, ratio)
     others = [flip_permute(own, flip) for flip in (1, 2, 3)]
-    near, message = call(gather_kernel, (pair, pair), own, *others)
-    far = [flip_permute(message[min(flip, 2) - 1], flip * GROUP) for flip in (1, 2, 3)]
+    plane = jax.ShapeDtypeStruct((azimuths, width), F32)
+    near, message_far, message_near = call(gather_kernel, (pair, plane, plane), own, *others)
+    messages = (message_near, message_far, message_far)
+    far = [flip_permute(item, flip * GROUP) for flip, item in zip((1, 2, 3), messages)]
     return call(
         last_kernel,
         (block, block),
@@ -591,7 +606,7 @@
         near,
         *far,
         remote_outs=True,
-        scratch=(held, held, pltpu.SemaphoreType.DMA((groups, rows // PIECE, 2))),
+        scratch=(held, held, pltpu.SemaphoreType.DMA((groups, 2, 2))),
     )
 
 

time: 56.9 us -> 57 us (level)
    pallas_call x8 -> x9, Pallas kernels: 6.11 us -> 6.4 us  [call(): pl.pallas_call(kernel, out_shape=outs, in_specs=[away if k in remote else...]
  transfers between devices with their start and end apart: 8 -> 8, of which waited for: 6 -> 6; matrix products, arithmetic and copies ran while one was open for 0% -> 0% of each run, Pallas kernels for 3% -> 4%
where the time goes in v7:
time: 57 us; the launch traced here: 56.8 us
  blocking collectives  31.3 us (55%)
  starting transfers between devices  10.1 us (18%)
  waiting for transfers between devices  8.22 us (14%)
  Pallas kernels  6.4 us (11%)
  between operations  0.74 us (1%)
    all_to_all x2, blocking collectives, exchange(): return lax.all_to_all(value, 'rad', 0, 0, tiled=True)  31.3 us
    ppermute x6, starting transfers between devices, flip_permute(): lax.ppermute(value, 'rad', [(i, i ^ flip) for i in range(lax.axis_size('r...  8.35 us
    ppermute x6, waiting for transfers between devices, flip_permute(): lax.ppermute(value, 'rad', [(i, i ^ flip) for i in range(lax.axis_size('r...  7.74 us
    pallas_call x9, Pallas kernels, call(): pl.pallas_call(kernel, out_shape=outs, in_specs=[away if k in remote else...  6.4 us
    ppermute x1, starting transfers between devices, swap_edges(): lax.ppermute(low_edge, 'azi', [((i + 1) % count, i) for i in range(count)])  1.72 us
  transfers between devices with their start and end apart: 8, of which 6 were waited for; matrix products, arithmetic and copies ran while one was open for 0% of the time, Pallas kernels for 4%

profile of v7, /device:TPU:64, one launch (start us, length us, event | category | flops | bytes accessed | tf_op | source)
XLA Modules:
  0.0 56.8 jit_solution(6653343461802024601)
XLA Ops:
  0.6 0.0 copy-start.4
  0.6 0.0 copy-start.3
  0.7 0.0 copy-start.2
  0.7 0.0 copy-start.1
  0.7 1.3 %shard_map.70 = (f32[3,16,512]{2,1,0:T(8,128)S(1)}, f32[3,16,512]{2,1,0:T(8,128)S(1)}) custom-call(f32[16,32,512]{2,1,0:T(8,128)} %heat.3, f32[16,32,512]{2,1,0:T(8,128)} %deform.3, f32[16,32,512]{2,1,0:T(8,128)} %flux.3, f32[16,32,512]{2,1,0:T(8,128)} %goal.3, f32[16,32,512]{2,1,0:T(8,128)} %old.5), custom_call_target="tpu_custom_call" | custom-call | flops 1000000 | bytes 5439488 | tf_op jit(solution)/shard_map/pallas_call | solution.py:496
  2.0 0.0 collective-permute-start
  2.0 0.0 copy-start
  2.1 1.7 %collective-permute-start.1 = (f32[3,16,512]{2,1,0:T(8,128)S(1)}, f32[3,16,512]{2,1,0:T(8,128)S(1)}, u32[]{:S(2)}, u32[]{:S(2)}) collective-permute-start(f32[3,16,512]{2,1,0:T(8,128)S(1)} %get-tuple-element.28), channel_id=1, source_target_pairs={{1,0},{2,1},{3,2},{4,3},{5,4},{6,5},{7,6},{8,7},{9,8},{10,9},{11,1... | collective-permute-start | bytes 294920 | tf_op jit(solution)/shard_map/ppermute | solution.py:510
  3.8 0.0 copy-done.4
  3.8 0.0 copy-done.3
  3.8 0.0 copy-done.2
  3.8 0.0 copy-done.1
  3.8 1.1 %shard_map.68 = (f32[16,32,512]{2,1,0:T(8,128)S(1)}, f32[16,32,512]{2,1,0:T(8,128)S(1)}, f32[16,32,512]{2,1,0:T(8,128)S(1)}, f32[16,32,512]{2,1,0:T(8,128)S(1)},...) custom-call(f32[16,32,512]{2,1,0:T(8,128)S(1)} %copy-done.1, ...), custom_call_target="tpu_custom_call" | custom-call | flops 20000000 | bytes 10682368 | tf_op jit(solution)/shard_map/pallas_call | solution.py:496
  4.9 0.0 copy-done
  4.9 0.7 %shard_map.69 = (f32[16,32,512]{2,1,0:T(8,128)S(1)}, f32[16,2,8,128]{3,2,1,0:T(8,128)S(1)}) custom-call(f32[16,32,512]{2,1,0:T(8,128)S(1)} %copy-done, f32[16,32,512]{2,1,0:T(8,128)S(1)} %get-tuple-element.21.ahead, f32[16,32,512]{2,1,0:T(8,128)S(1)} %get-tuple-element.22.given, f32[16,32,512]{2,1,0:T(8,128)S(1)} %get-tuple-element.23.ratio), custom_call_target="tpu_custom_call" | custom-call | flops 1000000 | bytes 5373952 | tf_op jit(solution)/shard_map/pallas_call | solution.py:496
  5.6 0.5 collective-permute-done.below
  6.1 0.0 collective-permute-done.1.above
  6.1 0.4 shard_map.71
  6.5 17.6 %all_to_all.10.got = f32[16,6,8,128]{3,2,1,0:T(8,128)S(1)} all-to-all(f32[16,6,8,128]{3,2,1,0:T(8,128)S(1)} %get-tuple-element.32), channel_id=1, replica_groups=mesh['rad'=16,'azi'=16] {'rad'}, dimensions={0} | all-to-all | bytes 786432 | tf_op jit(solution)/shard_map/all_to_all | solution.py:519
  24.0 0.2 shard_map.72
  24.2 13.7 %all_to_all.11.got = f32[16,6,8,128]{3,2,1,0:T(8,128)S(1)} all-to-all(f32[16,6,8,128]{3,2,1,0:T(8,128)S(1)} %shard_map.72), channel_id=1, replica_groups=mesh['rad'=16,'azi'=16] {'rad'}, dimensions={0} | all-to-all | bytes 786432 | tf_op jit(solution)/shard_map/all_to_all | solution.py:519
  38.0 0.9 %shard_map.73 = (f32[16,32,512]{2,1,0:T(8,128)S(1)}, f32[2,32,512]{2,1,0:T(8,128)S(1)}, f32[32,512]{1,0:T(8,128)S(1)}) custom-call(f32[16,32,512]{2,1,0:T(8,128)S(1)} %get-tuple-element.24.before, f32[16,32,512]{2,1,0:T(8,128)S(1)} %get-tuple-element.25.left_map, f32[16,32,512]{2,1,0:T(8,128)S(1)} %get-tuple-element.26.right_map, ...), custom_call_target="tpu_custom_call" | custom-call | flops 1000000 | bytes 7340032 | tf_op jit(solution)/shard_map/pallas_call | solution.py:496
  38.9 0.6 %collective-permute-start.4 = (f32[2,32,512]{2,1,0:T(8,128)S(1)}, f32[2,32,512]{2,1,0:T(8,128)S(1)}, u32[]{:S(2)}, u32[]{:S(2)}) collective-permute-start(f32[2,32,512]{2,1,0:T(8,128)S(1)} %get-tuple-element.35.own), channel_id=1, source_target_pairs={{0,48},{16,32},{32,16},{48,0},{64,112},{80,96},{96,80},{112,64},{1... | collective-permute-start | bytes 393224 | tf_op jit(solution)/shard_map/ppermute | solution.py:515
  39.6 2.1 %collective-permute-start.3 = (f32[2,32,512]{2,1,0:T(8,128)S(1)}, f32[2,32,512]{2,1,0:T(8,128)S(1)}, u32[]{:S(2)}, u32[]{:S(2)}) collective-permute-start(f32[2,32,512]{2,1,0:T(8,128)S(1)} %get-tuple-element.35.own), channel_id=1, source_target_pairs={{0,32},{16,48},{32,0},{48,16},{64,96},{80,112},{96,64},{112,80},{1... | collective-permute-start | bytes 393224 | tf_op jit(solution)/shard_map/ppermute | solution.py:515
  41.6 1.5 %collective-permute-start.2 = (f32[2,32,512]{2,1,0:T(8,128)S(1)}, f32[2,32,512]{2,1,0:T(8,128)S(1)}, u32[]{:S(2)}, u32[]{:S(2)}) collective-permute-start(f32[2,32,512]{2,1,0:T(8,128)S(1)} %get-tuple-element.35.own), channel_id=1, source_target_pairs={{0,16},{16,0},{32,48},{48,32},{64,80},{80,64},{96,112},{112,96},{1... | collective-permute-start | bytes 393224 | tf_op jit(solution)/shard_map/ppermute | solution.py:515
  43.1 4.3 %collective-permute-done.4.third = f32[2,32,512]{2,1,0:T(8,128)S(1)} collective-permute-done((f32[2,32,512]{2,1,0:T(8,128)S(1)}, f32[2,32,512]{2,1,0:T(8,128)S(1)}, u32[]{:S(2)}, u32[]{:S(2)}) %collective-permute-start.4) | collective-permute-done | bytes 131104 | tf_op jit(solution)/shard_map/ppermute | solution.py:515
  47.4 0.0 collective-permute-done.3.second
  47.4 0.6 %collective-permute-done.2.first = f32[2,32,512]{2,1,0:T(8,128)S(1)} collective-permute-done((f32[2,32,512]{2,1,0:T(8,128)S(1)}, f32[2,32,512]{2,1,0:T(8,128)S(1)}, u32[]{:S(2)}, u32[]{:S(2)}) %collective-permute-start.2) | collective-permute-done | bytes 131104 | tf_op jit(solution)/shard_map/ppermute | solution.py:515
  48.0 0.1 shard_map.75
  48.1 0.1 collective-permute-start.5
  48.2 1.3 %collective-permute-start.7 = (f32[32,512]{1,0:T(8,128)S(1)}, f32[32,512]{1,0:T(8,128)S(1)}, u32[]{:S(2)}, u32[]{:S(2)}) collective-permute-start(f32[32,512]{1,0:T(8,128)S(1)} %get-tuple-element.39), channel_id=1, source_target_pairs={{0,192},{16,208},{32,224},{48,240},{64,128},{80,144},{96,160},{112... | collective-permute-start | bytes 196616 | tf_op jit(solution)/shard_map/ppermute | solution.py:515
  49.5 2.7 %collective-permute-start.6 = (f32[32,512]{1,0:T(8,128)S(1)}, f32[32,512]{1,0:T(8,128)S(1)}, u32[]{:S(2)}, u32[]{:S(2)}) collective-permute-start(f32[32,512]{1,0:T(8,128)S(1)} %get-tuple-element.39), channel_id=1, source_target_pairs={{0,128},{16,144},{32,160},{48,176},{64,192},{80,208},{96,224},{112... | collective-permute-start | bytes 196616 | tf_op jit(solution)/shard_map/ppermute | solution.py:515
  52.3 0.2 shard_map.74.particular
  52.5 0.4 collective-permute-done.5.first
  52.9 0.8 %collective-permute-done.7.third = f32[32,512]{1,0:T(8,128)S(1)} collective-permute-done((f32[32,512]{1,0:T(8,128)S(1)}, f32[32,512]{1,0:T(8,128)S(1)}, u32[]{:S(2)}, u32[]{:S(2)}) %collective-permute-start.7) | collective-permute-done | bytes 65568 | tf_op jit(solution)/shard_map/ppermute | solution.py:515
  53.7 1.5 %collective-permute-done.6.second = f32[32,512]{1,0:T(8,128)S(1)} collective-permute-done((f32[32,512]{1,0:T(8,128)S(1)}, f32[32,512]{1,0:T(8,128)S(1)}, u32[]{:S(2)}, u32[]{:S(2)}) %collective-permute-start.6) | collective-permute-done | bytes 65568 | tf_op jit(solution)/shard_map/ppermute | solution.py:515
  55.3 1.5 %shard_map.76 = (f32[16,32,512]{2,1,0:T(8,128)}, f32[16,32,512]{2,1,0:T(8,128)}) custom-call(f32[16,32,512]{2,1,0:T(8,128)S(1)} %shard_map.74.particular, f32[16,32,512]{2,1,0:T(8,128)S(1)} %get-tuple-element.25.left_map, f32[16,32,512]{2,1,0:T(8,128)S(1)} %get-tuple-element.26.right_map, f32[16,32,512]{2,1,0:T(8,128)S(1)} %get-tuple-element.34.factor, ...), custom_call_target="tpu_custom_call" | custom-call | flops 1000000 | bytes 7208960 | tf_op jit(solution)/shard_map/pallas_call | solution.py:496
Async XLA Ops:
  0.6 3.1 %copy-start.4 = (f32[16,32,512]{2,1,0:T(8,128)S(1)}, f32[16,32,512]{2,1,0:T(8,128)}, u32[]{:S(2)}) copy-start(f32[16,32,512]{2,1,0:T(8,128)} %goal.3) | copy-start | bytes 3145732
  0.6 3.1 %copy-start.3 = (f32[16,32,512]{2,1,0:T(8,128)S(1)}, f32[16,32,512]{2,1,0:T(8,128)}, u32[]{:S(2)}) copy-start(f32[16,32,512]{2,1,0:T(8,128)} %flux.3) | copy-start | bytes 3145732
  0.7 3.1 %copy-start.2 = (f32[16,32,512]{2,1,0:T(8,128)S(1)}, f32[16,32,512]{2,1,0:T(8,128)}, u32[]{:S(2)}) copy-start(f32[16,32,512]{2,1,0:T(8,128)} %deform.3) | copy-start | bytes 3145732
  0.7 3.1 %copy-start.1 = (f32[16,32,512]{2,1,0:T(8,128)S(1)}, f32[16,32,512]{2,1,0:T(8,128)}, u32[]{:S(2)}) copy-start(f32[16,32,512]{2,1,0:T(8,128)} %heat.3) | copy-start | bytes 3145732
  2.0 4.1 %collective-permute-start = (f32[3,16,512]{2,1,0:T(8,128)S(1)}, f32[3,16,512]{2,1,0:T(8,128)S(1)}, u32[]{:S(2)}, u32[]{:S(2)}) collective-permute-start(f32[3,16,512]{2,1,0:T(8,128)S(1)} %get-tuple-element.27), channel_id=1, source_target_pairs={{0,1},{1,2},{2,3},{3,4},{4,5},{5,6},{6,7},{7,8},{8,9},{9,10},{10,1... | collective-permute-start | bytes 294920 | tf_op jit(solution)/shard_map/ppermute | solution.py:509
  2.0 2.8 %copy-start = (f32[16,32,512]{2,1,0:T(8,128)S(1)}, f32[16,32,512]{2,1,0:T(8,128)}, u32[]{:S(2)}) copy-start(f32[16,32,512]{2,1,0:T(8,128)} %old.5) | copy-start | bytes 3145732
  2.1 4.0 %collective-permute-start.1 = (f32[3,16,512]{2,1,0:T(8,128)S(1)}, f32[3,16,512]{2,1,0:T(8,128)S(1)}, u32[]{:S(2)}, u32[]{:S(2)}) collective-permute-start(f32[3,16,512]{2,1,0:T(8,128)S(1)} %get-tuple-element.28), channel_id=1, source_target_pairs={{1,0},{2,1},{3,2},{4,3},{5,4},{6,5},{7,6},{8,7},{9,8},{10,9},{11,1... | collective-permute-start | bytes 294920 | tf_op jit(solution)/shard_map/ppermute | solution.py:510
  38.9 8.5 %collective-permute-start.4 = (f32[2,32,512]{2,1,0:T(8,128)S(1)}, f32[2,32,512]{2,1,0:T(8,128)S(1)}, u32[]{:S(2)}, u32[]{:S(2)}) collective-permute-start(f32[2,32,512]{2,1,0:T(8,128)S(1)} %get-tuple-element.35.own), channel_id=1, source_target_pairs={{0,48},{16,32},{32,16},{48,0},{64,112},{80,96},{96,80},{112,64},{1... | collective-permute-start | bytes 393224 | tf_op jit(solution)/shard_map/ppermute | solution.py:515
  39.6 7.8 %collective-permute-start.3 = (f32[2,32,512]{2,1,0:T(8,128)S(1)}, f32[2,32,512]{2,1,0:T(8,128)S(1)}, u32[]{:S(2)}, u32[]{:S(2)}) collective-permute-start(f32[2,32,512]{2,1,0:T(8,128)S(1)} %get-tuple-element.35.own), channel_id=1, source_target_pairs={{0,32},{16,48},{32,0},{48,16},{64,96},{80,112},{96,64},{112,80},{1... | collective-permute-start | bytes 393224 | tf_op jit(solution)/shard_map/ppermute | solution.py:515
  41.6 6.4 %collective-permute-start.2 = (f32[2,32,512]{2,1,0:T(8,128)S(1)}, f32[2,32,512]{2,1,0:T(8,128)S(1)}, u32[]{:S(2)}, u32[]{:S(2)}) collective-permute-start(f32[2,32,512]{2,1,0:T(8,128)S(1)} %get-tuple-element.35.own), channel_id=1, source_target_pairs={{0,16},{16,0},{32,48},{48,32},{64,80},{80,64},{96,112},{112,96},{1... | collective-permute-start | bytes 393224 | tf_op jit(solution)/shard_map/ppermute | solution.py:515
  48.1 4.8 %collective-permute-start.5 = (f32[32,512]{1,0:T(8,128)S(1)}, f32[32,512]{1,0:T(8,128)S(1)}, u32[]{:S(2)}, u32[]{:S(2)}) collective-permute-start(f32[32,512]{1,0:T(8,128)S(1)} %get-tuple-element.38), channel_id=1, source_target_pairs={{0,64},{16,80},{32,96},{48,112},{64,0},{80,16},{96,32},{112,48},{1... | collective-permute-start | bytes 196616 | tf_op jit(solution)/shard_map/ppermute | solution.py:515
  48.2 5.6 %collective-permute-start.7 = (f32[32,512]{1,0:T(8,128)S(1)}, f32[32,512]{1,0:T(8,128)S(1)}, u32[]{:S(2)}, u32[]{:S(2)}) collective-permute-start(f32[32,512]{1,0:T(8,128)S(1)} %get-tuple-element.39), channel_id=1, source_target_pairs={{0,192},{16,208},{32,224},{48,240},{64,128},{80,144},{96,160},{112... | collective-permute-start | bytes 196616 | tf_op jit(solution)/shard_map/ppermute | solution.py:515
  49.5 5.8 %collective-permute-start.6 = (f32[32,512]{1,0:T(8,128)S(1)}, f32[32,512]{1,0:T(8,128)S(1)}, u32[]{:S(2)}, u32[]{:S(2)}) collective-permute-start(f32[32,512]{1,0:T(8,128)S(1)} %get-tuple-element.39), channel_id=1, source_target_pairs={{0,128},{16,144},{32,160},{48,176},{64,192},{80,208},{96,224},{112... | collective-permute-start | bytes 196616 | tf_op jit(solution)/shard_map/ppermute | solution.py:515

commit v8 on v6

--- a/solution.py
+++ b/solution.py
@@ -16,7 +16,6 @@
 
 SUB, LANE = 8, 128
 GROUP = 4
-PIECE = 16
 F32 = jnp.float32
 
 
@@ -404,7 +403,7 @@
         own[1, here, :] = fall_left * inner + fall_right * outer
 
 
-def gather_kernel(own, first, second, third, near, message):
+def gather_kernel(own, first, second, third, near, message_far, message_near):
     mine = lax.rem(lax.axis_index("rad"), GROUP)
     block = lax.div(lax.axis_index("rad"), GROUP)
     for group in range(own.shape[1] // SUB):
@@ -420,8 +419,8 @@
             upper = upper + jnp.where(below, 0.0, down)
         near[0, here, :] = lower
         near[1, here, :] = upper
-        for slot, flip in ((0, 1), (1, 2)):
-            message[slot, here, :] = jnp.where((block ^ flip) > block, upward, downward)
+        for message, flip in ((message_far, 2), (message_near, 1)):
+            message[here, :] = jnp.where((block ^ flip) > block, upward, downward)
 
 
 def last_kernel(
@@ -462,14 +461,15 @@
             value = particular[i, here, :] + left_map[i, here, :] * left + right_map[i, here, :] * right
             result_out[i, here, :] = value
             sensitivity_out[i, here, :] = value * factor[i, here, :]
-            if (i + 1) % PIECE:
+            piece = rows // 2 if group == azimuths // SUB - 1 else rows
+            if (i + 1) % piece:
                 continue
-            part = pl.ds(i + 1 - PIECE, PIECE)
+            part = pl.ds(i + 1 - piece, piece)
             for k, (source, target) in enumerate(
                 ((result_out, result), (sensitivity_out, sensitivity))
             ):
                 copy = pltpu.make_async_copy(
-                    source.at[part, here, :], target.at[part, here, :], done.at[group, i // PIECE, k]
+                    source.at[part, here, :], target.at[part, here, :], done.at[group, i // piece, k]
                 )
                 copy.start()
                 copies.append(copy)
@@ -576,8 +576,10 @@
         scratch=(padded,),
     )
     others = [flip_permute(own, flip) for flip in (1, 2, 3)]
-    near, message = call(gather_kernel, (pair, pair), own, *others)
-    far = [flip_permute(message[min(flip, 2) - 1], flip * GROUP) for flip in (1, 2, 3)]
+    plane = jax.ShapeDtypeStruct((azimuths, width), F32)
+    near, message_far, message_near = call(gather_kernel, (pair, plane, plane), own, *others)
+    messages = (message_near, message_far, message_far)
+    far = [flip_permute(item, flip * GROUP) for flip, item in zip((1, 2, 3), messages)]
     return call(
         last_kernel,
         (block, block),
@@ -591,7 +593,7 @@
         near,
         *far,
         remote_outs=True,
-        scratch=(held, held, pltpu.SemaphoreType.DMA((groups, rows // PIECE, 2))),
+        scratch=(held, held, pltpu.SemaphoreType.DMA((groups, 2, 2))),
     )
 
 

time: 56.9 us -> 57 us (level)
  no operation moved by 1% of the time
where the time goes in v8:
time: 57 us; the launch traced here: 56.8 us
  blocking collectives  31.3 us (55%)
  starting transfers between devices  10.1 us (18%)
  waiting for transfers between devices  8.44 us (15%)
  Pallas kernels  6.18 us (11%)
  between operations  0.75 us (1%)
    all_to_all x2, blocking collectives, exchange(): return lax.all_to_all(value, 'rad', 0, 0, tiled=True)  31.3 us
    ppermute x6, starting transfers between devices, flip_permute(): lax.ppermute(value, 'rad', [(i, i ^ flip) for i in range(lax.axis_size('r...  8.35 us
    ppermute x6, waiting for transfers between devices, flip_permute(): lax.ppermute(value, 'rad', [(i, i ^ flip) for i in range(lax.axis_size('r...  7.96 us
    pallas_call x8, Pallas kernels, call(): pl.pallas_call(kernel, out_shape=outs, in_specs=[away if k in remote else...  6.18 us
    ppermute x1, starting transfers between devices, swap_edges(): lax.ppermute(low_edge, 'azi', [((i + 1) % count, i) for i in range(count)])  1.72 us
  transfers between devices with their start and end apart: 8, of which 6 were waited for; matrix products, arithmetic and copies ran while one was open for 0% of the time, Pallas kernels for 3%

profile of v8, /device:TPU:64, one launch (start us, length us, event | category | flops | bytes accessed | tf_op | source)
XLA Modules:
  0.0 56.8 jit_solution(11536892584694760844)
XLA Ops:
  0.6 0.0 copy-start.4
  0.6 0.0 copy-start.3
  0.7 0.0 copy-start.2
  0.7 0.0 copy-start.1
  0.7 1.3 %shard_map.70 = (f32[3,16,512]{2,1,0:T(8,128)S(1)}, f32[3,16,512]{2,1,0:T(8,128)S(1)}) custom-call(f32[16,32,512]{2,1,0:T(8,128)} %heat.3, f32[16,32,512]{2,1,0:T(8,128)} %deform.3, f32[16,32,512]{2,1,0:T(8,128)} %flux.3, f32[16,32,512]{2,1,0:T(8,128)} %goal.3, f32[16,32,512]{2,1,0:T(8,128)} %old.5), custom_call_target="tpu_custom_call" | custom-call | flops 1000000 | bytes 5439488 | tf_op jit(solution)/shard_map/pallas_call | solution.py:483
  2.0 0.0 collective-permute-start
  2.0 0.0 copy-start
  2.1 1.7 %collective-permute-start.1 = (f32[3,16,512]{2,1,0:T(8,128)S(1)}, f32[3,16,512]{2,1,0:T(8,128)S(1)}, u32[]{:S(2)}, u32[]{:S(2)}) collective-permute-start(f32[3,16,512]{2,1,0:T(8,128)S(1)} %get-tuple-element.28), channel_id=1, source_target_pairs={{1,0},{2,1},{3,2},{4,3},{5,4},{6,5},{7,6},{8,7},{9,8},{10,9},{11,1... | collective-permute-start | bytes 294920 | tf_op jit(solution)/shard_map/ppermute | solution.py:497
  3.8 0.0 copy-done.4
  3.8 0.0 copy-done.3
  3.8 0.0 copy-done.2
  3.8 0.0 copy-done.1
  3.8 1.1 %shard_map.68 = (f32[16,32,512]{2,1,0:T(8,128)S(1)}, f32[16,32,512]{2,1,0:T(8,128)S(1)}, f32[16,32,512]{2,1,0:T(8,128)S(1)}, f32[16,32,512]{2,1,0:T(8,128)S(1)},...) custom-call(f32[16,32,512]{2,1,0:T(8,128)S(1)} %copy-done.1, ...), custom_call_target="tpu_custom_call" | custom-call | flops 20000000 | bytes 10682368 | tf_op jit(solution)/shard_map/pallas_call | solution.py:483
  4.9 0.0 copy-done
  4.9 0.7 %shard_map.69 = (f32[16,32,512]{2,1,0:T(8,128)S(1)}, f32[16,2,8,128]{3,2,1,0:T(8,128)S(1)}) custom-call(f32[16,32,512]{2,1,0:T(8,128)S(1)} %copy-done, f32[16,32,512]{2,1,0:T(8,128)S(1)} %get-tuple-element.21.ahead, f32[16,32,512]{2,1,0:T(8,128)S(1)} %get-tuple-element.22.given, f32[16,32,512]{2,1,0:T(8,128)S(1)} %get-tuple-element.23.ratio), custom_call_target="tpu_custom_call" | custom-call | flops 1000000 | bytes 5373952 | tf_op jit(solution)/shard_map/pallas_call | solution.py:483
  5.6 0.5 collective-permute-done.below
  6.1 0.0 collective-permute-done.1.above
  6.1 0.4 shard_map.71
  6.5 17.6 %all_to_all.10.got = f32[16,6,8,128]{3,2,1,0:T(8,128)S(1)} all-to-all(f32[16,6,8,128]{3,2,1,0:T(8,128)S(1)} %get-tuple-element.32), channel_id=1, replica_groups=mesh['rad'=16,'azi'=16] {'rad'}, dimensions={0} | all-to-all | bytes 786432 | tf_op jit(solution)/shard_map/all_to_all | solution.py:506
  24.0 0.2 shard_map.72
  24.2 13.7 %all_to_all.11.got = f32[16,6,8,128]{3,2,1,0:T(8,128)S(1)} all-to-all(f32[16,6,8,128]{3,2,1,0:T(8,128)S(1)} %shard_map.72), channel_id=1, replica_groups=mesh['rad'=16,'azi'=16] {'rad'}, dimensions={0} | all-to-all | bytes 786432 | tf_op jit(solution)/shard_map/all_to_all | solution.py:506
  38.0 0.9 %shard_map.73 = (f32[16,32,512]{2,1,0:T(8,128)S(1)}, f32[2,32,512]{2,1,0:T(8,128)S(1)}, f32[32,512]{1,0:T(8,128)S(1)}) custom-call(f32[16,32,512]{2,1,0:T(8,128)S(1)} %get-tuple-element.24.before, f32[16,32,512]{2,1,0:T(8,128)S(1)} %get-tuple-element.25.left_map, f32[16,32,512]{2,1,0:T(8,128)S(1)} %get-tuple-element.26.right_map, ...), custom_call_target="tpu_custom_call" | custom-call | flops 1000000 | bytes 8388608 | tf_op jit(solution)/shard_map/pallas_call | solution.py:483
  38.9 0.6 %collective-permute-start.4 = (f32[2,32,512]{2,1,0:T(8,128)S(1)}, f32[2,32,512]{2,1,0:T(8,128)S(1)}, u32[]{:S(2)}, u32[]{:S(2)}) collective-permute-start(f32[2,32,512]{2,1,0:T(8,128)S(1)} %get-tuple-element.35.own), channel_id=1, source_target_pairs={{0,48},{16,32},{32,16},{48,0},{64,112},{80,96},{96,80},{112,64},{1... | collective-permute-start | bytes 393224 | tf_op jit(solution)/shard_map/ppermute | solution.py:502
  39.6 2.1 %collective-permute-start.3 = (f32[2,32,512]{2,1,0:T(8,128)S(1)}, f32[2,32,512]{2,1,0:T(8,128)S(1)}, u32[]{:S(2)}, u32[]{:S(2)}) collective-permute-start(f32[2,32,512]{2,1,0:T(8,128)S(1)} %get-tuple-element.35.own), channel_id=1, source_target_pairs={{0,32},{16,48},{32,0},{48,16},{64,96},{80,112},{96,64},{112,80},{1... | collective-permute-start | bytes 393224 | tf_op jit(solution)/shard_map/ppermute | solution.py:502
  41.6 1.5 %collective-permute-start.2 = (f32[2,32,512]{2,1,0:T(8,128)S(1)}, f32[2,32,512]{2,1,0:T(8,128)S(1)}, u32[]{:S(2)}, u32[]{:S(2)}) collective-permute-start(f32[2,32,512]{2,1,0:T(8,128)S(1)} %get-tuple-element.35.own), channel_id=1, source_target_pairs={{0,16},{16,0},{32,48},{48,32},{64,80},{80,64},{96,112},{112,96},{1... | collective-permute-start | bytes 393224 | tf_op jit(solution)/shard_map/ppermute | solution.py:502
  43.1 4.3 %collective-permute-done.4.third = f32[2,32,512]{2,1,0:T(8,128)S(1)} collective-permute-done((f32[2,32,512]{2,1,0:T(8,128)S(1)}, f32[2,32,512]{2,1,0:T(8,128)S(1)}, u32[]{:S(2)}, u32[]{:S(2)}) %collective-permute-start.4) | collective-permute-done | bytes 131104 | tf_op jit(solution)/shard_map/ppermute | solution.py:502
  47.4 0.0 collective-permute-done.3.second
  47.4 0.6 %collective-permute-done.2.first = f32[2,32,512]{2,1,0:T(8,128)S(1)} collective-permute-done((f32[2,32,512]{2,1,0:T(8,128)S(1)}, f32[2,32,512]{2,1,0:T(8,128)S(1)}, u32[]{:S(2)}, u32[]{:S(2)}) %collective-permute-start.2) | collective-permute-done | bytes 131104 | tf_op jit(solution)/shard_map/ppermute | solution.py:502
  48.0 0.1 shard_map.74
  48.1 0.1 collective-permute-start.5
  48.2 1.3 %collective-permute-start.7 = (f32[32,512]{1,0:T(8,128)S(1)}, f32[32,512]{1,0:T(8,128)S(1)}, u32[]{:S(2)}, u32[]{:S(2)}) collective-permute-start(f32[32,512]{1,0:T(8,128)S(1)} %get-tuple-element.39), channel_id=1, source_target_pairs={{0,192},{16,208},{32,224},{48,240},{64,128},{80,144},{96,160},{112... | collective-permute-start | bytes 196616 | tf_op jit(solution)/shard_map/ppermute | solution.py:502
  49.5 2.7 %collective-permute-start.6 = (f32[32,512]{1,0:T(8,128)S(1)}, f32[32,512]{1,0:T(8,128)S(1)}, u32[]{:S(2)}, u32[]{:S(2)}) collective-permute-start(f32[32,512]{1,0:T(8,128)S(1)} %get-tuple-element.39), channel_id=1, source_target_pairs={{0,128},{16,144},{32,160},{48,176},{64,192},{80,208},{96,224},{112... | collective-permute-start | bytes 196616 | tf_op jit(solution)/shard_map/ppermute | solution.py:502
  52.3 0.6 %collective-permute-done.5.first = f32[32,512]{1,0:T(8,128)S(1)} collective-permute-done((f32[32,512]{1,0:T(8,128)S(1)}, f32[32,512]{1,0:T(8,128)S(1)}, u32[]{:S(2)}, u32[]{:S(2)}) %collective-permute-start.5) | collective-permute-done | bytes 65568 | tf_op jit(solution)/shard_map/ppermute | solution.py:502
  52.9 0.8 %collective-permute-done.7.third = f32[32,512]{1,0:T(8,128)S(1)} collective-permute-done((f32[32,512]{1,0:T(8,128)S(1)}, f32[32,512]{1,0:T(8,128)S(1)}, u32[]{:S(2)}, u32[]{:S(2)}) %collective-permute-start.7) | collective-permute-done | bytes 65568 | tf_op jit(solution)/shard_map/ppermute | solution.py:502
  53.7 1.5 %collective-permute-done.6.second = f32[32,512]{1,0:T(8,128)S(1)} collective-permute-done((f32[32,512]{1,0:T(8,128)S(1)}, f32[32,512]{1,0:T(8,128)S(1)}, u32[]{:S(2)}, u32[]{:S(2)}) %collective-permute-start.6) | collective-permute-done | bytes 65568 | tf_op jit(solution)/shard_map/ppermute | solution.py:502
  55.3 1.5 %shard_map.75 = (f32[16,32,512]{2,1,0:T(8,128)}, f32[16,32,512]{2,1,0:T(8,128)}) custom-call(f32[16,32,512]{2,1,0:T(8,128)S(1)} %get-tuple-element.33.particular, f32[16,32,512]{2,1,0:T(8,128)S(1)} %get-tuple-element.25.left_map, f32[16,32,512]{2,1,0:T(8,128)S(1)} %get-tuple-element.26.right_map, f32[16,32,512]{2,1,0:T(8,128)S(1)} %get-tuple-element.34.factor, ...), custom_call_target="tpu_custom_call" | custom-call | flops 1000000 | bytes 7208960 | tf_op jit(solution)/shard_map/pallas_call | solution.py:483
Async XLA Ops:
  0.6 3.1 %copy-start.4 = (f32[16,32,512]{2,1,0:T(8,128)S(1)}, f32[16,32,512]{2,1,0:T(8,128)}, u32[]{:S(2)}) copy-start(f32[16,32,512]{2,1,0:T(8,128)} %goal.3) | copy-start | bytes 3145732
  0.6 3.1 %copy-start.3 = (f32[16,32,512]{2,1,0:T(8,128)S(1)}, f32[16,32,512]{2,1,0:T(8,128)}, u32[]{:S(2)}) copy-start(f32[16,32,512]{2,1,0:T(8,128)} %flux.3) | copy-start | bytes 3145732
  0.7 3.1 %copy-start.2 = (f32[16,32,512]{2,1,0:T(8,128)S(1)}, f32[16,32,512]{2,1,0:T(8,128)}, u32[]{:S(2)}) copy-start(f32[16,32,512]{2,1,0:T(8,128)} %deform.3) | copy-start | bytes 3145732
  0.7 3.1 %copy-start.1 = (f32[16,32,512]{2,1,0:T(8,128)S(1)}, f32[16,32,512]{2,1,0:T(8,128)}, u32[]{:S(2)}) copy-start(f32[16,32,512]{2,1,0:T(8,128)} %heat.3) | copy-start | bytes 3145732
  2.0 4.1 %collective-permute-start = (f32[3,16,512]{2,1,0:T(8,128)S(1)}, f32[3,16,512]{2,1,0:T(8,128)S(1)}, u32[]{:S(2)}, u32[]{:S(2)}) collective-permute-start(f32[3,16,512]{2,1,0:T(8,128)S(1)} %get-tuple-element.27), channel_id=1, source_target_pairs={{0,1},{1,2},{2,3},{3,4},{4,5},{5,6},{6,7},{7,8},{8,9},{9,10},{10,1... | collective-permute-start | bytes 294920 | tf_op jit(solution)/shard_map/ppermute | solution.py:496
  2.0 2.8 %copy-start = (f32[16,32,512]{2,1,0:T(8,128)S(1)}, f32[16,32,512]{2,1,0:T(8,128)}, u32[]{:S(2)}) copy-start(f32[16,32,512]{2,1,0:T(8,128)} %old.5) | copy-start | bytes 3145732
  2.1 4.0 %collective-permute-start.1 = (f32[3,16,512]{2,1,0:T(8,128)S(1)}, f32[3,16,512]{2,1,0:T(8,128)S(1)}, u32[]{:S(2)}, u32[]{:S(2)}) collective-permute-start(f32[3,16,512]{2,1,0:T(8,128)S(1)} %get-tuple-element.28), channel_id=1, source_target_pairs={{1,0},{2,1},{3,2},{4,3},{5,4},{6,5},{7,6},{8,7},{9,8},{10,9},{11,1... | collective-permute-start | bytes 294920 | tf_op jit(solution)/shard_map/ppermute | solution.py:497
  38.9 8.5 %collective-permute-start.4 = (f32[2,32,512]{2,1,0:T(8,128)S(1)}, f32[2,32,512]{2,1,0:T(8,128)S(1)}, u32[]{:S(2)}, u32[]{:S(2)}) collective-permute-start(f32[2,32,512]{2,1,0:T(8,128)S(1)} %get-tuple-element.35.own), channel_id=1, source_target_pairs={{0,48},{16,32},{32,16},{48,0},{64,112},{80,96},{96,80},{112,64},{1... | collective-permute-start | bytes 393224 | tf_op jit(solution)/shard_map/ppermute | solution.py:502
  39.6 7.8 %collective-permute-start.3 = (f32[2,32,512]{2,1,0:T(8,128)S(1)}, f32[2,32,512]{2,1,0:T(8,128)S(1)}, u32[]{:S(2)}, u32[]{:S(2)}) collective-permute-start(f32[2,32,512]{2,1,0:T(8,128)S(1)} %get-tuple-element.35.own), channel_id=1, source_target_pairs={{0,32},{16,48},{32,0},{48,16},{64,96},{80,112},{96,64},{112,80},{1... | collective-permute-start | bytes 393224 | tf_op jit(solution)/shard_map/ppermute | solution.py:502
  41.6 6.4 %collective-permute-start.2 = (f32[2,32,512]{2,1,0:T(8,128)S(1)}, f32[2,32,512]{2,1,0:T(8,128)S(1)}, u32[]{:S(2)}, u32[]{:S(2)}) collective-permute-start(f32[2,32,512]{2,1,0:T(8,128)S(1)} %get-tuple-element.35.own), channel_id=1, source_target_pairs={{0,16},{16,0},{32,48},{48,32},{64,80},{80,64},{96,112},{112,96},{1... | collective-permute-start | bytes 393224 | tf_op jit(solution)/shard_map/ppermute | solution.py:502
  48.1 4.8 %collective-permute-start.5 = (f32[32,512]{1,0:T(8,128)S(1)}, f32[32,512]{1,0:T(8,128)S(1)}, u32[]{:S(2)}, u32[]{:S(2)}) collective-permute-start(f32[32,512]{1,0:T(8,128)S(1)} %get-tuple-element.38), channel_id=1, source_target_pairs={{0,64},{16,80},{32,96},{48,112},{64,0},{80,16},{96,32},{112,48},{1... | collective-permute-start | bytes 196616 | tf_op jit(solution)/shard_map/ppermute | solution.py:502
  48.2 5.6 %collective-permute-start.7 = (f32[32,512]{1,0:T(8,128)S(1)}, f32[32,512]{1,0:T(8,128)S(1)}, u32[]{:S(2)}, u32[]{:S(2)}) collective-permute-start(f32[32,512]{1,0:T(8,128)S(1)} %get-tuple-element.39), channel_id=1, source_target_pairs={{0,192},{16,208},{32,224},{48,240},{64,128},{80,144},{96,160},{112... | collective-permute-start | bytes 196616 | tf_op jit(solution)/shard_map/ppermute | solution.py:502
  49.5 5.8 %collective-permute-start.6 = (f32[32,512]{1,0:T(8,128)S(1)}, f32[32,512]{1,0:T(8,128)S(1)}, u32[]{:S(2)}, u32[]{:S(2)}) collective-permute-start(f32[32,512]{1,0:T(8,128)S(1)} %get-tuple-element.39), channel_id=1, source_target_pairs={{0,128},{16,144},{32,160},{48,176},{64,192},{80,208},{96,224},{112... | collective-permute-start | bytes 196616 | tf_op jit(solution)/shard_map/ppermute | solution.py:502
